TPU v7x, 32 devices: a whole 2x2x4 slice. The times are simulated.
32 devices in a mesh: section: 4 (over y, x), dp: 8 (over z, core).
Axes of the slice: x: 2, y: 2, z: 4, core: 2. Of those that a mesh axis runs over, the one named last changes fastest.
Arguments:
- hidden_in: bfloat16 [2, 2048, 1024], P(None, 'dp'), may hold values from -6 to 6
- cotangent: bfloat16 [2, 2048, 1024], P(None, 'dp'), may hold values from -6 to 6
- bucket_len: int32 [2, 8, 4], P(None, 'dp'), may hold values from 1 to 192, 256 in all within a row
- live_mask: int32 [2, 2048], P(None, 'dp'), may hold values 0 or 1
- routes: int32 [2, 2048, 1], P(None, 'dp'), may hold values from 0 to 7; in each aligned block of 256 rows (0 to 255, 256 to 511, ..., all dimensions but the last counted through in order) at most 48 rows name the same one
- ln1_gain: bfloat16 [1024], P(('section', 'dp')), may hold values from 0.5 to 1.5
- ln1_bias: bfloat16 [1024], P(('section', 'dp')), may hold values from -4 to 4
- w_qkv: bfloat16 [1024, 3072], P(('section', 'dp')), may hold values from -0.1875 to 0.1875
- w_attn_out: bfloat16 [1024, 1024], P(('section', 'dp')), may hold values from -0.75 to 0.75
- ln2_gain: bfloat16 [1024], P(('section', 'dp')), may hold values from 0.5 to 1.5
- ln2_bias: bfloat16 [1024], P(('section', 'dp')), may hold values from -4 to 4
- w_up: bfloat16 [1024, 4096], P(('section', 'dp')), may hold values from -0.1875 to 0.1875
- w_down: bfloat16 [4096, 1024], P(('section', 'dp')), may hold values from -0.09375 to 0.09375
- expert_in: bfloat16 [8, 1024, 4096], P('dp', None, 'section'), may hold values from -0.1875 to 0.1875
- expert_out: bfloat16 [8, 4096, 1024], P('dp', 'section'), may hold values from -0.09375 to 0.09375
- expert_gain: bfloat16 [8, 1024], P('dp', 'section'), may hold values from 0.5 to 1.5
- expert_bias: bfloat16 [8, 1024], P('dp', 'section'), may hold values from -4 to 4
- centroids: bfloat16 [8, 1024], P('dp', 'section'), may hold values from -0.09375 to 0.09375
Outputs:
- block_out: bfloat16 [2, 2048, 1024], P(None, 'dp', 'section')
- input_grad: float32 [2, 2048, 1024], P(None, 'dp', 'section')
- grad_ln1_gain: float32 [1024], P(('section', 'dp'))
- grad_ln1_bias: float32 [1024], P(('section', 'dp'))
- grad_w_qkv: float32 [1024, 3072], P(('section', 'dp'))
- grad_w_attn_out: float32 [1024, 1024], P(('section', 'dp'))
- grad_ln2_gain: float32 [1024], P(('section', 'dp'))
- grad_ln2_bias: float32 [1024], P(('section', 'dp'))
- grad_w_up: float32 [1024, 4096], P(('section', 'dp'))
- grad_w_down: float32 [4096, 1024], P(('section', 'dp'))
- grad_expert_in: float32 [8, 1024, 4096], P('dp', None, 'section')
- grad_expert_out: float32 [8, 4096, 1024], P('dp', 'section')
- grad_expert_gain: float32 [8, 1024], P('dp', 'section')
- grad_expert_bias: float32 [8, 1024], P('dp', 'section')
- grad_centroids: float32 [8, 1024], P('dp', 'section')
Inputs may be any that keep to these rules, and one draw needn't show every extreme that they name: `routes`: in each block of 256 slots of a micro-batch (the slots of one index of dp), at most 48 slots name one expert. `bucket_len`: each block's 4 lengths sum to 256.
All inputs are finite; a program needn't handle non-finite values. No bound on the sum of `live_mask` on one device may be relied on, other than what follows from the above.
Results may differ from a plain program's by a relative error of at most 0.013.
Values may be sent and summed in bfloat16 or wider, within the bound.
A program may use at most 448 MiB of HBM per device.

v0:
```python
import jax
import jax.numpy as jnp
from jax import lax
from jax.sharding import PartitionSpec as P

HEADS = 16


epsilon = 1e-05
masked_value = -1e30


def for_sending(shard):

    def short(part):
        return part.astype(jnp.bfloat16) if part.dtype == jnp.float32 else part

    return jax.tree.map(short, shard)


def passed_along(shard, axis, by):
    length = lax.axis_size(axis)
    pairs = [(i, i + by) for i in range(length) if 0 <= i + by < length]
    return lax.ppermute(shard, axis, pairs)


def layer_norm(values, gain, bias):
    center = values - jnp.mean(values, axis=-1, keepdims=True)
    spread = jnp.mean(center * center, axis=-1, keepdims=True)
    return center * lax.rsqrt(spread + epsilon) * gain + bias


def norm_back(values, gain, bias, grad):
    outputs, pullback = jax.vjp(layer_norm, values, gain, bias)
    return pullback(grad)


def gelu_back(pre, grad):
    outputs, pullback = jax.vjp(jax.nn.gelu, pre)
    return pullback(grad)[0]


def allowed_pairs(segment, live):
    places = jnp.arange(segment.shape[0], dtype=jnp.int32)
    same = segment[:, None] == segment[None, :]
    causal = places[None, :] <= places[:, None]
    opened = (live[None, :] == 1) | (places[None, :] == places[:, None])
    return same & causal & opened


def slot_places(chosen, experts, capacity):
    picks = (chosen[:, None] == jnp.arange(experts, dtype=jnp.int32)[None, :]).astype(jnp.int32)
    ranks = jnp.sum((jnp.cumsum(picks, axis=0) - picks) * picks, axis=1)
    return chosen * capacity + ranks


def dispatch_rows(values, places, total):
    count = values.shape[0]
    source = jnp.full((total,), count, jnp.int32).at[places].set(jnp.arange(count, dtype=jnp.int32))
    return jnp.take(values, source, axis=0, mode="fill", fill_value=0)


def select_batch(values, position):
    return lax.dynamic_index_in_dim(values, position, 0, False)


def write_batch(values, update, position):
    return lax.dynamic_update_index_in_dim(values, update, position, 0)


def contract_rows(left, right):
    return jnp.einsum("rd,re->de", left, right, preferred_element_type=jnp.float32)


def times_transposed(left, right):
    return jnp.einsum("re,de->rd", left, right, preferred_element_type=jnp.float32)


def split_heads(mixed_qkv, heads):
    row_count, triple = mixed_qkv.shape
    width = triple // 3
    size = width // heads
    queries = mixed_qkv[:, :width].reshape(row_count, heads, size)
    key_rows = mixed_qkv[:, width : 2 * width].reshape(row_count, heads, size)
    value_rows = mixed_qkv[:, 2 * width :].reshape(row_count, heads, size)
    return (queries, key_rows, value_rows, size ** (-0.5))


def attention_forward(normed, segment, live, w_qkv, heads):
    row_count, width = normed.shape
    mixed_qkv = jnp.dot(normed, w_qkv, preferred_element_type=jnp.float32).astype(jnp.bfloat16)
    queries, key_rows, value_rows, scale = split_heads(mixed_qkv, heads)
    raw = jnp.einsum("qhd,khd->hqk", queries, key_rows, preferred_element_type=jnp.float32) * scale
    scores = jnp.where(allowed_pairs(segment, live)[None], raw, masked_value)
    top = jnp.max(scores, axis=-1, keepdims=True)
    weights = jnp.exp(scores - top)
    probs = weights / jnp.sum(weights, axis=-1, keepdims=True)
    probs_low = probs.astype(jnp.bfloat16)
    mixed = jnp.einsum("hqk,khd->qhd", probs_low, value_rows, preferred_element_type=jnp.float32)
    return (mixed_qkv, probs, probs_low, mixed.reshape(row_count, width).astype(jnp.bfloat16))


def attention_back(mixed_qkv, probs, probs_low, out_grad, heads):
    row_count, triple = mixed_qkv.shape
    width = triple // 3
    queries, key_rows, value_rows, scale = split_heads(mixed_qkv, heads)
    grad_heads = out_grad.reshape(queries.shape)
    grad_probs = jnp.einsum(
        "qhd,khd->hqk", grad_heads, value_rows, preferred_element_type=jnp.float32
    )
    grad_values = jnp.einsum(
        "hqk,qhd->khd", probs_low, grad_heads, preferred_element_type=jnp.float32
    )
    delta = jnp.sum(probs * grad_probs, axis=-1, keepdims=True)
    grad_scores = (probs * (grad_probs - delta)).astype(jnp.bfloat16)
    grad_queries = (
        jnp.einsum("hqk,khd->qhd", grad_scores, key_rows, preferred_element_type=jnp.float32)
        * scale
    )
    grad_keys = (
        jnp.einsum("hqk,qhd->khd", grad_scores, queries, preferred_element_type=jnp.float32) * scale
    )
    joined = jnp.concatenate(
        [
            grad_queries.reshape(row_count, width),
            grad_keys.reshape(row_count, width),
            grad_values.reshape(row_count, width),
        ],
        axis=1,
    )
    return joined.astype(jnp.bfloat16)


def on_device(
    hidden_in,
    cotangent,
    bucket_len,
    live_mask,
    routes,
    ln1_gain,
    ln1_bias,
    w_qkv,
    w_attn_out,
    ln2_gain,
    ln2_bias,
    w_up,
    w_down,
    expert_in,
    expert_out,
    expert_gain,
    expert_bias,
    centroids,
):
    section_count = lax.axis_size("section")
    groups = lax.axis_size("dp")
    section_index = lax.axis_index("section")
    micro, tok_rows, width = hidden_in.shape
    capacity = 3 * tok_rows // (2 * groups)
    exp_rows = groups * capacity
    dense = (
        lax.all_gather(ln1_gain, ("section", "dp"), axis=0, tiled=True),
        lax.all_gather(ln1_bias, ("section", "dp"), axis=0, tiled=True),
        lax.all_gather(w_qkv, ("section", "dp"), axis=0, tiled=True),
        lax.all_gather(w_attn_out, ("section", "dp"), axis=0, tiled=True),
        lax.all_gather(ln2_gain, ("section", "dp"), axis=0, tiled=True),
        lax.all_gather(ln2_bias, ("section", "dp"), axis=0, tiled=True),
        lax.all_gather(w_up, ("section", "dp"), axis=0, tiled=True),
        lax.all_gather(w_down, ("section", "dp"), axis=0, tiled=True),
    )
    expert = (
        lax.all_gather(expert_in, "section", axis=2, tiled=True),
        lax.all_gather(expert_out, "section", axis=1, tiled=True),
        lax.all_gather(expert_gain, "section", axis=1, tiled=True),
        lax.all_gather(expert_bias, "section", axis=1, tiled=True),
        lax.all_gather(centroids, "section", axis=1, tiled=True),
    )
    gain_one = dense[0].astype(jnp.float32)
    bias_one = dense[1].astype(jnp.float32)
    qkv_weight = dense[2]
    out_weight = dense[3]
    gain_two = dense[4].astype(jnp.float32)
    bias_two = dense[5].astype(jnp.float32)
    up_weight = dense[6]
    down_weight = dense[7]
    in_weight = expert[0][0]
    back_weight = expert[1][0]
    expert_g = expert[2][0].astype(jnp.float32)
    expert_b = expert[3][0].astype(jnp.float32)
    centroid = expert[4][0].astype(jnp.float32)
    ends = jnp.cumsum(bucket_len[:, 0, :], axis=-1)
    slot_ids = jnp.arange(tok_rows, dtype=jnp.int32)
    segments = jnp.sum((slot_ids[None, :, None] >= ends[:, None, :]).astype(jnp.int32), axis=-1)
    chosen_all = routes[:, :, 0]

    def attention_section(rows, segment, live):
        start = rows.astype(jnp.float32)
        normed = layer_norm(start, gain_one, bias_one).astype(jnp.bfloat16)
        mixed_qkv, probs, probs_low, attended = attention_forward(
            normed, segment, live, qkv_weight, HEADS
        )
        result = (start + jnp.dot(attended, out_weight, preferred_element_type=jnp.float32)).astype(
            jnp.bfloat16
        )
        return (start, normed, mixed_qkv, probs, probs_low, attended, result)

    def dense_section(rows):
        start = rows.astype(jnp.float32)
        normed = layer_norm(start, gain_two, bias_two).astype(jnp.bfloat16)
        pre = jnp.dot(normed, up_weight, preferred_element_type=jnp.float32)
        hidden = jax.nn.gelu(pre).astype(jnp.bfloat16)
        result = (start + jnp.dot(hidden, down_weight, preferred_element_type=jnp.float32)).astype(
            jnp.bfloat16
        )
        return (start, normed, pre, hidden, result)

    def expert_section(rows):
        start = rows.astype(jnp.float32)
        normed = layer_norm(start, expert_g, expert_b).astype(jnp.bfloat16)
        pre = jnp.dot(normed, in_weight, preferred_element_type=jnp.float32)
        hidden = jax.nn.gelu(pre).astype(jnp.bfloat16)
        result = jnp.dot(hidden, back_weight, preferred_element_type=jnp.float32)
        alpha = jax.nn.sigmoid(jnp.sum(start * centroid, axis=-1, keepdims=True))
        gated = (alpha * result).astype(jnp.bfloat16)
        return (start, normed, pre, hidden, result, alpha, gated)

    blank_tok = jnp.zeros((tok_rows, width), jnp.bfloat16)
    blank_exp = jnp.zeros((exp_rows, width), jnp.bfloat16)
    blank_out = jnp.zeros((tok_rows, width), jnp.float32)
    blank_send = jnp.zeros((groups, capacity, width), jnp.bfloat16)
    kept_tok = jnp.zeros((micro, tok_rows, width), jnp.bfloat16)
    kept_exp = jnp.zeros((micro, exp_rows, width), jnp.bfloat16)
    block_rows = jnp.zeros((micro, tok_rows, width), jnp.float32)
    arriving = (blank_tok, blank_exp)
    for moment in range(micro + section_count - 1):
        batch_now = moment - section_index
        active = (batch_now >= 0) & (batch_now < micro)
        batch_index = jnp.clip(batch_now, 0, micro - 1)
        branch = jnp.where(active, section_index, section_count)
        places = slot_places(select_batch(chosen_all, batch_index), groups, capacity)
        token_in, expert_rows_in = arriving
        outgoing = lax.switch(
            branch,
            [
                lambda: blank_send,
                lambda: blank_send,
                lambda: dispatch_rows(token_in, places, exp_rows).reshape(groups, capacity, width),
                lambda: expert_rows_in.reshape(groups, capacity, width),
                lambda: blank_send,
            ],
        )
        arrived = jax.tree.map(
            lambda part, own: part.astype(own.dtype),
            lax.all_to_all(for_sending(outgoing), "dp", split_axis=0, concat_axis=0, tiled=True),
            outgoing,
        ).reshape(exp_rows, width)

        def forward_attention():
            result = attention_section(
                select_batch(hidden_in, batch_index),
                select_batch(segments, batch_index),
                select_batch(live_mask, batch_index),
            )[-1]
            return (result, blank_exp, blank_out)

        def forward_dense():
            return (dense_section(token_in)[-1], blank_exp, blank_out)

        def forward_expert():
            return (token_in, expert_section(arrived)[-1], blank_out)

        def forward_combine():
            combined = token_in.astype(jnp.float32) + jnp.take(arrived, places, axis=0).astype(
                jnp.float32
            )
            return (blank_tok, blank_exp, combined)

        def forward_spare():
            return (blank_tok, blank_exp, blank_out)

        sent_tok, sent_exp, emitted = lax.switch(
            branch,
            [forward_attention, forward_dense, forward_expert, forward_combine, forward_spare],
        )
        kept_tok = write_batch(
            kept_tok, jnp.where(active, token_in, select_batch(kept_tok, batch_index)), batch_index
        )
        kept_exp = write_batch(
            kept_exp, jnp.where(active, arrived, select_batch(kept_exp, batch_index)), batch_index
        )
        block_rows = write_batch(
            block_rows, select_batch(block_rows, batch_index) + emitted, batch_index
        )
        arriving = (
            passed_along(for_sending(sent_tok), "section", 1).astype(sent_tok.dtype),
            passed_along(for_sending(sent_exp), "section", 1).astype(sent_exp.dtype),
        )
    dense_grads = tuple((jnp.zeros(weight.shape, jnp.float32) for weight in dense))
    expert_grads = tuple((jnp.zeros(weight.shape, jnp.float32) for weight in expert))
    input_rows = jnp.zeros((micro, tok_rows, width), jnp.float32)
    arriving = (blank_tok, blank_exp)
    for moment in range(micro + section_count - 1):
        batch_now = moment - (section_count - 1 - section_index)
        active = (batch_now >= 0) & (batch_now < micro)
        batch_index = jnp.clip(batch_now, 0, micro - 1)
        branch = jnp.where(active, section_index, section_count)
        places = slot_places(select_batch(chosen_all, batch_index), groups, capacity)
        token_in, expert_rows_in = arriving
        cot_rows = select_batch(cotangent, batch_index)

        def backward_attention(grads_dense, grads_expert):
            start, normed, mixed_qkv, probs, probs_low, attended, result = attention_section(
                select_batch(hidden_in, batch_index),
                select_batch(segments, batch_index),
                select_batch(live_mask, batch_index),
            )
            grad_out_weight = contract_rows(attended, token_in)
            grad_attended = times_transposed(token_in, out_weight).astype(jnp.bfloat16)
            grad_qkv = attention_back(mixed_qkv, probs, probs_low, grad_attended, HEADS)
            grad_qkv_weight = contract_rows(normed, grad_qkv)
            grad_normed = times_transposed(grad_qkv, qkv_weight)
            grad_start, grad_gain, grad_bias = norm_back(start, gain_one, bias_one, grad_normed)
            input_part = token_in.astype(jnp.float32) + grad_start
            updated = (
                grads_dense[0] + grad_gain,
                grads_dense[1] + grad_bias,
                grads_dense[2] + grad_qkv_weight,
                grads_dense[3] + grad_out_weight,
                grads_dense[4],
                grads_dense[5],
                grads_dense[6],
                grads_dense[7],
            )
            return (blank_tok, blank_send, input_part, updated, grads_expert)

        def backward_dense(grads_dense, grads_expert):
            start, normed, pre, hidden, result = dense_section(select_batch(kept_tok, batch_index))
            grad_down = contract_rows(hidden, token_in)
            grad_hidden = times_transposed(token_in, down_weight)
            grad_pre = gelu_back(pre, grad_hidden).astype(jnp.bfloat16)
            grad_up = contract_rows(normed, grad_pre)
            grad_normed = times_transposed(grad_pre, up_weight)
            grad_start, grad_gain, grad_bias = norm_back(start, gain_two, bias_two, grad_normed)
            message = (token_in.astype(jnp.float32) + grad_start).astype(jnp.bfloat16)
            updated = (
                grads_dense[0],
                grads_dense[1],
                grads_dense[2],
                grads_dense[3],
                grads_dense[4] + grad_gain,
                grads_dense[5] + grad_bias,
                grads_dense[6] + grad_up,
                grads_dense[7] + grad_down,
            )
            return (message, blank_send, blank_out, updated, grads_expert)

        def backward_expert(grads_dense, grads_expert):
            start, normed, pre, hidden, result, alpha, gated = expert_section(
                select_batch(kept_exp, batch_index)
            )
            grad_gated = expert_rows_in.astype(jnp.float32)
            grad_result = (alpha * grad_gated).astype(jnp.bfloat16)
            grad_alpha = jnp.sum(grad_gated * result, axis=-1, keepdims=True)
            grad_back = contract_rows(hidden, grad_result)
            grad_hidden = times_transposed(grad_result, back_weight)
            grad_pre = gelu_back(pre, grad_hidden).astype(jnp.bfloat16)
            grad_in_weight = contract_rows(normed, grad_pre)
            grad_normed = times_transposed(grad_pre, in_weight)
            grad_start, grad_gain, grad_bias = norm_back(start, expert_g, expert_b, grad_normed)
            grad_logit = grad_alpha * alpha * (1.0 - alpha)
            grad_centroid = jnp.sum(grad_logit * start, axis=0)
            grad_rows = (grad_start + grad_logit * centroid).astype(jnp.bfloat16)
            updated = (
                grads_expert[0] + grad_in_weight[None],
                grads_expert[1] + grad_back[None],
                grads_expert[2] + grad_gain[None],
                grads_expert[3] + grad_bias[None],
                grads_expert[4] + grad_centroid[None],
            )
            return (
                blank_tok,
                grad_rows.reshape(groups, capacity, width),
                blank_out,
                grads_dense,
                updated,
            )

        def backward_combine(grads_dense, grads_expert):
            outgoing_rows = dispatch_rows(cot_rows, places, exp_rows).reshape(
                groups, capacity, width
            )
            return (blank_tok, outgoing_rows, blank_out, grads_dense, grads_expert)

        def backward_spare(grads_dense, grads_expert):
            return (blank_tok, blank_send, blank_out, grads_dense, grads_expert)

        sent_tok, outgoing, emitted, dense_grads, expert_grads = lax.switch(
            branch,
            [backward_attention, backward_dense, backward_expert, backward_combine, backward_spare],
            dense_grads,
            expert_grads,
        )
        arrived = jax.tree.map(
            lambda part, own: part.astype(own.dtype),
            lax.all_to_all(for_sending(outgoing), "dp", split_axis=0, concat_axis=0, tiled=True),
            outgoing,
        ).reshape(exp_rows, width)
        merged_tok = lax.cond(
            active & (section_index == 2),
            lambda: (
                cot_rows.astype(jnp.float32) + jnp.take(arrived, places, axis=0).astype(jnp.float32)
            ).astype(jnp.bfloat16),
            lambda: sent_tok,
        )
        input_rows = write_batch(
            input_rows, select_batch(input_rows, batch_index) + emitted, batch_index
        )
        arriving = (
            passed_along(for_sending(merged_tok), "section", -1).astype(merged_tok.dtype),
            passed_along(for_sending(arrived), "section", -1).astype(arrived.dtype),
        )
    dense_out = (
        lax.psum_scatter(dense_grads[0], ("section", "dp"), scatter_dimension=0, tiled=True),
        lax.psum_scatter(dense_grads[1], ("section", "dp"), scatter_dimension=0, tiled=True),
        lax.psum_scatter(dense_grads[2], ("section", "dp"), scatter_dimension=0, tiled=True),
        lax.psum_scatter(dense_grads[3], ("section", "dp"), scatter_dimension=0, tiled=True),
        lax.psum_scatter(dense_grads[4], ("section", "dp"), scatter_dimension=0, tiled=True),
        lax.psum_scatter(dense_grads[5], ("section", "dp"), scatter_dimension=0, tiled=True),
        lax.psum_scatter(dense_grads[6], ("section", "dp"), scatter_dimension=0, tiled=True),
        lax.psum_scatter(dense_grads[7], ("section", "dp"), scatter_dimension=0, tiled=True),
    )
    expert_out_grads = (
        lax.psum_scatter(
            expert_grads[0].astype(jnp.bfloat16), "section", scatter_dimension=2, tiled=True
        ).astype(jnp.float32),
        lax.psum_scatter(
            expert_grads[1].astype(jnp.bfloat16), "section", scatter_dimension=1, tiled=True
        ).astype(jnp.float32),
        lax.psum_scatter(
            expert_grads[2].astype(jnp.bfloat16), "section", scatter_dimension=1, tiled=True
        ).astype(jnp.float32),
        lax.psum_scatter(
            expert_grads[3].astype(jnp.bfloat16), "section", scatter_dimension=1, tiled=True
        ).astype(jnp.float32),
        lax.psum_scatter(
            expert_grads[4].astype(jnp.bfloat16), "section", scatter_dimension=1, tiled=True
        ).astype(jnp.float32),
    )
    final = (
        lax.psum_scatter(
            block_rows.astype(jnp.bfloat16), "section", scatter_dimension=2, tiled=True
        ).astype(jnp.float32),
        lax.psum_scatter(
            input_rows.astype(jnp.bfloat16), "section", scatter_dimension=2, tiled=True
        ).astype(jnp.float32),
    )
    return (
        final[0].astype(jnp.bfloat16),
        final[1],
        dense_out[0],
        dense_out[1],
        dense_out[2],
        dense_out[3],
        dense_out[4],
        dense_out[5],
        dense_out[6],
        dense_out[7],
        expert_out_grads[0],
        expert_out_grads[1],
        expert_out_grads[2],
        expert_out_grads[3],
        expert_out_grads[4],
    )


def solution(mesh):
    placed = (
        P(None, "dp", None),
        P(None, "dp", None),
        P(None, "dp", None),
        P(None, "dp"),
        P(None, "dp", None),
        P(("section", "dp")),
        P(("section", "dp")),
        P(("section", "dp"), None),
        P(("section", "dp"), None),
        P(("section", "dp")),
        P(("section", "dp")),
        P(("section", "dp"), None),
        P(("section", "dp"), None),
        P("dp", None, "section"),
        P("dp", "section", None),
        P("dp", "section"),
        P("dp", "section"),
        P("dp", "section"),
    )
    return jax.shard_map(
        on_device,
        mesh=mesh,
        in_specs=placed,
        out_specs=(
            P(None, "dp", "section"),
            P(None, "dp", "section"),
            P(("section", "dp")),
            P(("section", "dp")),
            P(("section", "dp"), None),
            P(("section", "dp"), None),
            P(("section", "dp")),
            P(("section", "dp")),
            P(("section", "dp"), None),
            P(("section", "dp"), None),
            P("dp", None, "section"),
            P("dp", "section", None),
            P("dp", "section"),
            P("dp", "section"),
            P("dp", "section"),
        ),
        check_vma=False,
    )
```

profile of v0, /device:TPU:0, one launch (start us, length us, event | category | flops | bytes accessed | tf_op | source)
XLA Modules:
  0.0 2425.1 jit_solution(16824473546175815172)
XLA Ops:
  21.1 41.8 %all-reduce.9 = (bf16[1024]{0:T(1024)(128)(2,1)S(1)}, bf16[1024]{0:T(1024)(128)(2,1)S(1)}, bf16[1024]{0:T(1024)(128)(2,1)S(1)}, bf16[1024]{0:T(1024)(128)(2,1)S(1)}) all-reduce(bf16[1024]{0:T(1024)(128)(2,1)S(1)} %dynamic-update-slice, bf16[1024]{0:T(1024)(128)(2,1)S(1)} %dynamic-update-slice.1, ...), channel_id=1, replica_groups=mesh['section'=4,'dp'=8] {'section','dp'}, use_global_device_ids=true, to_apply=%add | all-reduce | flops 4096 | bytes 16384
  87.3 57.1 %all-gather.7.cloned.1.call-done = bf16[1024,3072]{1,0:T(8,128)(2,1)} async-done(((bf16[32,3072]{1,0:T(8,128)(2,1)}), bf16[1024,3072]{1,0:T(8,128)(2,1)}) %all-gather.7.cloned.1.call-update) | async-done | bytes 6291472 | tf_op jit(solution)/shard_map/all_gather | solution.py:163
  144.4 88.0 %all-gather.15.cloned.1.call-done = bf16[1,1024,4096]{2,1,0:T(8,128)(2,1)} async-done(((bf16[1,1024,1024]{2,1,0:T(8,128)(2,1)}), bf16[1,1024,4096]{2,1,0:T(8,128)(2,1)}) %all-gather.15.cloned.1.call-update) | async-done | bytes 8388624 | tf_op jit(solution)/shard_map/all_gather | solution.py:171
  232.4 89.3 %all-gather.17.cloned.1.call-done = bf16[1,4096,1024]{2,1,0:T(8,128)(2,1)} async-done(((bf16[1,1024,1024]{2,1,0:T(8,128)(2,1)}), bf16[1,4096,1024]{2,1,0:T(8,128)(2,1)}) %all-gather.17.cloned.1.call-update) | async-done | bytes 8388624 | tf_op jit(solution)/shard_map/all_gather | solution.py:172
  321.7 80.3 %all-gather.11.cloned.1.call-done = bf16[1024,4096]{1,0:T(8,128)(2,1)} async-done(((bf16[32,4096]{1,0:T(8,128)(2,1)}), bf16[1024,4096]{1,0:T(8,128)(2,1)}) %all-gather.11.cloned.1.call-update) | async-done | bytes 8388624 | tf_op jit(solution)/shard_map/all_gather | solution.py:167
  402.0 78.9 %all-gather.13.cloned.1.call-done = bf16[4096,1024]{1,0:T(8,128)(2,1)} async-done(((bf16[128,1024]{1,0:T(8,128)(2,1)}), bf16[4096,1024]{1,0:T(8,128)(2,1)}) %all-gather.13.cloned.1.call-update) | async-done | bytes 8388624 | tf_op jit(solution)/shard_map/all_gather | solution.py:168
  480.8 26.2 %conditional.20 = (bf16[256,1024]{1,0:T(8,128)(2,1)S(1)}, bf16[384,1024]{1,0:T(8,128)(2,1)}, f32[1,256,1024]{2,1,0:T(8,128)S(1)}) conditional(s32[]{:T(128)} %clamp.35, (s32[]{:T(128)}, bf16[2,256,1024]{2,1,0:T(8,128)(2,1)S(1)}, f32[1024]{0:T(1024)S(1)}, f32[1024]{0:T(1024)S(1)}, bf16[1024,3072]{1,0:T(8,128)(2,1)}, ...), branch_computations={%region_11.17_spmd, %region_16.18_spmd, %region_17.22_spmd, %regio... | conditional | flops 6462899200 | bytes 40294004 | solution.py:280
  511.5 26.7 %collective-permute-done = bf16[256,1024]{1,0:T(8,128)(2,1)S(1)} collective-permute-done((bf16[256,1024]{1,0:T(8,128)(2,1)}, bf16[256,1024]{1,0:T(8,128)(2,1)S(1)}, u32[]{:S(2)}, u32[]{:S(2)}) %collective-permute-start) | collective-permute-done | bytes 524320 | tf_op jit(solution)/shard_map/ppermute | solution.py:24
  739.6 27.1 %collective-permute-start.6 = (bf16[256,1024]{1,0:T(8,128)(2,1)}, bf16[256,1024]{1,0:T(8,128)(2,1)}, u32[]{:S(2)}, u32[]{:S(2)}) collective-permute-start(bf16[256,1024]{1,0:T(8,128)(2,1)} %get-tuple-element.1671), channel_id=1, source_target_pairs={{0,8},{8,16},{16,24},{1,9},{9,17},{17,25},{2,10},{10,18},{18,26},{... | collective-permute-start | bytes 1572872 | tf_op jit(solution)/shard_map/ppermute | solution.py:24
  803.5 79.0 %conditional.29 = (bf16[256,1024]{1,0:T(8,128)(2,1)}, bf16[8,48,1024]{2,1,0:T(8,128)(2,1)S(1)}, f32[1024]{0:T(1024)S(1)}, f32[1024]{0:T(1024)S(1)}, f32[1024,307...) conditional(s32[]{:T(128)} %clamp.40, (s32[]{:T(128)}, ...), branch_computations={%region_110.122_spmd, %region_120.129_spmd, %region_127.139_spmd, ... | conditional | flops 19404816384 | bytes 259898464 | solution.py:396
  910.4 51.4 %collective-permute-done.8 = bf16[256,1024]{1,0:T(8,128)(2,1)} collective-permute-done((bf16[256,1024]{1,0:T(8,128)(2,1)}, bf16[256,1024]{1,0:T(8,128)(2,1)}, u32[]{:S(2)}, u32[]{:S(2)}) %collective-permute-start.8) | collective-permute-done | bytes 524320 | tf_op jit(solution)/shard_map/ppermute | solution.py:24
  961.9 26.2 %conditional.31 = (bf16[8,48,1024]{2,1,0:T(8,128)(2,1)}, f32[256,1024]{1,0:T(8,128)}, f32[1024]{0:T(1024)S(1)}, f32[1024]{0:T(1024)S(1)}, f32[1024,3072]{1,0:T(8...) conditional(s32[]{:T(128)} %clamp.41, ...), branch_computations={%region_145.157_spmd, %region_155.164_spmd, %region_162.174_spmd, ... | conditional | flops 19415957504 | bytes 176297184 | solution.py:396
  1017.0 30.5 %collective-permute-done.10 = bf16[256,1024]{1,0:T(8,128)(2,1)} collective-permute-done((bf16[256,1024]{1,0:T(8,128)(2,1)}, bf16[256,1024]{1,0:T(8,128)(2,1)}, u32[]{:S(2)}, u32[]{:S(2)}) %collective-permute-start.10) | collective-permute-done | bytes 524320 | tf_op jit(solution)/shard_map/ppermute | solution.py:24
  1102.4 120.5 %collective-permute-done.12 = bf16[256,1024]{1,0:T(8,128)(2,1)} collective-permute-done((bf16[256,1024]{1,0:T(8,128)(2,1)}, bf16[256,1024]{1,0:T(8,128)(2,1)}, u32[]{:S(2)}, u32[]{:S(2)}) %collective-permute-start.12) | collective-permute-done | bytes 524320 | tf_op jit(solution)/shard_map/ppermute | solution.py:24
  1223.0 71.9 %conditional.35 = (bf16[8,48,1024]{2,1,0:T(8,128)(2,1)}, f32[256,1024]{1,0:T(8,128)}, f32[1024]{0:T(1024)S(1)}, f32[1024]{0:T(1024)S(1)}, f32[1024,3072]{1,0:T(8...) conditional(s32[]{:T(128)} %clamp.43, ...), branch_computations={%region_215.227_spmd, %region_225.234_spmd, %region_232.244_spmd, ... | conditional | flops 19415957504 | bytes 176305376 | solution.py:396
  1352.5 67.1 %conditional.37 = (f32[256,1024]{1,0:T(8,128)S(1)}, f32[1024]{0:T(1024)S(1)}, f32[1024]{0:T(1024)S(1)}, f32[1024,3072]{1,0:T(8,128)}, f32[1024,1024]{1,0:T(8,128...) conditional(s32[]{:T(128)} %clamp.44, ...), branch_computations={%region_247.259_spmd, %region_257.264_spmd, %region_262.272_spmd, ... | conditional | flops 19410059264 | bytes 214015216 | solution.py:396
  1459.0 37.2 %all-reduce.8 = (f32[1024]{0:T(1024)S(1)}, f32[1024]{0:T(1024)S(1)}, f32[1024]{0:T(1024)S(1)}, f32[1024]{0:T(1024)S(1)}) all-reduce(f32[1024]{0:T(1024)S(1)} %get-tuple-element.1738, f32[1024]{0:T(1024)S(1)} %get-tuple-element.1739, f32[1024]{0:T(1024)S(1)} %get-tuple-element.1742, ...), channel_id=4, replica_groups=mesh['section'=4,'dp'=8] {'section','dp'}, use_global_device_ids=true, to_apply=%region_273.276.clone | all-reduce | flops 4096 | bytes 32768
  1529.2 87.7 %reduce-scatter.30.cloned.1.call-done = bf16[1,1024,1024]{2,1,0:T(8,128)(2,1)} async-done(((bf16[1,1024,4096]{2,1,0:T(8,128)(2,1)}), bf16[1,1024,1024]{2,1,0:T(8,128)(2,1)}) %reduce-scatter.30.cloned.1.call-update) | async-done | bytes 2097168 | tf_op jit(solution)/shard_map/reduce_scatter | solution.py:432
  1621.0 85.6 %reduce-scatter.32.cloned.1.call-done = bf16[1,1024,1024]{2,1,0:T(8,128)(2,1)} async-done(((bf16[1,4096,1024]{2,1,0:T(8,128)(2,1)}), bf16[1,1024,1024]{2,1,0:T(8,128)(2,1)}) %reduce-scatter.32.cloned.1.call-update) | async-done | bytes 2097168 | tf_op jit(solution)/shard_map/reduce_scatter | solution.py:435
  1710.7 27.2 %reduce-scatter.18.cloned.1.call-done = bf16[2,256,256]{2,1,0:T(8,128)(2,1)} async-done(((bf16[2,256,1024]{2,1,0:T(8,128)(2,1)}), bf16[2,256,256]{2,1,0:T(8,128)(2,1)}) %reduce-scatter.18.cloned.1.call-update) | async-done | bytes 262160 | tf_op jit(solution)/shard_map/reduce_scatter | solution.py:449
  1737.8 145.4 %reduce-scatter.24.cloned.1.call-done = f32[32,1024]{1,0:T(8,128)} async-done(((f32[1024,1024]{1,0:T(8,128)}), f32[32,1024]{1,0:T(8,128)}) %reduce-scatter.24.cloned.1.call-update) | async-done | bytes 131088 | tf_op jit(solution)/shard_map/reduce_scatter | solution.py:425
  1883.2 159.6 %reduce-scatter.22.cloned.1.call-done = f32[32,3072]{1,0:T(8,128)} async-done(((f32[1024,3072]{1,0:T(8,128)}), f32[32,3072]{1,0:T(8,128)}) %reduce-scatter.22.cloned.1.call-update) | async-done | bytes 393232 | tf_op jit(solution)/shard_map/reduce_scatter | solution.py:424
  2042.8 188.5 %reduce-scatter.26.cloned.1.call-done = f32[32,4096]{1,0:T(8,128)} async-done(((f32[1024,4096]{1,0:T(8,128)}), f32[32,4096]{1,0:T(8,128)}) %reduce-scatter.26.cloned.1.call-update) | async-done | bytes 524304 | tf_op jit(solution)/shard_map/reduce_scatter | solution.py:428
  2231.3 187.1 %reduce-scatter.28.cloned.1.call-done = f32[128,1024]{1,0:T(8,128)} async-done(((f32[4096,1024]{1,0:T(8,128)}), f32[128,1024]{1,0:T(8,128)}) %reduce-scatter.28.cloned.1.call-update) | async-done | bytes 524304 | tf_op jit(solution)/shard_map/reduce_scatter | solution.py:429
  (501 shorter events, 726.8 us)
Async XLA Ops:
  7.2 80.1 %all-gather.9.cloned.1.call-start = ((), (), s32[]{:S(2)}) async-start(), calls=%async_computation.21 | async-start | bytes 2162688 | tf_op jit(solution)/shard_map/all_gather | solution.py:164
  7.9 136.4 %all-gather.7.cloned.1.call-start = ((), (), s32[]{:S(2)}) async-start(), calls=%async_computation.20 | async-start | bytes 6488064 | tf_op jit(solution)/shard_map/all_gather | solution.py:163
  8.7 223.7 %all-gather.15.cloned.1.call-start = ((), (), s32[]{:S(2)}) async-start(), calls=%async_computation.24 | async-start | bytes 10485760 | tf_op jit(solution)/shard_map/all_gather | solution.py:171
  9.4 312.3 %all-gather.17.cloned.1.call-start = ((), (), s32[]{:S(2)}) async-start(), calls=%async_computation.25 | async-start | bytes 10485760 | tf_op jit(solution)/shard_map/all_gather | solution.py:172
  10.0 392.0 %all-gather.11.cloned.1.call-start = ((), (), s32[]{:S(2)}) async-start(), calls=%async_computation.22 | async-start | bytes 8650752 | tf_op jit(solution)/shard_map/all_gather | solution.py:167
  10.6 470.3 %all-gather.13.cloned.1.call-start = ((), (), s32[]{:S(2)}) async-start(), calls=%async_computation.23 | async-start | bytes 8650752 | tf_op jit(solution)/shard_map/all_gather | solution.py:168
  13.9 73.4 %all-to-all-start = ((bf16[8,48,1024]{2,1,0:T(8,128)(2,1)}), bf16[8,48,1024]{2,1,0:T(8,128)(2,1)S(1)}, u32[]{:S(2)}, u32[]{:S(2)}) async-start(bf16[8,48,1024]{2,1,0:T(8,128)(2,1)} %get-tuple-element.2404), calls=%async_computation | async-start | bytes 1572864 | tf_op jit(solution)/shard_map/all_to_all | solution.py:253
  725.6 51.3 %collective-permute-start.7 = (bf16[384,1024]{1,0:T(8,128)(2,1)}, bf16[384,1024]{1,0:T(8,128)(2,1)S(1)}, u32[]{:S(2)}, u32[]{:S(2)}) collective-permute-start(bf16[384,1024]{1,0:T(8,128)(2,1)} %get-tuple-element.1672), channel_id=1, source_target_pairs={{0,8},{8,16},{16,24},{1,9},{9,17},{17,25},{2,10},{10,18},{18,26},{... | collective-permute-start | bytes 2359304 | tf_op jit(solution)/shard_map/ppermute | solution.py:24
  739.6 37.3 %collective-permute-start.6 = (bf16[256,1024]{1,0:T(8,128)(2,1)}, bf16[256,1024]{1,0:T(8,128)(2,1)}, u32[]{:S(2)}, u32[]{:S(2)}) collective-permute-start(bf16[256,1024]{1,0:T(8,128)(2,1)} %get-tuple-element.1671), channel_id=1, source_target_pairs={{0,8},{8,16},{16,24},{1,9},{9,17},{17,25},{2,10},{10,18},{18,26},{... | collective-permute-start | bytes 1572872 | tf_op jit(solution)/shard_map/ppermute | solution.py:24
  906.8 55.0 %collective-permute-start.9 = (bf16[384,1024]{1,0:T(8,128)(2,1)}, bf16[384,1024]{1,0:T(8,128)(2,1)}, u32[]{:S(2)}, u32[]{:S(2)}) collective-permute-start(bf16[384,1024]{1,0:T(8,128)(2,1)} %bitcast.210), channel_id=1, source_target_pairs={{8,0},{16,8},{24,16},{9,1},{17,9},{25,17},{10,2},{18,10},{26,18},{... | collective-permute-start | bytes 2359304 | tf_op jit(solution)/shard_map/ppermute | solution.py:24
  908.1 53.7 %collective-permute-start.8 = (bf16[256,1024]{1,0:T(8,128)(2,1)}, bf16[256,1024]{1,0:T(8,128)(2,1)}, u32[]{:S(2)}, u32[]{:S(2)}) collective-permute-start(bf16[256,1024]{1,0:T(8,128)(2,1)} %get-tuple-element.2410), channel_id=1, source_target_pairs={{8,0},{16,8},{24,16},{9,1},{17,9},{25,17},{10,2},{18,10},{26,18},{... | collective-permute-start | bytes 1572872 | tf_op jit(solution)/shard_map/ppermute | solution.py:24
  1098.8 124.1 %collective-permute-start.13 = (bf16[384,1024]{1,0:T(8,128)(2,1)}, bf16[384,1024]{1,0:T(8,128)(2,1)}, u32[]{:S(2)}, u32[]{:S(2)}) collective-permute-start(bf16[384,1024]{1,0:T(8,128)(2,1)} %bitcast.226), channel_id=1, source_target_pairs={{8,0},{16,8},{24,16},{9,1},{17,9},{25,17},{10,2},{18,10},{26,18},{... | collective-permute-start | bytes 2359304 | tf_op jit(solution)/shard_map/ppermute | solution.py:24
  1100.1 122.8 %collective-permute-start.12 = (bf16[256,1024]{1,0:T(8,128)(2,1)}, bf16[256,1024]{1,0:T(8,128)(2,1)}, u32[]{:S(2)}, u32[]{:S(2)}) collective-permute-start(bf16[256,1024]{1,0:T(8,128)(2,1)} %get-tuple-element.2412), channel_id=1, source_target_pairs={{8,0},{16,8},{24,16},{9,1},{17,9},{25,17},{10,2},{18,10},{26,18},{... | collective-permute-start | bytes 1572872 | tf_op jit(solution)/shard_map/ppermute | solution.py:24
  1299.1 199.5 %reduce-scatter.34.cloned.1.call-start = ((), (), s32[]{:S(2)}) async-start(), calls=%async_computation.34 | async-start | bytes 327680
  1420.5 79.6 %reduce-scatter.36.cloned.1.call-start = ((), (), s32[]{:S(2)}) async-start(), calls=%async_computation.35 | async-start | bytes 327680
  1424.2 77.4 %reduce-scatter.38.cloned.1.call-start = ((), (), s32[]{:S(2)}) async-start(), calls=%async_computation.36 | async-start | bytes 327680
  1426.5 100.9 %reduce-scatter.20.cloned.1.call-start = ((), (), s32[]{:S(2)}) async-start(), calls=%async_computation.27 | async-start | bytes 1310720 | tf_op jit(solution)/shard_map/reduce_scatter | solution.py:452
  1430.5 186.4 %reduce-scatter.30.cloned.1.call-start = ((), (), s32[]{:S(2)}) async-start(), calls=%async_computation.32 | async-start | bytes 10485760 | tf_op jit(solution)/shard_map/reduce_scatter | solution.py:432
  1439.6 267.0 %reduce-scatter.32.cloned.1.call-start = ((), (), s32[]{:S(2)}) async-start(), calls=%async_computation.33 | async-start | bytes 10485760 | tf_op jit(solution)/shard_map/reduce_scatter | solution.py:435
  1448.7 289.1 %reduce-scatter.18.cloned.1.call-start = ((), (), s32[]{:S(2)}) async-start(), calls=%async_computation.26 | async-start | bytes 1310720 | tf_op jit(solution)/shard_map/reduce_scatter | solution.py:449
  1456.7 426.5 %reduce-scatter.24.cloned.1.call-start = ((), (), s32[]{:S(2)}) async-start(), calls=%async_computation.29 | async-start | bytes 4325376 | tf_op jit(solution)/shard_map/reduce_scatter | solution.py:425
  1457.3 585.5 %reduce-scatter.22.cloned.1.call-start = ((), (), s32[]{:S(2)}) async-start(), calls=%async_computation.28 | async-start | bytes 12976128 | tf_op jit(solution)/shard_map/reduce_scatter | solution.py:424
  1457.8 773.4 %reduce-scatter.26.cloned.1.call-start = ((), (), s32[]{:S(2)}) async-start(), calls=%async_computation.30 | async-start | bytes 17301504 | tf_op jit(solution)/shard_map/reduce_scatter | solution.py:428
  1458.4 960.0 %reduce-scatter.28.cloned.1.call-start = ((), (), s32[]{:S(2)}) async-start(), calls=%async_computation.31 | async-start | bytes 17301504 | tf_op jit(solution)/shard_map/reduce_scatter | solution.py:429
  (80 other events, 4181.6 us)
Sparse Core Ops, SparseCore 0:
  11.0 61.9 all-gather.8
  76.1 68.2 all-gather.6
  146.2 86.0 all-gather.14
  234.1 87.5 all-gather.16
  324.5 77.3 all-gather.10
  404.8 75.9 all-gather.12
  1420.6 21.4 reduce-scatter.33
  1445.1 24.0 reduce-scatter.35
  1472.0 24.0 reduce-scatter.37
  1499.7 27.7 reduce-scatter.19
  1530.5 86.3 reduce-scatter.29
  1620.1 86.4 reduce-scatter.31
  1710.0 27.7 reduce-scatter.17
  1740.6 142.5 reduce-scatter.23
  1890.7 152.0 reduce-scatter.21
  2045.5 185.7 reduce-scatter.25
  2234.0 184.3 reduce-scatter.27
where the time goes:
time: 2440 us; the launch traced here: 2430 us
  waiting for transfers between devices  1690 us (69%)
  blocking collectives  178 us (7%)
  loops' own time  147 us (6%)
  local copies, waits for them, and re-layouts  120 us (5%)
  starting transfers between devices  105 us (4%)
  matrix products  104 us (4%)
  other arithmetic  66.6 us (3%)
    ppermute x16, waiting for transfers between devices, passed_along(): return lax.ppermute(shard, axis, pairs)  297 us
    reduce_scatter x1, waiting for transfers between devices, on_device(): lax.psum_scatter(dense_grads[6], ('section', 'dp'), scatter_dimension=0,...  189 us
    reduce_scatter x1, waiting for transfers between devices, on_device(): lax.psum_scatter(dense_grads[7], ('section', 'dp'), scatter_dimension=0,...  187 us
    reduce_scatter x1, waiting for transfers between devices, on_device(): lax.psum_scatter(dense_grads[2], ('section', 'dp'), scatter_dimension=0,...  160 us
    reduce_scatter x1, waiting for transfers between devices, on_device(): lax.psum_scatter(dense_grads[3], ('section', 'dp'), scatter_dimension=0,...  145 us
    another operation x5, loops' own time, on_device(): lax.switch(branch, [backward_attention, backward_dense, backward_expert,...  121 us
    all_gather x1, waiting for transfers between devices, on_device(): lax.all_gather(expert_out, 'section', axis=1, tiled=True)  89.3 us
    all_gather x1, waiting for transfers between devices, on_device(): lax.all_gather(expert_in, 'section', axis=2, tiled=True)  88 us
  transfers between devices with their start and end apart: 39, of which 26 were waited for; matrix products, arithmetic and copies ran while one was open for 4% of the time, Pallas kernels for 0%

commit v1 on v0

v1 whole, which is shorter than its diff:
```python
import jax
import jax.numpy as jnp
from jax import lax
from jax.sharding import PartitionSpec as P

HEADS = 16
epsilon = 1e-05
masked_value = -1e30
f32 = jnp.float32
bf16 = jnp.bfloat16


def norm_parts(values):
    center = values - jnp.mean(values, axis=-1, keepdims=True)
    spread = jnp.mean(center * center, axis=-1, keepdims=True)
    rs = lax.rsqrt(spread + epsilon)
    return center * rs, rs


def gelu_back(pre, grad):
    outputs, pullback = jax.vjp(jax.nn.gelu, pre)
    return pullback(grad)[0]


def dot(a, b):
    return jnp.dot(a, b, preferred_element_type=f32)


def dot_tn(a, b):
    return jnp.einsum("rd,re->de", a, b, preferred_element_type=f32)


def dot_nt(a, b):
    return jnp.einsum("re,de->rd", a, b, preferred_element_type=f32)


def sum_scatter(part):
    return lax.psum_scatter(
        part.astype(bf16), "section", scatter_dimension=part.ndim - 1, tiled=True
    ).astype(f32)


def gather_features(part):
    return lax.all_gather(part, "section", axis=part.ndim - 1, tiled=True)


def on_device(
    hidden_in,
    cotangent,
    bucket_len,
    live_mask,
    routes,
    ln1_gain,
    ln1_bias,
    w_qkv,
    w_attn_out,
    ln2_gain,
    ln2_bias,
    w_up,
    w_down,
    expert_in,
    expert_out,
    expert_gain,
    expert_bias,
    centroids,
):
    sections = lax.axis_size("section")
    groups = lax.axis_size("dp")
    section = lax.axis_index("section")
    micro, rows, width = hidden_in.shape
    quarter = width // sections
    heads = HEADS // sections
    size = width // HEADS
    ff = w_up.shape[1] // sections
    capacity = 3 * rows // (2 * groups)
    shard = w_up.shape[0]
    own_cols = section * quarter

    def mine(values):
        return lax.dynamic_slice_in_dim(values, own_cols, quarter, values.ndim - 1)

    def column_group(weight, pieces):
        cols = weight.shape[1] // (pieces * sections)
        parts = weight.reshape(shard, pieces, sections, cols).transpose(2, 0, 1, 3)
        parts = parts.reshape(sections, shard, pieces * cols)
        parts = lax.all_to_all(parts, "section", split_axis=0, concat_axis=0, tiled=True)
        full = lax.all_gather(parts, "dp", axis=1, tiled=True)
        return full.reshape(width, pieces * cols)

    def column_group_back(grad, pieces):
        cols = grad.shape[1] // pieces
        parts = grad.astype(bf16).reshape(sections, groups * shard, pieces * cols)
        parts = lax.psum_scatter(parts, "dp", scatter_dimension=1, tiled=True)
        parts = lax.all_to_all(parts, "section", split_axis=0, concat_axis=0, tiled=True)
        parts = parts.reshape(sections, shard, pieces, cols).transpose(1, 2, 0, 3)
        return parts.reshape(shard, pieces * sections * cols).astype(f32)

    def row_group_back(grad):
        return lax.psum_scatter(
            grad.astype(bf16), "dp", scatter_dimension=0, tiled=True
        ).astype(f32)

    vectors = lax.all_gather(
        jnp.stack([ln1_gain, ln1_bias, ln2_gain, ln2_bias]), ("section", "dp"), axis=1, tiled=True
    ).astype(f32)
    gain_one, bias_one, gain_two, bias_two = vectors
    expert_vectors = lax.all_gather(
        jnp.concatenate([expert_gain, expert_bias, centroids]), "section", axis=1, tiled=True
    ).astype(f32)
    expert_g, expert_b, centroid = expert_vectors
    wqkv = column_group(w_qkv, 3)
    wo = lax.all_gather(w_attn_out, "dp", axis=0, tiled=True)
    wup = column_group(w_up, 1)
    wdown = lax.all_gather(w_down, "dp", axis=0, tiled=True)
    win = expert_in[0]
    wout = expert_out[0]

    ends = jnp.cumsum(bucket_len[:, 0, :], axis=-1)
    slot_ids = jnp.arange(rows, dtype=jnp.int32)
    segments = jnp.sum((slot_ids[None, :, None] >= ends[:, None, :]).astype(jnp.int32), axis=-1)
    same = segments[:, :, None] == segments[:, None, :]
    causal = slot_ids[None, None, :] <= slot_ids[None, :, None]
    opened = (live_mask[:, None, :] == 1) | (slot_ids[None, None, :] == slot_ids[None, :, None])
    allowed = (same & causal & opened)[:, None]
    chosen = routes[:, :, 0]
    picks = (chosen[:, :, None] == jnp.arange(groups, dtype=jnp.int32)).astype(jnp.int32)
    ranks = jnp.sum((jnp.cumsum(picks, axis=1) - picks) * picks, axis=2)
    places = chosen * capacity + ranks
    place_ids = jnp.arange(groups * capacity, dtype=jnp.int32)
    picked = (places[:, None, :] == place_ids[None, :, None]).astype(bf16)

    def dispatch(values):
        out = jnp.einsum("mpt,mtf->pmf", picked, values, preferred_element_type=f32).astype(bf16)
        out = out.reshape(groups, capacity * micro, quarter)
        return lax.all_to_all(out, "dp", split_axis=0, concat_axis=0, tiled=True)

    def give_back(values):
        out = lax.all_to_all(values, "dp", split_axis=0, concat_axis=0, tiled=True)
        out = out.reshape(groups * capacity, micro, quarter)
        return jnp.einsum("mpt,pmf->mtf", picked, out, preferred_element_type=f32)

    dge = gather_features(dispatch(mine(cotangent))).reshape(-1, width).astype(f32)

    x = hidden_in.reshape(micro * rows, width).astype(f32)
    n1, rs1 = norm_parts(x)
    a1 = (n1 * gain_one + bias_one).astype(bf16)
    qkv = dot(a1, wqkv).astype(bf16)
    q, k, v = (
        qkv[:, i * quarter : (i + 1) * quarter].reshape(micro, rows, heads, size) for i in range(3)
    )
    scale = size ** (-0.5)
    raw = jnp.einsum("mqhd,mkhd->mhqk", q, k, preferred_element_type=f32) * scale
    scores = jnp.where(allowed, raw, masked_value)
    weights = jnp.exp(scores - jnp.max(scores, axis=-1, keepdims=True))
    probs = weights / jnp.sum(weights, axis=-1, keepdims=True)
    probs_low = probs.astype(bf16)
    mixed = jnp.einsum("mhqk,mkhd->mqhd", probs_low, v, preferred_element_type=f32)
    o = mixed.reshape(micro * rows, quarter).astype(bf16)
    y1q = (mine(x) + sum_scatter(dot(o, wo))).astype(bf16)
    y1 = gather_features(y1q).astype(f32)
    n2, rs2 = norm_parts(y1)
    a2 = (n2 * gain_two + bias_two).astype(bf16)
    h = dot(a2, wup)
    u = jax.nn.gelu(h).astype(bf16)
    y2q = (y1q.astype(f32) + sum_scatter(dot(u, wdown))).astype(bf16)

    xe = gather_features(dispatch(y2q.reshape(micro, rows, quarter))).reshape(-1, width)
    xe = xe.astype(f32)
    ne, rse = norm_parts(xe)
    en = (ne * expert_g + expert_b).astype(bf16)
    he = dot(en, win)
    ue = jax.nn.gelu(he).astype(bf16)
    fe_part = dot(ue, wout)
    alpha = jax.nn.sigmoid(jnp.sum(xe * centroid, axis=-1, keepdims=True))
    fe = sum_scatter(fe_part)
    ge = (alpha * fe).astype(bf16).reshape(groups, capacity * micro, quarter)
    block_out = (
        y2q.reshape(micro, rows, quarter).astype(f32) + give_back(ge)
    ).astype(bf16)

    dfe = (alpha * dge).astype(bf16)
    due = dot_nt(dfe, wout)
    grad_out = dot_tn(ue, dfe)
    dhe = gelu_back(he, due).astype(bf16)
    grad_in = dot_tn(en, dhe)
    den_part = dot_nt(dhe, win)
    gden = den_part * expert_g
    stats = lax.psum(
        jnp.stack(
            [
                jnp.mean(gden, axis=-1),
                jnp.mean(gden * ne, axis=-1),
                jnp.sum(dge * fe_part, axis=-1),
            ]
        ),
        "section",
    )[..., None]
    den = sum_scatter(den_part)
    neq = mine(ne)
    dlogit = stats[2] * alpha * (1.0 - alpha)
    dxe_ln = rse * (mine(expert_g) * den - stats[0] - neq * stats[1])
    dxe = (dxe_ln + dlogit * mine(centroid)).astype(bf16)
    grad_expert_gain = jnp.sum(den * neq, axis=0)
    grad_expert_bias = jnp.sum(den, axis=0)
    grad_centroid = jnp.sum(dlogit * mine(xe), axis=0)
    back = give_back(dxe.reshape(groups, capacity * micro, quarter))
    dy2q = (mine(cotangent).astype(f32) + back).astype(bf16).reshape(micro * rows, quarter)

    dy2 = gather_features(dy2q)
    grad_down = dot_tn(u, dy2)
    dh = gelu_back(h, dot_nt(dy2, wdown)).astype(bf16)
    grad_up = dot_tn(a2, dh)
    da2_part = dot_nt(dh, wup)
    gda2 = da2_part * gain_two
    stats = lax.psum(
        jnp.stack([jnp.mean(gda2, axis=-1), jnp.mean(gda2 * n2, axis=-1)]), "section"
    )[..., None]
    da2 = sum_scatter(da2_part)
    n2q = mine(n2)
    dy1q = dy2q.astype(f32) + rs2 * (mine(gain_two) * da2 - stats[0] - n2q * stats[1])
    dy1q = dy1q.astype(bf16)
    dy1 = gather_features(dy1q)
    grad_wo = dot_tn(o, dy1)
    do = dot_nt(dy1, wo).astype(bf16).reshape(micro, rows, heads, size)
    dp = jnp.einsum("mqhd,mkhd->mhqk", do, v, preferred_element_type=f32)
    dv = jnp.einsum("mhqk,mqhd->mkhd", probs_low, do, preferred_element_type=f32)
    delta = jnp.sum(probs * dp, axis=-1, keepdims=True)
    ds = (probs * (dp - delta)).astype(bf16)
    dq = jnp.einsum("mhqk,mkhd->mqhd", ds, k, preferred_element_type=f32) * scale
    dk = jnp.einsum("mhqk,mqhd->mkhd", ds, q, preferred_element_type=f32) * scale
    dqkv = jnp.concatenate(
        [part.reshape(micro * rows, quarter) for part in (dq, dk, dv)], axis=1
    ).astype(bf16)
    grad_qkv = dot_tn(a1, dqkv)
    da1_part = dot_nt(dqkv, wqkv)
    gda1 = da1_part * gain_one
    stats = lax.psum(
        jnp.stack([jnp.mean(gda1, axis=-1), jnp.mean(gda1 * n1, axis=-1)]), "section"
    )[..., None]
    da1 = sum_scatter(da1_part)
    n1q = mine(n1)
    dx = dy1q.astype(f32) + rs1 * (mine(gain_one) * da1 - stats[0] - n1q * stats[1])

    vector_grads = lax.psum_scatter(
        jnp.stack(
            [
                jnp.sum(da1 * n1q, axis=0),
                jnp.sum(da1, axis=0),
                jnp.sum(da2 * n2q, axis=0),
                jnp.sum(da2, axis=0),
            ]
        ),
        "dp",
        scatter_dimension=1,
        tiled=True,
    )
    return (
        block_out,
        dx.reshape(micro, rows, quarter),
        vector_grads[0],
        vector_grads[1],
        column_group_back(grad_qkv, 3),
        row_group_back(grad_wo),
        vector_grads[2],
        vector_grads[3],
        column_group_back(grad_up, 1),
        row_group_back(grad_down),
        grad_in[None],
        grad_out[None],
        grad_expert_gain[None],
        grad_expert_bias[None],
        grad_centroid[None],
    )


def solution(mesh):
    everywhere = ("section", "dp")
    tokens = P(None, "dp", None)
    outs = P(None, "dp", "section")
    per_expert = P("dp", "section")
    return jax.shard_map(
        on_device,
        mesh=mesh,
        in_specs=(
            tokens,
            tokens,
            tokens,
            P(None, "dp"),
            tokens,
            P(everywhere),
            P(everywhere),
            P(everywhere, None),
            P(everywhere, None),
            P(everywhere),
            P(everywhere),
            P(everywhere, None),
            P(everywhere, None),
            P("dp", None, "section"),
            P("dp", "section", None),
            per_expert,
            per_expert,
            per_expert,
        ),
        out_specs=(
            outs,
            outs,
            P(everywhere),
            P(everywhere),
            P(everywhere, None),
            P(everywhere, None),
            P(everywhere),
            P(everywhere),
            P(everywhere, None),
            P(everywhere, None),
            P("dp", None, "section"),
            P("dp", "section", None),
            per_expert,
            per_expert,
            per_expert,
        ),
        check_vma=False,
    )
```

time: 2440 us -> 758 us (0.31)
  waiting for transfers between devices: 1690 us -> 395 us
  loops' own time: 147 us -> 0 us
  starting transfers between devices: 105 us -> 17.4 us
  local copies, waits for them, and re-layouts: 120 us -> 48.1 us
  other arithmetic: 66.6 us -> 37.1 us
    reduce_scatter x8 -> x10, waiting for transfers between devices: 905 us -> 208 us  [the longest x6 106 us: sum_scatter(): lax.psum_scatter(part.astype(bf16), 'section', scatter_dimension=part.ndi...]
    ppermute x16 -> x0, waiting for transfers between devices: 297 us -> none  [passed_along(): return lax.ppermute(shard, axis, pairs)]
    all_gather x6 -> x8, waiting for transfers between devices: 394 us -> 137 us  [the longest x5 85 us: gather_features(): return lax.all_gather(part, 'section', axis=part.ndim - 1, tiled=True)]
    another operation x19 -> x0, loops' own time: 147 us -> none  [the longest x5 121 us: on_device(): lax.switch(branch, [backward_attention, backward_dense, backward_expert,...]
    unnamed x2 -> x0, blocking collectives: 79 us -> none
    ppermute x16 -> x0, starting transfers between devices: 78.6 us -> none  [passed_along(): return lax.ppermute(shard, axis, pairs)]
    all_to_all x6 -> x4, waiting for transfers between devices: 87 us -> 20 us  [the longest x2 20 us: give_back(): out = lax.all_to_all(values, 'dp', split_axis=0, concat_axis=0, tiled=True)]
    broadcast_in_dim x26 -> x0, local copies, waits for them, and re-layouts: 55.2 us -> none  [the longest x6 39.9 us: on_device(): jnp.zeros(weight.shape, jnp.float32)]
  transfers between devices with their start and end apart: 39 -> 23, of which waited for: 26 -> 19; matrix products, arithmetic and copies ran while one was open for 4% -> 13% of each run, Pallas kernels for 0% -> 0%
where the time goes in v1:
time: 758 us; the launch traced here: 748 us
  waiting for transfers between devices  395 us (52%)
  blocking collectives  154 us (20%)
  matrix products  81.7 us (11%)
  local copies, waits for them, and re-layouts  48.1 us (6%)
  other arithmetic  37.1 us (5%)
  starting transfers between devices  17.4 us (2%)
  between operations  15 us (2%)
    reduce_scatter x6, waiting for transfers between devices, sum_scatter(): lax.psum_scatter(part.astype(bf16), 'section', scatter_dimension=part.ndi...  106 us
    all_gather x5, waiting for transfers between devices, gather_features(): return lax.all_gather(part, 'section', axis=part.ndim - 1, tiled=True)  85 us
    reduce_scatter x2, waiting for transfers between devices, row_group_back(): lax.psum_scatter(grad.astype(bf16), 'dp', scatter_dimension=0, tiled=True)  62.5 us
    reduce_scatter x2, waiting for transfers between devices, column_group_back(): parts = lax.psum_scatter(parts, 'dp', scatter_dimension=1, tiled=True)  40.4 us
    all_gather x1, blocking collectives, on_device(): lax.all_gather(jnp.stack([ln1_gain, ln1_bias, ln2_gain, ln2_bias]), ('sec...  40.4 us
    all_to_all x2, blocking collectives, dispatch(): return lax.all_to_all(out, 'dp', split_axis=0, concat_axis=0, tiled=True)  33.9 us
    unnamed x20, waiting for transfers between devices  29.1 us
    all_gather x2, waiting for transfers between devices, column_group(): full = lax.all_gather(parts, 'dp', axis=1, tiled=True)  28.9 us
  transfers between devices with their start and end apart: 23, of which 19 were waited for; matrix products, arithmetic and copies ran while one was open for 13% of the time, Pallas kernels for 0%

profile of v1, /device:TPU:0, one launch (start us, length us, event | category | flops | bytes accessed | tf_op | source)
XLA Modules:
  0.0 747.7 jit_solution(4590724776124472528)
XLA Ops:
  11.1 10.8 %all_to_all.40 = bf16[4,32,768]{2,1,0:T(8,128)(2,1)} all-to-all(bf16[4,32,768]{2,1,0:T(8,128)(2,1)} %reshape.433), channel_id=1, replica_groups=mesh['section'=4,'dp'=8] {'section'}, dimensions={0} | all-to-all | bytes 393216 | tf_op jit(solution)/shard_map/all_to_all | solution.py:86
  22.7 40.4 %all-gather = bf16[32,32,4]{1,2,0:T(4,128)(2,1)S(1)} all-gather(bf16[1,32,4]{1,2,0:T(4,128)(2,1)S(1)} %maximum_bitcast_fusion), channel_id=1, replica_groups=mesh['section'=4,'dp'=8] {'section','dp'}, dimensions={0}, use_global_device_ids=true | all-gather | bytes 8448 | tf_op jit(solution)/shard_map/all_gather | solution.py:103
  66.0 15.8 %all_gather.35 = bf16[256,1024]{1,0:T(8,128)(2,1)} all-gather(bf16[32,1024]{1,0:T(8,128)(2,1)S(1)} %copy-done.26), channel_id=1, replica_groups=mesh['section'=4,'dp'=8] {'dp'}, dimensions={0}, use_global_device_ids=true | all-gather | bytes 589824 | tf_op jit(solution)/shard_map/all_gather | solution.py:112
  107.3 11.4 %all_to_all.41 = bf16[4,32,1024]{2,1,0:T(8,128)(2,1)S(1)} all-to-all(bf16[4,32,1024]{2,1,0:T(8,128)(2,1)S(1)} %copy.205), channel_id=1, replica_groups=mesh['section'=4,'dp'=8] {'section'}, dimensions={0} | all-to-all | bytes 524288 | tf_op jit(solution)/shard_map/all_to_all | solution.py:86
  121.3 10.6 %reduce-scatter.14.cloned.1.call-done = bf16[512,256]{1,0:T(8,128)(2,1)} async-done(((bf16[512,1024]{1,0:T(8,128)(2,1)}), bf16[512,256]{1,0:T(8,128)(2,1)}) %reduce-scatter.14.cloned.1.call-update) | async-done | bytes 262160 | tf_op jit(solution)/shard_map/reduce_scatter | solution.py:38
  134.4 28.8 %all-gather.14.cloned.1.call-done = bf16[4,256,1024]{2,0,1:T(4,128)(2,1)} async-done(((bf16[4,32,1024]{2,0,1:T(4,128)(2,1)}), bf16[4,256,1024]{2,0,1:T(4,128)(2,1)}) %all-gather.14.cloned.1.call-update) | async-done | bytes 2097168 | tf_op jit(solution)/shard_map/all_gather | solution.py:87
  166.9 24.8 %all-gather.12.cloned.1.call-done = bf16[512,1024]{1,0:T(8,128)(2,1)} async-done(((bf16[512,256]{1,0:T(8,128)(2,1)}), bf16[512,1024]{1,0:T(8,128)(2,1)}) %all-gather.12.cloned.1.call-update) | async-done | bytes 1048592 | tf_op jit(solution)/shard_map/all_gather | solution.py:44
  199.2 23.2 %all-gather.16.cloned.1.call-done = bf16[1024,1024]{1,0:T(8,128)(2,1)} async-done(((bf16[128,1024]{1,0:T(8,128)(2,1)}), bf16[1024,1024]{1,0:T(8,128)(2,1)}) %all-gather.16.cloned.1.call-update) | async-done | bytes 2097168 | tf_op jit(solution)/shard_map/all_gather | solution.py:114
  228.8 25.6 %reduce-scatter.16.cloned.1.call-done = bf16[512,256]{1,0:T(8,128)(2,1)} async-done(((bf16[512,1024]{1,0:T(8,128)(2,1)}), bf16[512,256]{1,0:T(8,128)(2,1)}) %reduce-scatter.16.cloned.1.call-update) | async-done | bytes 262160 | tf_op jit(solution)/shard_map/reduce_scatter | solution.py:38
  261.2 17.3 %all_to_all.42 = bf16[8,96,256]{2,1,0:T(8,128)(2,1)} all-to-all(bf16[8,96,256]{2,1,0:T(8,128)(2,1)} %reshape.443), channel_id=1, replica_groups=mesh['section'=4,'dp'=8] {'dp'}, dimensions={0} | all-to-all | bytes 786432 | tf_op jit(solution)/shard_map/all_to_all | solution.py:135
  285.3 16.6 %all_to_all.43 = bf16[8,96,256]{2,1,0:T(8,128)(2,1)} all-to-all(bf16[8,96,256]{2,1,0:T(8,128)(2,1)} %reshape.446), channel_id=1, replica_groups=mesh['section'=4,'dp'=8] {'dp'}, dimensions={0} | all-to-all | bytes 786432 | tf_op jit(solution)/shard_map/all_to_all | solution.py:135
  319.9 20.3 %all-gather.20.cloned.1.call-done = bf16[8,96,1024]{2,1,0:T(8,128)(2,1)} async-done(((bf16[8,96,256]{2,1,0:T(8,128)(2,1)}), bf16[8,96,1024]{2,1,0:T(8,128)(2,1)}) %all-gather.20.cloned.1.call-update) | async-done | bytes 1572880 | tf_op jit(solution)/shard_map/all_gather | solution.py:44
  358.9 15.7 %psum.21 = f32[3,768]{1,0:T(4,128)S(1)} all-reduce(f32[3,768]{1,0:T(4,128)S(1)} %pad_maximum_fusion), channel_id=1, replica_groups=mesh['section'=4,'dp'=8] {'section'}, use_global_device_ids=true, to_apply=%region_21.22 | all-reduce | flops 2304 | bytes 18432 | tf_op jit(solution)/shard_map/psum | solution.py:188
  391.2 12.4 %all-to-all-done.5 = bf16[8,96,256]{2,1,0:T(8,128)(2,1)S(1)} async-done(((bf16[8,96,256]{2,1,0:T(8,128)(2,1)}), bf16[8,96,256]{2,1,0:T(8,128)(2,1)S(1)}, u32[]{:S(2)}, u32[]{:S(2)}) %all-to-all-start.5) | async-done | bytes 393248 | tf_op jit(solution)/shard_map/all_to_all | solution.py:138
  405.1 24.5 %all-gather.22.cloned.1.call-done = bf16[512,1024]{1,0:T(8,128)(2,1)} async-done(((bf16[512,256]{1,0:T(8,128)(2,1)}), bf16[512,1024]{1,0:T(8,128)(2,1)}) %all-gather.22.cloned.1.call-update) | async-done | bytes 1048592 | tf_op jit(solution)/shard_map/all_gather | solution.py:44
  437.9 9.0 %psum.22 = f32[2,512]{1,0:T(2,128)S(1)} all-reduce(f32[2,512]{1,0:T(2,128)S(1)} %pad_maximum_fusion.1), channel_id=1, replica_groups=mesh['section'=4,'dp'=8] {'section'}, use_global_device_ids=true, to_apply=%region_25.26 | all-reduce | flops 1024 | bytes 8192 | tf_op jit(solution)/shard_map/psum | solution.py:215
  447.0 18.7 %reduce-scatter.22.cloned.1.call-done = bf16[512,256]{1,0:T(8,128)(2,1)} async-done(((bf16[512,1024]{1,0:T(8,128)(2,1)}), bf16[512,256]{1,0:T(8,128)(2,1)}) %reduce-scatter.22.cloned.1.call-update) | async-done | bytes 262160 | tf_op jit(solution)/shard_map/reduce_scatter | solution.py:38
  479.1 15.4 %all-gather.24.cloned.1.call-done = bf16[512,1024]{1,0:T(8,128)(2,1)} async-done(((bf16[512,256]{1,0:T(8,128)(2,1)}), bf16[512,1024]{1,0:T(8,128)(2,1)}) %all-gather.24.cloned.1.call-update) | async-done | bytes 1048592 | tf_op jit(solution)/shard_map/all_gather | solution.py:44
  512.0 16.7 %reduce-scatter.18.cloned.1.call-done = bf16[768,256]{1,0:T(8,128)(2,1)} async-done(((bf16[768,1024]{1,0:T(8,128)(2,1)}), bf16[768,256]{1,0:T(8,128)(2,1)}) %reduce-scatter.18.cloned.1.call-update) | async-done | bytes 393232 | tf_op jit(solution)/shard_map/reduce_scatter | solution.py:38
  573.9 33.9 %reduce-scatter.32.cloned.1.call-done = bf16[128,1024]{1,0:T(8,128)(2,1)} async-done(((bf16[1024,1024]{1,0:T(8,128)(2,1)}), bf16[128,1024]{1,0:T(8,128)(2,1)}) %reduce-scatter.32.cloned.1.call-update) | async-done | bytes 262160 | tf_op jit(solution)/shard_map/reduce_scatter | solution.py:99
  609.7 27.7 %reduce-scatter.24.cloned.1.call-done = bf16[512,256]{1,0:T(8,128)(2,1)} async-done(((bf16[512,1024]{1,0:T(8,128)(2,1)}), bf16[512,256]{1,0:T(8,128)(2,1)}) %reduce-scatter.24.cloned.1.call-update) | async-done | bytes 262160 | tf_op jit(solution)/shard_map/reduce_scatter | solution.py:38
  641.9 28.5 %reduce-scatter.28.cloned.1.call-done = bf16[32,1024]{1,0:T(8,128)(2,1)} async-done(((bf16[256,1024]{1,0:T(8,128)(2,1)}), bf16[32,1024]{1,0:T(8,128)(2,1)}) %reduce-scatter.28.cloned.1.call-update) | async-done | bytes 65552 | tf_op jit(solution)/shard_map/reduce_scatter | solution.py:99
  671.9 33.2 %reduce-scatter.26.cloned.1.call-done = bf16[4,32,768]{2,1,0:T(8,128)(2,1)} async-done(((bf16[4,256,768]{2,1,0:T(8,128)(2,1)}), bf16[4,32,768]{2,1,0:T(8,128)(2,1)}) %reduce-scatter.26.cloned.1.call-update) | async-done | bytes 196624 | tf_op jit(solution)/shard_map/reduce_scatter | solution.py:93
  708.7 27.5 %reduce-scatter.34.cloned.1.call-done = f32[32,4]{1,0:T(8,128)} async-done(((f32[256,4]{1,0:T(8,128)}), f32[32,4]{1,0:T(8,128)}) %reduce-scatter.34.cloned.1.call-update) | async-done | bytes 528
  (288 shorter events, 223.8 us)
Async XLA Ops:
  7.2 309.2 %copy-start = (bf16[1,1024,1024]{2,1,0:T(8,128)(2,1)S(1)}, bf16[1,1024,1024]{2,1,0:T(8,128)(2,1)}, u32[]{:S(2)}) copy-start(bf16[1,1024,1024]{2,1,0:T(8,128)(2,1)} %param.31) | copy-start | bytes 6291460
  7.2 76.2 %all-gather.10.cloned.1.call-start = ((), (), s32[]{:S(2)}) async-start(), calls=%async_computation.19 | async-start | bytes 1769472 | tf_op jit(solution)/shard_map/all_gather | solution.py:87
  22.0 109.9 %reduce-scatter.14.cloned.1.call-start = ((), (), s32[]{:S(2)}) async-start(), calls=%async_computation.20 | async-start | bytes 1310720 | tf_op jit(solution)/shard_map/reduce_scatter | solution.py:38
  104.4 58.9 %all-gather.14.cloned.1.call-start = ((), (), s32[]{:S(2)}) async-start(), calls=%async_computation.22 | async-start | bytes 2359296 | tf_op jit(solution)/shard_map/all_gather | solution.py:87
  119.6 72.1 %all-gather.12.cloned.1.call-start = ((), (), s32[]{:S(2)}) async-start(), calls=%async_computation.21 | async-start | bytes 1310720 | tf_op jit(solution)/shard_map/all_gather | solution.py:44
  133.8 88.6 %all-gather.16.cloned.1.call-start = ((), (), s32[]{:S(2)}) async-start(), calls=%async_computation.23 | async-start | bytes 2359296 | tf_op jit(solution)/shard_map/all_gather | solution.py:114
  134.4 120.0 %reduce-scatter.16.cloned.1.call-start = ((), (), s32[]{:S(2)}) async-start(), calls=%async_computation.24 | async-start | bytes 1310720 | tf_op jit(solution)/shard_map/reduce_scatter | solution.py:38
  227.0 83.1 %all-gather.18.cloned.1.call-start = ((), (), s32[]{:S(2)}) async-start(), calls=%async_computation.25 | async-start | bytes 1966080 | tf_op jit(solution)/shard_map/all_gather | solution.py:44
  278.5 61.7 %all-gather.20.cloned.1.call-start = ((), (), s32[]{:S(2)}) async-start(), calls=%async_computation.27 | async-start | bytes 1966080 | tf_op jit(solution)/shard_map/all_gather | solution.py:44
  302.0 81.1 %reduce-scatter.20.cloned.1.call-start = ((), (), s32[]{:S(2)}) async-start(), calls=%async_computation.28 | async-start | bytes 1966080 | tf_op jit(solution)/shard_map/reduce_scatter | solution.py:38
  386.4 17.2 %all-to-all-start.5 = ((bf16[8,96,256]{2,1,0:T(8,128)(2,1)}), bf16[8,96,256]{2,1,0:T(8,128)(2,1)S(1)}, u32[]{:S(2)}, u32[]{:S(2)}) async-start(bf16[8,96,256]{2,1,0:T(8,128)(2,1)} %bitcast.38), calls=%async_computation.9 | async-start | bytes 786432 | tf_op jit(solution)/shard_map/all_to_all | solution.py:138
  391.0 38.6 %all-gather.22.cloned.1.call-start = ((), (), s32[]{:S(2)}) async-start(), calls=%async_computation.29 | async-start | bytes 1310720 | tf_op jit(solution)/shard_map/all_gather | solution.py:44
  405.0 60.7 %reduce-scatter.22.cloned.1.call-start = ((), (), s32[]{:S(2)}) async-start(), calls=%async_computation.30 | async-start | bytes 1310720 | tf_op jit(solution)/shard_map/reduce_scatter | solution.py:38
  437.8 56.7 %all-gather.24.cloned.1.call-start = ((), (), s32[]{:S(2)}) async-start(), calls=%async_computation.31 | async-start | bytes 1310720 | tf_op jit(solution)/shard_map/all_gather | solution.py:44
  467.9 60.9 %reduce-scatter.18.cloned.1.call-start = ((), (), s32[]{:S(2)}) async-start(), calls=%async_computation.26 | async-start | bytes 1966080 | tf_op jit(solution)/shard_map/reduce_scatter | solution.py:38
  468.6 101.9 %reduce-scatter.30.cloned.1.call-start = ((), (), s32[]{:S(2)}) async-start(), calls=%async_computation.35 | async-start | bytes 2359296 | tf_op jit(solution)/shard_map/reduce_scatter | solution.py:93
  472.7 135.1 %reduce-scatter.32.cloned.1.call-start = ((), (), s32[]{:S(2)}) async-start(), calls=%async_computation.36 | async-start | bytes 2359296 | tf_op jit(solution)/shard_map/reduce_scatter | solution.py:99
  478.4 158.9 %reduce-scatter.24.cloned.1.call-start = ((), (), s32[]{:S(2)}) async-start(), calls=%async_computation.32 | async-start | bytes 1310720 | tf_op jit(solution)/shard_map/reduce_scatter | solution.py:38
  506.8 163.6 %reduce-scatter.28.cloned.1.call-start = ((), (), s32[]{:S(2)}) async-start(), calls=%async_computation.34 | async-start | bytes 589824 | tf_op jit(solution)/shard_map/reduce_scatter | solution.py:99
  508.2 196.9 %reduce-scatter.26.cloned.1.call-start = ((), (), s32[]{:S(2)}) async-start(), calls=%async_computation.33 | async-start | bytes 1769472 | tf_op jit(solution)/shard_map/reduce_scatter | solution.py:93
  530.6 22.5 %all-to-all-start.3 = ((bf16[8,96,256]{2,1,0:T(8,128)(2,1)}), bf16[8,96,256]{2,1,0:T(8,128)(2,1)S(1)}, u32[]{:S(2)}, u32[]{:S(2)}) async-start(bf16[8,96,256]{2,1,0:T(8,128)(2,1)} %bitcast.31), calls=%async_computation.6 | async-start | bytes 786432 | tf_op jit(solution)/shard_map/all_to_all | solution.py:138
  570.5 69.9 %all-to-all-start.7 = ((bf16[4,32,1024]{2,1,0:T(8,128)(2,1)}), bf16[4,32,1024]{2,1,0:T(8,128)(2,1)S(1)}, u32[]{:S(2)}, u32[]{:S(2)}) async-start(bf16[4,32,1024]{2,1,0:T(8,128)(2,1)} %reduce-scatter.30.cloned.1.call-done), calls=%async_computation.16 | async-start | bytes 524288 | tf_op jit(solution)/shard_map/all_to_all | solution.py:94
  573.9 162.3 %reduce-scatter.34.cloned.1.call-start = ((), (), s32[]{:S(2)}) async-start(), calls=%async_computation.37 | async-start | bytes 147456
  705.1 34.4 %all-to-all-start.6 = ((bf16[4,32,768]{2,1,0:T(8,128)(2,1)}), bf16[4,32,768]{2,1,0:T(8,128)(2,1)S(1)}, u32[]{:S(2)}, u32[]{:S(2)}) async-start(bf16[4,32,768]{2,1,0:T(8,128)(2,1)} %reduce-scatter.26.cloned.1.call-done), calls=%async_computation.13 | async-start | bytes 393216 | tf_op jit(solution)/shard_map/all_to_all | solution.py:94
  (44 other events, 808.2 us)
Sparse Core Ops, SparseCore 0:
  22.1 24.9 all-gather.9
  104.5 27.3 reduce-scatter.13
  134.2 29.0 all-gather.13
  165.7 25.9 all-gather.11
  193.2 29.0 all-gather.15
  227.1 27.2 reduce-scatter.15
  278.6 28.7 all-gather.17
  309.3 30.8 all-gather.19
  351.8 31.1 reduce-scatter.19
  405.1 24.3 all-gather.21
  437.9 27.7 reduce-scatter.21
  468.0 26.4 all-gather.23
  497.8 30.9 reduce-scatter.17
  531.0 39.4 reduce-scatter.29
  572.7 35.1 reduce-scatter.31
  610.9 26.4 reduce-scatter.23
  639.4 30.9 reduce-scatter.27
  672.7 32.3 reduce-scatter.25
  708.0 28.1 reduce-scatter.33

commit v2 on v1

--- a/solution.py
+++ b/solution.py
@@ -1,6 +1,11 @@
+import functools
+import types
+
 import jax
 import jax.numpy as jnp
 from jax import lax
+from jax.experimental import pallas as pl
+from jax.experimental.pallas import tpu as pltpu
 from jax.sharding import PartitionSpec as P
 
 HEADS = 16
@@ -44,7 +49,7 @@
     return lax.all_gather(part, "section", axis=part.ndim - 1, tiled=True)
 
 
-def on_device(
+def with_collectives(
     hidden_in,
     cotangent,
     bucket_len,
@@ -271,6 +276,948 @@
         grad_expert_bias[None],
         grad_centroid[None],
     )
+
+
+MESH = pl.DeviceIdType.MESH
+KEYS = 320
+CHUNK = 32
+
+
+def tn(a, b):
+    return lax.dot_general(a, b, (((0,), (0,)), ((), ())), preferred_element_type=f32)
+
+
+def nt(a, b):
+    return lax.dot_general(a, b, (((1,), (1,)), ((), ())), preferred_element_type=f32)
+
+
+def tanh_parts(v):
+    root = 0.7978845608028654
+    t = jnp.tanh(root * (v + 0.044715 * (v * v * v)))
+    return t, root
+
+
+def gelu_of(v):
+    t, _ = tanh_parts(v)
+    return v * (0.5 * (1.0 + t))
+
+
+def gelu_slope(v):
+    t, root = tanh_parts(v)
+    return 0.5 * (1.0 + t) + 0.5 * v * (1.0 - t * t) * root * (1.0 + 0.134145 * (v * v))
+
+
+def to_rows(columns):
+    lane = lax.broadcasted_iota(jnp.int32, (columns[0].shape[0], 128), 1)
+    wide = jnp.zeros(lane.shape, f32)
+    for i, column in enumerate(columns):
+        wide = jnp.where(lane == i, column, wide)
+    return wide.T[:8]
+
+
+def to_columns(rows):
+    return jnp.concatenate([rows, jnp.zeros((120, rows.shape[1]), f32)], axis=0).T
+
+
+def layout(dims):
+    S, G, M, T, D, Q, FQ, C, sh, shd = dims
+    nz = G // 2
+    R = G * C
+    heads = HEADS // S
+    return dict(
+        wqkv=((S, nz, 2, sh, 3 * Q), bf16),
+        wo=((nz, 2, sh, D), bf16),
+        wup=((S, nz, 2, sh, FQ), bf16),
+        wdn=((nz, 2, shd, D), bf16),
+        win=((S, nz, 2, sh, FQ), bf16),
+        wout=((nz, 2, shd, D), bf16),
+        vg=((S, G, 8, 128), f32),
+        vecs=((8, D), f32),
+        evec=((8, D), f32),
+        mask=((M, T, T), f32),
+        perm=((M, R, T), bf16),
+        cots=((M, R, Q), bf16),
+        y2s=((M, R, Q), bf16),
+        ges=((M, R, Q), bf16),
+        dxs=((M, R, Q), bf16),
+        ger=((M, R, Q), bf16),
+        dxr=((M, R, Q), bf16),
+        tst=((M, T, 128), f32),
+        est=((M, R, 128), f32),
+        a=((M, T, D), bf16),
+        qkv=((M, T, 3 * Q), bf16),
+        probs=((M, heads, T, T), f32),
+        o=((M, T, Q), bf16),
+        y1=((M, T, D), bf16),
+        h=((M, T, FQ), f32),
+        u=((M, T, FQ), bf16),
+        y2q=((M, T, Q), bf16),
+        xe=((M, R, D), bf16),
+        dge=((M, R, D), bf16),
+        en=((M, R, D), bf16),
+        ue=((M, R, FQ), bf16),
+        dhe=((M, R, FQ), bf16),
+        dfe=((M, R, D), bf16),
+        he=((R, FQ), f32),
+        fes=((M, S - 1, R, Q), bf16),
+        fer=((M, S - 1, R, Q), bf16),
+        feo=((M, R, Q), f32),
+        dns=((M, S - 1, R, Q), bf16),
+        dnr=((M, S - 1, R, Q), bf16),
+        dno=((M, R, Q), f32),
+        ess=((M, 8, R), f32),
+        esr=((M, S - 1, 8, R), f32),
+        ts=((M, S - 1, T, Q), bf16),
+        r1=((M, S - 1, T, Q), bf16),
+        r2=((M, S - 1, T, Q), bf16),
+        own=((M, T, Q), f32),
+        tss=((2, M, 8, T), f32),
+        tsr=((2, M, S - 1, 8, T), f32),
+        dy2=((M, T, D), bf16),
+        dh=((M, T, FQ), bf16),
+        dqkv=((M, T, 3 * Q), bf16),
+        gwo=((nz, 2, sh, D), bf16),
+        gqk=((S, nz, 2, sh, 3 * Q), bf16),
+        bdn=((nz, shd, D), bf16),
+        bup=((S, nz, sh, FQ), bf16),
+        bwo=((nz, sh, D), bf16),
+        bqk=((S, nz, sh, 3 * Q), bf16),
+        zdn=((nz - 1, shd, D), bf16),
+        zup=((nz - 1, S, sh, FQ), bf16),
+        zwo=((nz - 1, sh, D), bf16),
+        zqk=((nz - 1, S, sh, 3 * Q), bf16),
+        ups=((S, sh, FQ), bf16),
+        upr=((S - 1, sh, FQ), bf16),
+        qks=((S, sh, 3 * Q), bf16),
+        qkr=((S - 1, sh, 3 * Q), bf16),
+        stage=((2, 256, D), f32),
+        vsum=((8, Q), f32),
+        vsr=((G - 1, 8, Q), f32),
+    )
+
+
+INPUTS = [
+    "hidden",
+    "cot",
+    "bucket",
+    "live",
+    "routes",
+    "vin",
+    "ein",
+    "wqkv_in",
+    "wo_in",
+    "wup_in",
+    "wdn_in",
+    "win_in",
+    "wout_in",
+]
+OUTPUTS = [
+    "out",
+    "dx",
+    "vgo",
+    "gqk_out",
+    "gwo_out",
+    "gup_out",
+    "gdn_out",
+    "gin_out",
+    "gout_out",
+    "evo",
+]
+
+
+def block_kernel(dims, names, *args):
+    r = types.SimpleNamespace(**dict(zip(names, args)))
+    S, G, M, T, D, Q, FQ, C, sh, shd = dims
+    nz = G // 2
+    R = G * C
+    heads = HEADS // S
+    size = D // HEADS
+    scale = size ** (-0.5)
+    s = lax.axis_index("section")
+    d = lax.axis_index("dp")
+    z = lax.div(d, 2)
+    c = lax.rem(d, 2)
+    beside = (s, d + 1 - 2 * c)
+
+    def sec(i):
+        return lax.rem(s + i, S)
+
+    def dpi(j):
+        return lax.rem(d + j, G)
+
+    def zi(j):
+        return lax.rem(z + j, nz)
+
+    def to_sec(i):
+        return (sec(i), d)
+
+    def to_dp(j):
+        return (s, dpi(j))
+
+    def to_z(j):
+        return (s, zi(j) * 2 + c)
+
+    def col(q, n=Q):
+        return pl.ds(pl.multiple_of(q * n, n), n)
+
+    def seats(e):
+        return pl.ds(pl.multiple_of(e * C, C), C)
+
+    mine = col(s)
+    places = {}
+    pending = {}
+
+    def copy(src, dst, k, device):
+        i = places.setdefault(k, len(places))
+        return pltpu.make_async_remote_copy(
+            src_ref=src,
+            dst_ref=dst,
+            send_sem=r.ssem.at[i],
+            recv_sem=r.rsem.at[i],
+            device_id=device,
+            device_id_type=MESH,
+        )
+
+    def send(src, dst, k, device):
+        pending[k] = copy(src, dst, k, device)
+        pending[k].start()
+
+    def sent(k):
+        pending.pop(k).wait_send()
+
+    def recv(dst, k):
+        copy(dst, dst, k, beside).wait_recv()
+
+    def each(rows, step, body):
+        @pl.loop(0, rows // step)
+        def _(i):
+            body(pl.ds(pl.multiple_of(i * step, step), step))
+
+    others = range(1, S)
+
+    def gather_send(ref, m, k):
+        for i in others:
+            send(ref.at[m, :, mine], ref.at[m, :, mine], (k, m, i), to_sec(i))
+
+    def gather_recv(ref, m, k):
+        for i in others:
+            recv(ref.at[m, :, col(sec(S - i))], (k, m, i))
+
+    def sum_send(tile, out, arrive, own, m, k, before=None, hold=False):
+        for i in others:
+            if before is not None:
+                sent((before, m, i))
+            out[m, i - 1] = tile(sec(i)).astype(bf16)
+            if not hold:
+                send(out.at[m, i - 1], arrive.at[m, i - 1], (k, m, i), to_sec(i))
+        own[m] = tile(s)
+
+    def sum_start(out, arrive, m, k):
+        for i in others:
+            send(out.at[m, i - 1], arrive.at[m, i - 1], (k, m, i), to_sec(i))
+
+    def sum_recv(arrive, m, k):
+        for i in others:
+            recv(arrive.at[m, i - 1], (k, m, i))
+
+    def summed(own, arrive, m, rows):
+        total = own[m, rows]
+        for i in others:
+            total += arrive[m, i - 1, rows].astype(f32)
+        return total
+
+    def dispatch_send(src, dst, m, k):
+        dst[m, seats(d), mine] = src[m, seats(d)]
+        for j in range(1, G):
+            send(src.at[m, seats(dpi(j))], dst.at[m, seats(d), mine], (k, m, j), to_dp(j))
+
+    def dispatch_recv(dst, m, k):
+        for j in range(1, G):
+            recv(dst.at[m, seats(dpi(G - j)), mine], (k, m, j))
+
+    def return_send(src, dst, m, k):
+        dst[m, seats(d)] = src[m, seats(d)]
+        for j in range(1, G):
+            send(src.at[m, seats(dpi(j))], dst.at[m, seats(d)], (k, m, j), to_dp(j))
+
+    def return_recv(dst, m, k):
+        for j in range(1, G):
+            recv(dst.at[m, seats(dpi(G - j))], (k, m, j))
+
+    def part(ref, zz, cc):
+        return ref.at[:, zz, cc] if len(ref.shape) == 5 else ref.at[zz, cc]
+
+    def weight_start(ref, k):
+        for j in range(1, nz):
+            send(part(ref, z, c), part(ref, z, c), (k, "z", j), to_z(j))
+        send(part(ref, z, c), part(ref, z, c), (k, "c", 0), beside)
+
+    def weight_wait(ref, k):
+        for j in range(1, nz):
+            zz = zi(nz - j)
+            recv(part(ref, zz, c), (k, "z", j))
+            send(part(ref, zz, c), part(ref, zz, c), (k, "c", j), beside)
+        for j in range(nz):
+            recv(part(ref, zi(nz - j) if j else z, 1 - c), (k, "c", j))
+
+    barrier = pltpu.get_barrier_semaphore()
+    for i in others:
+        pl.semaphore_signal(barrier, inc=1, device_id=to_sec(i), device_id_type=MESH)
+    for j in range(1, G):
+        pl.semaphore_signal(barrier, inc=1, device_id=to_dp(j), device_id_type=MESH)
+    pl.semaphore_wait(barrier, S + G - 2)
+
+    load_in = pltpu.make_async_copy(r.win_in, r.win, r.lsem.at[0])
+    load_out = pltpu.make_async_copy(r.wout_in, r.wout, r.lsem.at[1])
+    for i in others:
+        for piece in range(3):
+            src = r.wqkv_in.at[:, pl.ds(pl.multiple_of(piece * D + sec(i) * Q, Q), Q)]
+            dst = r.wqkv.at[s, z, c, :, piece * Q : (piece + 1) * Q]
+            send(src, dst, ("q1", piece, i), to_sec(i))
+        send(r.vin, r.vg.at[s, d], ("v1", i), to_sec(i))
+        send(r.ein, r.evec.at[:, mine], ("e1", i), to_sec(i))
+    for i in others:
+        send(r.wup_in.at[:, col(sec(i), FQ)], r.wup.at[s, z, c], ("u1", i), to_sec(i))
+    load_in.start()
+    load_out.start()
+    for piece in range(3):
+        r.wqkv[s, z, c, :, piece * Q : (piece + 1) * Q] = r.wqkv_in[
+            :, pl.ds(pl.multiple_of(piece * D + s * Q, Q), Q)
+        ]
+    r.wup[s, z, c] = r.wup_in[:, col(s, FQ)]
+    r.wo[z, c] = r.wo_in[...]
+    r.wdn[z, c] = r.wdn_in[...]
+    r.vg[s, d] = r.vin[...]
+    r.evec[:, mine] = r.ein[...]
+
+    early = lax.broadcasted_iota(jnp.int32, (T, T), 0)
+    late = lax.broadcasted_iota(jnp.int32, (T, T), 1)
+    for m in range(M):
+        route = r.routes[m : m + 1, :]
+        expert_ids = lax.broadcasted_iota(jnp.int32, (G, T), 0)
+        picks = jnp.where(expert_ids == route, 1.0, 0.0)
+        before = jnp.where(early < late, 1.0, 0.0).astype(bf16)
+        counts = jnp.dot(picks.astype(bf16), before, preferred_element_type=f32)
+        rank = jnp.sum(counts * picks, axis=0, keepdims=True)
+        place = route.astype(f32) * float(C) + rank
+        seat_ids = lax.broadcasted_iota(jnp.int32, (R, T), 0).astype(f32)
+        r.perm[m] = jnp.where(seat_ids == place, 1.0, 0.0).astype(bf16)
+        r.cots[m] = jnp.dot(r.perm[m], r.cot[m, :, mine], preferred_element_type=f32).astype(bf16)
+
+    for i in others:
+        for piece in range(3):
+            recv(r.wqkv.at[sec(S - i), z, c, :, piece * Q : (piece + 1) * Q], ("q1", piece, i))
+    weight_start(r.wqkv, "wqkv")
+    for i in others:
+        recv(r.vg.at[sec(S - i), d], ("v1", i))
+        recv(r.evec.at[:, col(sec(S - i))], ("e1", i))
+    for j in range(1, G):
+        send(r.vg.at[:, d], r.vg.at[:, d], ("v2", j), to_dp(j))
+    for m in range(M):
+        dispatch_send(r.cots, r.dge, m, "cot")
+    weight_start(r.wo, "wo")
+
+    for m in range(M):
+        end = r.bucket[m, 0]
+        seg_q = (early >= end).astype(jnp.int32)
+        seg_k = (late >= end).astype(jnp.int32)
+        for b in range(1, r.bucket.shape[1]):
+            end = end + r.bucket[m, b]
+            seg_q += (early >= end).astype(jnp.int32)
+            seg_k += (late >= end).astype(jnp.int32)
+        live = jnp.broadcast_to(r.live[m : m + 1, :], (T, T))
+        allowed = (seg_q == seg_k) & (late <= early) & ((live == 1) | (late == early))
+        r.mask[m] = jnp.where(allowed, 1.0, 0.0)
+
+    for j in range(1, G):
+        recv(r.vg.at[:, dpi(G - j)], ("v2", j))
+    spread_row = lax.broadcasted_iota(jnp.int32, (128, D), 0)
+    spread_lane = lax.broadcasted_iota(jnp.int32, (128, D), 1)
+    spread = jnp.where(lax.rem(spread_lane, sh) == spread_row, 1.0, 0.0).astype(bf16)
+    stacked = r.vg[...].reshape(S * G * 8, 128).astype(bf16)
+    wide = jnp.dot(stacked, spread, preferred_element_type=f32)
+    row_id = lax.broadcasted_iota(jnp.int32, (S * G * 8, D), 0)
+    lane_id = lax.broadcasted_iota(jnp.int32, (S * G * 8, D), 1)
+    low = lax.shift_right_logical(row_id, 3) * sh
+    wide = jnp.where((lane_id >= low) & (lane_id < low + sh), wide, 0.0)
+    r.vecs[...] = jnp.sum(wide.reshape(S * G, 8, D), axis=0)
+
+    def normed(values):
+        mean = jnp.mean(values, axis=1, keepdims=True)
+        center = values - mean
+        rs = lax.rsqrt(jnp.mean(center * center, axis=1, keepdims=True) + epsilon)
+        return center * rs, mean, rs
+
+    def norm_tokens(src, m, at, keep):
+        gain = r.vecs[2 * at : 2 * at + 1, :]
+        bias = r.vecs[2 * at + 1 : 2 * at + 2, :]
+
+        def body(rows):
+            n, mean, rs = normed(src[m, rows].astype(f32))
+            if keep:
+                r.tst[m, rows, 2 * at : 2 * at + 1] = mean
+                r.tst[m, rows, 2 * at + 1 : 2 * at + 2] = rs
+            r.a[m, rows] = (n * gain + bias).astype(bf16)
+
+        each(T, CHUNK, body)
+
+    for m in range(M):
+        norm_tokens(r.hidden, m, 0, True)
+    for i in others:
+        recv(r.wup.at[sec(S - i), z, c], ("u1", i))
+    weight_start(r.wup, "wup")
+    weight_wait(r.wqkv, "wqkv")
+    weight_start(r.wdn, "wdn")
+
+    def attend(m):
+        @pl.loop(0, 3)
+        def _(t):
+            w = r.wqkv[:, :, :, :, col(t)].reshape(D, Q)
+            r.qkv[m, :, col(t)] = jnp.dot(r.a[m], w, preferred_element_type=f32).astype(bf16)
+
+        for hh in range(heads):
+            at = hh * size
+            q = r.qkv[m, :, at : at + size]
+            k = r.qkv[m, :, Q + at : Q + at + size]
+            v = r.qkv[m, :, 2 * Q + at : 2 * Q + at + size]
+            scores = jnp.where(r.mask[m] > 0.0, nt(q, k) * scale, masked_value)
+            weights = jnp.exp(scores - jnp.max(scores, axis=1, keepdims=True))
+            p = weights / jnp.sum(weights, axis=1, keepdims=True)
+            r.probs[m, hh] = p
+            mixed = jnp.dot(p.astype(bf16), v, preferred_element_type=f32)
+            r.o[m, :, at : at + size] = mixed.astype(bf16)
+
+    def y1_tile(m):
+        return lambda q: jnp.dot(
+            r.o[m], r.wo[:, :, :, col(q)].reshape(Q, Q), preferred_element_type=f32
+        )
+
+    attend(0)
+    weight_wait(r.wo, "wo")
+    sum_send(y1_tile(0), r.ts, r.r1, r.own, 0, "y1")
+    attend(1)
+    sum_send(y1_tile(1), r.ts, r.r1, r.own, 1, "y1")
+    weight_wait(r.wup, "wup")
+
+    def finish_y1(m):
+        sum_recv(r.r1, m, "y1")
+
+        def body(rows):
+            total = r.hidden[m, rows, mine].astype(f32) + summed(r.own, r.r1, m, rows)
+            r.y1[m, rows, mine] = total.astype(bf16)
+
+        each(T, 64, body)
+        gather_send(r.y1, m, "y1g")
+
+    finish_y1(0)
+    finish_y1(1)
+    for m in range(M):
+        dispatch_recv(r.dge, m, "cot")
+        gather_send(r.dge, m, "dge")
+
+    def up(m):
+        gather_recv(r.y1, m, "y1g")
+        norm_tokens(r.y1, m, 1, True)
+
+        @pl.loop(0, FQ // Q)
+        def _(t):
+            w = r.wup[:, :, :, :, col(t)].reshape(D, Q)
+            pre = jnp.dot(r.a[m], w, preferred_element_type=f32)
+            r.h[m, :, col(t)] = pre
+            r.u[m, :, col(t)] = gelu_of(pre).astype(bf16)
+
+    def y2_tile(m):
+        return lambda q: jnp.dot(
+            r.u[m], r.wdn[:, :, :, col(q)].reshape(FQ, Q), preferred_element_type=f32
+        )
+
+    up(0)
+    weight_wait(r.wdn, "wdn")
+    sum_send(y2_tile(0), r.ts, r.r2, r.own, 0, "y2", "y1")
+    up(1)
+    sum_send(y2_tile(1), r.ts, r.r2, r.own, 1, "y2", "y1")
+
+    def finish_y2(m):
+        sum_recv(r.r2, m, "y2")
+
+        def body(rows):
+            total = r.y1[m, rows, mine].astype(f32) + summed(r.own, r.r2, m, rows)
+            r.y2q[m, rows] = total.astype(bf16)
+
+        each(T, 64, body)
+        r.y2s[m] = jnp.dot(r.perm[m], r.y2q[m], preferred_element_type=f32).astype(bf16)
+        dispatch_send(r.y2s, r.xe, m, "y2d")
+
+    finish_y2(0)
+    finish_y2(1)
+    for m in range(M):
+        dispatch_recv(r.xe, m, "y2d")
+        gather_send(r.xe, m, "xe")
+    load_in.wait()
+    load_out.wait()
+
+    def expert(m):
+        gather_recv(r.dge, m, "dge")
+        gather_recv(r.xe, m, "xe")
+        gain, bias, centroid = r.evec[0:1, :], r.evec[1:2, :], r.evec[2:3, :]
+
+        def body(rows):
+            v = r.xe[m, rows].astype(f32)
+            n, mean, rs = normed(v)
+            alpha = jax.nn.sigmoid(jnp.sum(v * centroid, axis=1, keepdims=True))
+            r.est[m, rows, 0:1] = mean
+            r.est[m, rows, 1:2] = rs
+            r.est[m, rows, 2:3] = alpha
+            r.en[m, rows] = (n * gain + bias).astype(bf16)
+            r.dfe[m, rows] = (alpha * r.dge[m, rows].astype(f32)).astype(bf16)
+
+        each(R, CHUNK, body)
+
+        @pl.loop(0, FQ // Q)
+        def _(t):
+            w = r.win[:, :, :, :, col(t)].reshape(D, Q)
+            pre = jnp.dot(r.en[m], w, preferred_element_type=f32)
+            r.ue[m, :, col(t)] = gelu_of(pre).astype(bf16)
+            due = nt(r.dfe[m], r.wout[t].reshape(Q, D))
+            r.dhe[m, :, col(t)] = (due * gelu_slope(pre)).astype(bf16)
+
+        stats = [jnp.zeros((R, 1), f32) for _ in range(3)]
+
+        def fe_tile(q):
+            tile = jnp.dot(
+                r.ue[m], r.wout[:, :, :, col(q)].reshape(FQ, Q), preferred_element_type=f32
+            )
+            stats[2] += jnp.sum(tile * r.dge[m, :, col(q)].astype(f32), axis=1, keepdims=True)
+            return tile
+
+        def den_tile(q):
+            tile = nt(r.dhe[m], r.win[q].reshape(Q, FQ))
+            scaled = tile * r.evec[0:1, col(q)]
+            n = (r.xe[m, :, col(q)].astype(f32) - r.est[m, :, 0:1]) * r.est[m, :, 1:2]
+            stats[0] += jnp.sum(scaled, axis=1, keepdims=True)
+            stats[1] += jnp.sum(scaled * n, axis=1, keepdims=True)
+            return tile
+
+        sum_send(fe_tile, r.fes, r.fer, r.feo, m, "fe", hold=True)
+        sum_send(den_tile, r.dns, r.dnr, r.dno, m, "den")
+        r.ess[m] = to_rows(stats)
+        for i in others:
+            send(r.ess.at[m], r.esr.at[m, i - 1], ("est", m, i), to_sec(i))
+
+    expert(0)
+    expert(1)
+
+    def finish_den(m):
+        sum_recv(r.dnr, m, "den")
+        total = r.ess[m]
+        for i in others:
+            recv(r.esr.at[m, i - 1], ("est", m, i))
+            total += r.esr[m, i - 1]
+        r.est[m, :, 8:16] = to_columns(total)[:, 0:8]
+        gain, centroid = r.evec[0:1, mine], r.evec[2:3, mine]
+        if m == 0:
+            r.evo[...] = jnp.zeros_like(r.evo)
+
+        def body(rows):
+            den = summed(r.dno, r.dnr, m, rows)
+            xq = r.xe[m, rows, mine].astype(f32)
+            rs, alpha = r.est[m, rows, 1:2], r.est[m, rows, 2:3]
+            n = (xq - r.est[m, rows, 0:1]) * rs
+            m1, m2 = r.est[m, rows, 8:9] * (1.0 / D), r.est[m, rows, 9:10] * (1.0 / D)
+            dlogit = r.est[m, rows, 10:11] * alpha * (1.0 - alpha)
+            grad = rs * (gain * den - m1 - n * m2) + dlogit * centroid
+            r.dxs[m, rows] = grad.astype(bf16)
+            r.evo[0:1, :] += jnp.sum(den * n, axis=0, keepdims=True)
+            r.evo[1:2, :] += jnp.sum(den, axis=0, keepdims=True)
+            r.evo[2:3, :] += jnp.sum(dlogit * xq, axis=0, keepdims=True)
+
+        each(R, 64 if R % 64 == 0 else CHUNK, body)
+        return_send(r.dxs, r.dxr, m, "dxb")
+
+    finish_den(0)
+    finish_den(1)
+    for m in range(M):
+        sum_start(r.fes, r.fer, m, "fe")
+
+    writes = []
+    for left, right, out in ((r.en, r.dhe, r.gin_out), (r.ue, r.dfe, r.gout_out)):
+        for t in range(D // 256):
+            slot = len(writes) % 2
+            if len(writes) >= 2:
+                writes[-2].wait()
+            rows = slice(t * 256, (t + 1) * 256)
+            lhs = left[:, :, rows].reshape(M * R, 256)
+            r.stage[slot] = tn(lhs, right[...].reshape(M * R, D))
+            writes.append(pltpu.make_async_copy(r.stage.at[slot], out.at[rows], r.lsem.at[2 + slot]))
+            writes[-1].start()
+
+    def finish_dxe(m):
+        return_recv(r.dxr, m, "dxb")
+        back = tn(r.perm[m], r.dxr[m])
+        r.dy2[m, :, mine] = (r.cot[m, :, mine].astype(f32) + back).astype(bf16)
+        gather_send(r.dy2, m, "dy2")
+
+    finish_dxe(0)
+    finish_dxe(1)
+
+    def token_stats(m, at, src):
+        stats = [jnp.zeros((T, 1), f32) for _ in range(2)]
+
+        def add(q, tile):
+            scaled = tile * r.vecs[2 * at : 2 * at + 1, col(q)]
+            mean, rs = r.tst[m, :, 2 * at : 2 * at + 1], r.tst[m, :, 2 * at + 1 : 2 * at + 2]
+            n = (src[m, :, col(q)].astype(f32) - mean) * rs
+            stats[0] += jnp.sum(scaled, axis=1, keepdims=True)
+            stats[1] += jnp.sum(scaled * n, axis=1, keepdims=True)
+            return tile
+
+        return stats, add
+
+    def stats_send(m, at, stats):
+        r.tss[at, m] = to_rows(stats)
+        for i in others:
+            send(r.tss.at[at, m], r.tsr.at[at, m, i - 1], ("tst", at, m, i), to_sec(i))
+
+    def stats_recv(m, at):
+        total = r.tss[at, m]
+        for i in others:
+            recv(r.tsr.at[at, m, i - 1], ("tst", at, m, i))
+            total += r.tsr[at, m, i - 1]
+        r.tst[m, :, 8:16] = to_columns(total)[:, 0:8]
+
+    def dense_back(m):
+        gather_recv(r.dy2, m, "dy2")
+
+        @pl.loop(0, FQ // Q)
+        def _(t):
+            du = nt(r.dy2[m], r.wdn[t].reshape(Q, D))
+            r.dh[m, :, col(t)] = (du * gelu_slope(r.h[m, :, col(t)])).astype(bf16)
+
+        stats, add = token_stats(m, 1, r.y1)
+        sum_send(
+            lambda q: add(q, nt(r.dh[m], r.wup[q].reshape(Q, FQ))),
+            r.ts,
+            r.r1,
+            r.own,
+            m,
+            "da2",
+            "y2",
+        )
+        stats_send(m, 1, stats)
+
+    def norm_back(m, at, src, grad_in, own, arrive, emit):
+        gain = r.vecs[2 * at : 2 * at + 1, mine]
+
+        def body(rows):
+            grad = summed(own, arrive, m, rows)
+            mean, rs = r.tst[m, rows, 2 * at : 2 * at + 1], r.tst[m, rows, 2 * at + 1 : 2 * at + 2]
+            n = (src[m, rows, mine].astype(f32) - mean) * rs
+            m1, m2 = r.tst[m, rows, 8:9] * (1.0 / D), r.tst[m, rows, 9:10] * (1.0 / D)
+            emit(rows, grad_in[m, rows, mine].astype(f32) + rs * (gain * grad - m1 - n * m2))
+            r.vsum[2 * at : 2 * at + 1, :] += jnp.sum(grad * n, axis=0, keepdims=True)
+            r.vsum[2 * at + 1 : 2 * at + 2, :] += jnp.sum(grad, axis=0, keepdims=True)
+
+        each(T, 64, body)
+
+    def finish_da2(m):
+        sum_recv(r.r1, m, "da2")
+        stats_recv(m, 1)
+        for i in others:
+            sent(("y1g", m, i))
+
+        def emit(rows, value):
+            r.y1[m, rows, mine] = value.astype(bf16)
+
+        norm_back(m, 1, r.y1, r.dy2, r.own, r.r1, emit)
+        gather_send(r.y1, m, "dy1")
+
+    def grads_pair(g, b, k):
+        src = g.at[:, :, 1 - c] if len(g.shape) == 5 else g.at[:, 1 - c]
+        send(src, b, (k, "p"), beside)
+
+    def grads_spread(g, b, arrive, k):
+        recv(b, (k, "p"))
+        if len(g.shape) == 5:
+
+            @pl.loop(0, nz)
+            def _(zz):
+                for q in range(S):
+                    g[q, zz, c] = (g[q, zz, c].astype(f32) + b[q, zz].astype(f32)).astype(bf16)
+        else:
+
+            @pl.loop(0, nz)
+            def _(zz):
+                g[zz, c] = (g[zz, c].astype(f32) + b[zz].astype(f32)).astype(bf16)
+
+        for j in range(1, nz):
+            send(part(g, zi(j), c), arrive.at[j - 1], (k, "g", j), to_z(j))
+
+    def grads_recv(arrive, k):
+        for j in range(1, nz):
+            recv(arrive.at[j - 1], (k, "g", j))
+
+    dense_back(0)
+    dense_back(1)
+
+    @pl.loop(0, nz)
+    def _(t):
+        lhs = r.u[:, :, col(t)].reshape(M * T, Q)
+        grad = tn(lhs, r.dy2[...].reshape(M * T, D))
+        r.wout[t] = grad.astype(bf16).reshape(2, shd, D)
+
+    grads_pair(r.wout, r.bdn, "gdn")
+
+    r.vsum[...] = jnp.zeros_like(r.vsum)
+    finish_da2(0)
+    finish_da2(1)
+
+    @pl.loop(0, S)
+    def _(t):
+        lhs = r.a[:, :, col(t)].reshape(M * T, Q)
+        grad = tn(lhs, r.dh[...].reshape(M * T, FQ))
+        r.win[t] = grad.astype(bf16).reshape(nz, 2, sh, FQ)
+
+    grads_pair(r.win, r.bup, "gup")
+    grads_spread(r.wout, r.bdn, r.zdn, "gdn")
+
+    def finish_fe(m):
+        sum_recv(r.fer, m, "fe")
+
+        def body(rows):
+            fe = summed(r.feo, r.fer, m, rows)
+            r.ges[m, rows] = (r.est[m, rows, 2:3] * fe).astype(bf16)
+
+        each(R, 64 if R % 64 == 0 else CHUNK, body)
+        return_send(r.ges, r.ger, m, "geb")
+
+    for m in range(M):
+        norm_tokens(r.hidden, m, 0, False)
+        finish_fe(m)
+
+    def attend_back(m):
+        gather_recv(r.y1, m, "dy1")
+        out_grad = nt(r.y1[m], r.wo[...].reshape(Q, D)).astype(bf16)
+        for hh in range(heads):
+            at = hh * size
+            q = r.qkv[m, :, at : at + size]
+            k = r.qkv[m, :, Q + at : Q + at + size]
+            v = r.qkv[m, :, 2 * Q + at : 2 * Q + at + size]
+            go = out_grad[:, at : at + size]
+            p = r.probs[m, hh]
+            dp = nt(go, v)
+            dv = tn(p.astype(bf16), go)
+            ds = (p * (dp - jnp.sum(p * dp, axis=1, keepdims=True))).astype(bf16)
+            dq = jnp.dot(ds, k, preferred_element_type=f32) * scale
+            dk = tn(ds, q) * scale
+            r.dqkv[m, :, at : at + size] = dq.astype(bf16)
+            r.dqkv[m, :, Q + at : Q + at + size] = dk.astype(bf16)
+            r.dqkv[m, :, 2 * Q + at : 2 * Q + at + size] = dv.astype(bf16)
+        stats, add = token_stats(m, 0, r.hidden)
+        sum_send(
+            lambda q: add(q, nt(r.dqkv[m], r.wqkv[q].reshape(Q, 3 * Q))),
+            r.ts,
+            r.r2,
+            r.own,
+            m,
+            "da1",
+            "da2",
+        )
+        stats_send(m, 0, stats)
+
+    attend_back(0)
+    attend_back(1)
+
+    @pl.loop(0, S)
+    def _(t):
+        lhs = r.a[:, :, col(t)].reshape(M * T, Q)
+        grad = tn(lhs, r.dqkv[...].reshape(M * T, 3 * Q))
+        r.gqk[t] = grad.astype(bf16).reshape(nz, 2, sh, 3 * Q)
+
+    grads_pair(r.gqk, r.bqk, "gqk")
+    grad = tn(r.o[...].reshape(M * T, Q), r.y1[...].reshape(M * T, D))
+    r.gwo[...] = grad.astype(bf16).reshape(nz, 2, sh, D)
+    grads_pair(r.gwo, r.bwo, "gwo")
+    grads_spread(r.win, r.bup, r.zup, "gup")
+    grads_spread(r.gqk, r.bqk, r.zqk, "gqk")
+    grads_spread(r.gwo, r.bwo, r.zwo, "gwo")
+
+    def finish_da1(m):
+        sum_recv(r.r2, m, "da1")
+        stats_recv(m, 0)
+
+        def emit(rows, value):
+            r.dx[m, rows] = value
+
+        norm_back(m, 0, r.hidden, r.y1, r.own, r.r2, emit)
+
+    finish_da1(0)
+    finish_da1(1)
+    for j in range(1, G):
+        send(r.vsum, r.vsr.at[j - 1], ("vs", j), to_dp(j))
+
+    for m in range(M):
+        return_recv(r.ger, m, "geb")
+        back = tn(r.perm[m], r.ger[m])
+        r.out[m] = (r.y2q[m].astype(f32) + back).astype(bf16)
+
+    def row_result(g, arrive, out, k, rows):
+        grads_recv(arrive, k)
+        mine_part = part(g, z, c)
+
+        def body(at):
+            total = mine_part[at].astype(f32)
+            for j in range(1, nz):
+                total += arrive[j - 1, at].astype(f32)
+            out[at] = total
+
+        each(rows, CHUNK, body)
+
+    def column_send(g, arrive, out, back, k):
+        grads_recv(arrive, k)
+
+        @pl.loop(0, S)
+        def _(q):
+            total = g[q, z, c].astype(f32)
+            for j in range(1, nz):
+                total += arrive[j - 1, q].astype(f32)
+            out[q] = total.astype(bf16)
+
+        for i in others:
+            send(out.at[sec(i)], back.at[i - 1], (k, "s", i), to_sec(i))
+
+    def column_result(sums, back, out, pieces, k):
+        width = sums.shape[2] // pieces
+        for i in range(S):
+            if i:
+                recv(back.at[i - 1], (k, "s", i))
+            q = sec(S - i) if i else s
+            value = (back[i - 1] if i else sums[s]).astype(f32)
+            for piece in range(pieces):
+                at = pl.ds(pl.multiple_of(piece * S * width + q * width, width), width)
+                out[:, at] = value[:, piece * width : (piece + 1) * width]
+
+    row_result(r.wout, r.zdn, r.gdn_out, "gdn", shd)
+    column_send(r.win, r.zup, r.ups, r.upr, "gup")
+    column_send(r.gqk, r.zqk, r.qks, r.qkr, "gqk")
+    row_result(r.gwo, r.zwo, r.gwo_out, "gwo", sh)
+    total = r.vsum[...]
+    for j in range(1, G):
+        recv(r.vsr.at[j - 1], ("vs", j))
+        total += r.vsr[j - 1]
+    r.vgo[...] = total
+    column_result(r.ups, r.upr, r.gup_out, 1, "gup")
+    column_result(r.qks, r.qkr, r.gqk_out, 3, "gqk")
+    for write in writes[-2:]:
+        write.wait()
+    for k in list(pending):
+        sent(k)
+    assert len(places) <= KEYS, len(places)
+
+
+def with_kernel(
+    hidden_in,
+    cotangent,
+    bucket_len,
+    live_mask,
+    routes,
+    ln1_gain,
+    ln1_bias,
+    w_qkv,
+    w_attn_out,
+    ln2_gain,
+    ln2_bias,
+    w_up,
+    w_down,
+    expert_in,
+    expert_out,
+    expert_gain,
+    expert_bias,
+    centroids,
+):
+    S = lax.axis_size("section")
+    G = lax.axis_size("dp")
+    M, T, D = hidden_in.shape
+    Q = D // S
+    FQ = w_up.shape[1] // S
+    C = 3 * T // (2 * G)
+    sh, shd = w_up.shape[0], w_down.shape[0]
+    dims = (S, G, M, T, D, Q, FQ, C, sh, shd)
+    vin = jnp.stack([ln1_gain, ln1_bias, ln2_gain, ln2_bias]).astype(f32)
+    vin = jnp.pad(vin, ((0, 4), (0, 128 - sh)))
+    ein = jnp.concatenate([expert_gain, expert_bias, centroids]).astype(f32)
+    ein = jnp.pad(ein, ((0, 5), (0, 0)))
+    scratch = layout(dims)
+    names = INPUTS + OUTPUTS + list(scratch) + ["ssem", "rsem", "lsem"]
+    vmem = pl.BlockSpec(memory_space=pltpu.VMEM)
+    smem = pl.BlockSpec(memory_space=pltpu.SMEM)
+    anywhere = pl.BlockSpec(memory_space=pl.ANY)
+    shapes = (
+        ((M, T, Q), bf16),
+        ((M, T, Q), f32),
+        ((8, Q), f32),
+        ((sh, 3 * D), f32),
+        ((sh, D), f32),
+        ((sh, S * FQ), f32),
+        ((shd, D), f32),
+        ((D, FQ), f32),
+        ((FQ, D), f32),
+        ((8, Q), f32),
+    )
+    outs = pl.pallas_call(
+        functools.partial(block_kernel, dims, names),
+        name="block",
+        out_shape=[jax.ShapeDtypeStruct(*shape) for shape in shapes],
+        in_specs=[vmem, vmem, smem] + [vmem] * 8 + [anywhere] * 2,
+        out_specs=[vmem] * 7 + [anywhere] * 2 + [vmem],
+        scratch_shapes=[pltpu.VMEM(*shape) for shape in scratch.values()]
+        + [pltpu.SemaphoreType.DMA((KEYS,))] * 2
+        + [pltpu.SemaphoreType.DMA((4,))],
+        compiler_params=pltpu.CompilerParams(
+            collective_id=0, has_side_effects=True, vmem_limit_bytes=63 << 20
+        ),
+    )(
+        hidden_in,
+        cotangent,
+        bucket_len[:, 0, :],
+        live_mask,
+        routes[:, :, 0],
+        vin,
+        ein,
+        w_qkv,
+        w_attn_out,
+        w_up,
+        w_down,
+        expert_in.reshape(S, G // 2, 2, sh, FQ),
+        expert_out.reshape(G // 2, 2, shd, D),
+    )
+    out, dx, vectors, gqkv, gwo, gup, gdn, gin, gout, evectors = outs
+    vectors = lax.dynamic_slice_in_dim(vectors, lax.axis_index("dp") * sh, sh, 1)
+    return (
+        out,
+        dx,
+        vectors[0],
+        vectors[1],
+        gqkv,
+        gwo,
+        vectors[2],
+        vectors[3],
+        gup,
+        gdn,
+        gin[None],
+        gout[None],
+        evectors[0:1],
+        evectors[1:2],
+        evectors[2:3],
+    )
+
+
+def on_device(*args):
+    groups = lax.axis_size("dp")
+    rows, shard = args[0].shape[1], args[11].shape[0]
+    capacity = 3 * rows // (2 * groups)
+    if capacity % 16 or shard % 16:
+        return with_collectives(*args)
+    return with_kernel(*args)
 
 
 def solution(mesh):

time: 758 us -> 320 us (0.42); the launches traced: 748 us -> 319 us
  waiting for transfers between devices: 395 us -> 0 us
  Pallas kernels: 0 us -> 296 us
  blocking collectives: 154 us -> 0 us
  matrix products: 81.7 us -> 0 us
  other arithmetic: 37.1 us -> 2.62 us
  local copies, waits for them, and re-layouts: 48.1 us -> 20.3 us
  starting transfers between devices: 17.4 us -> 0 us
  between operations: 15 us -> 0.67 us
    pallas_call x0 -> x1, Pallas kernels: none -> 296 us  [with_kernel(): pl.pallas_call(functools.partial(block_kernel, dims, names), name='block'...]
    reduce_scatter x10 -> x0, waiting for transfers between devices: 208 us -> none  [the longest x6 106 us: sum_scatter(): lax.psum_scatter(part.astype(bf16), 'section', scatter_dimension=part.ndi...]
    all_gather x8 -> x0, waiting for transfers between devices: 137 us -> none  [the longest x5 85 us: gather_features(): return lax.all_gather(part, 'section', axis=part.ndim - 1, tiled=True)]
    dot_general x27 -> x0, matrix products: 78.5 us -> none  [the longest x6 23.5 us: dot(): return jnp.dot(a, b, preferred_element_type=f32)]
    all_gather x3 -> x0, blocking collectives: 64.2 us -> none  [the longest x1 40.4 us: on_device(): lax.all_gather(jnp.stack([ln1_gain, ln1_bias, ln2_gain, ln2_bias]), ('sec...]
    all_to_all x4 -> x0, blocking collectives: 56.1 us -> none  [the longest x2 33.9 us: dispatch(): return lax.all_to_all(out, 'dp', split_axis=0, concat_axis=0, tiled=True)]
    psum x3 -> x0, blocking collectives: 33.6 us -> none  [the longest x1 15.7 us: on_device(): lax.psum(jnp.stack([jnp.mean(gden, axis=-1), jnp.mean(gden * ne, axis=-1)...]
    unnamed x20 -> x0, waiting for transfers between devices: 29.1 us -> none
  transfers between devices with their start and end apart: 23 -> 0, of which waited for: 19 -> 0; matrix products, arithmetic and copies ran while one was open for 13% -> 0% of each run, Pallas kernels for 0% -> 0%
where the time goes in v2:
time: 320 us; the launch traced here: 319 us
  Pallas kernels  296 us (92%)
  local copies, waits for them, and re-layouts  20.3 us (6%)
    pallas_call x1, Pallas kernels, with_kernel(): pl.pallas_call(functools.partial(block_kernel, dims, names), name='block'...  296 us
    unnamed x13, local copies, waits for them, and re-layouts  17.6 us

profile of v2, /device:TPU:0, one launch (start us, length us, event | category | flops | bytes accessed | tf_op | source)
XLA Modules:
  0.0 319.3 jit_solution(75401218396035345)
XLA Ops:
  0.6 1.3 copy.35
  1.9 1.3 fusion.15.args_5_
  3.2 1.3 fusion.5.args_6_
  4.5 295.6 %block.1 = (bf16[2,256,256]{2,1,0:T(8,128)(2,1)}, f32[2,256,256]{2,1,0:T(8,128)}, f32[8,256]{1,0:T(8,128)}, f32[32,3072]{1,0:T(8,128)}, f32[32,1024]{1,0:T(8,128...) custom-call(bf16[2,256,1024]{2,1,0:T(8,128)(2,1)} %args_0_.4, ...), custom_call_target="tpu_custom_call" | custom-call | tf_op jit(solution)/shard_map/block/pallas_call | solution.py:1166
  300.2 0.0 copy-start.1
  300.2 1.5 fusion.19
  301.6 0.7 constant_dynamic-slice_fusion
  302.4 0.5 slice_bitcast_fusion
  302.9 1.7 copy.44
  304.6 1.9 copy.45
  306.4 1.8 copy.46
  308.2 1.6 copy.47
  309.8 1.9 copy.48
  311.7 1.9 copy.49
  313.5 0.0 copy-done.1
  313.5 0.0 copy-start
  313.5 2.1 copy.50
  315.7 1.6 copy-done
  317.2 2.0 copy.51
Async XLA Ops:
  300.2 13.4 %copy-start.1 = (f32[1024,1024]{1,0:T(8,128)S(1)}, f32[1024,1024]{1,0:T(8,128)}, u32[]{:S(2)}) copy-start(f32[1024,1024]{1,0:T(8,128)} %get-tuple-element.32) | copy-start | bytes 12582916
  313.5 3.7 %copy-start = (f32[1024,1024]{1,0:T(8,128)S(1)}, f32[1024,1024]{1,0:T(8,128)}, u32[]{:S(2)}) copy-start(f32[1024,1024]{1,0:T(8,128)} %get-tuple-element.33) | copy-start | bytes 12582916

commit v3 on v2

--- a/solution.py
+++ b/solution.py
@@ -297,14 +297,10 @@
     return t, root
 
 
-def gelu_of(v):
-    t, _ = tanh_parts(v)
-    return v * (0.5 * (1.0 + t))
-
-
-def gelu_slope(v):
+def gelu_both(v):
     t, root = tanh_parts(v)
-    return 0.5 * (1.0 + t) + 0.5 * v * (1.0 - t * t) * root * (1.0 + 0.134145 * (v * v))
+    half = 0.5 * (1.0 + t)
+    return v * half, half + 0.5 * v * (1.0 - t * t) * root * (1.0 + 0.134145 * (v * v))
 
 
 def to_rows(columns):
@@ -358,7 +354,7 @@
         ue=((M, R, FQ), bf16),
         dhe=((M, R, FQ), bf16),
         dfe=((M, R, D), bf16),
-        he=((R, FQ), f32),
+        slope=((R, FQ), f32),
         fes=((M, S - 1, R, Q), bf16),
         fer=((M, S - 1, R, Q), bf16),
         feo=((M, R, Q), f32),
@@ -438,6 +434,9 @@
     z = lax.div(d, 2)
     c = lax.rem(d, 2)
     beside = (s, d + 1 - 2 * c)
+    near = z + 1 - 2 * lax.rem(z, 2)
+    far = lax.rem(z + 2, nz)
+    near_far = lax.rem(near + 2, nz)
 
     def sec(i):
         return lax.rem(s + i, S)
@@ -548,17 +547,24 @@
         return ref.at[:, zz, cc] if len(ref.shape) == 5 else ref.at[zz, cc]
 
     def weight_start(ref, k):
-        for j in range(1, nz):
-            send(part(ref, z, c), part(ref, z, c), (k, "z", j), to_z(j))
+        send(part(ref, z, c), part(ref, z, c), (k, "far"), (s, far * 2 + c))
+        send(part(ref, z, c), part(ref, z, c), (k, "near"), (s, near * 2 + c))
         send(part(ref, z, c), part(ref, z, c), (k, "c", 0), beside)
 
+    def weight_far(ref, k):
+        recv(part(ref, far, c), (k, "far"))
+        send(part(ref, far, c), part(ref, far, c), (k, "near far"), (s, near * 2 + c))
+        send(part(ref, far, c), part(ref, far, c), (k, "c", 1), beside)
+
+    def weight_near(ref, k):
+        recv(part(ref, near, c), (k, "near"))
+        send(part(ref, near, c), part(ref, near, c), (k, "c", 2), beside)
+        recv(part(ref, near_far, c), (k, "near far"))
+        send(part(ref, near_far, c), part(ref, near_far, c), (k, "c", 3), beside)
+
     def weight_wait(ref, k):
-        for j in range(1, nz):
-            zz = zi(nz - j)
-            recv(part(ref, zz, c), (k, "z", j))
-            send(part(ref, zz, c), part(ref, zz, c), (k, "c", j), beside)
-        for j in range(nz):
-            recv(part(ref, zi(nz - j) if j else z, 1 - c), (k, "c", j))
+        for i, zz in enumerate((z, far, near, near_far)):
+            recv(part(ref, zz, 1 - c), (k, "c", i))
 
     barrier = pltpu.get_barrier_semaphore()
     for i in others:
@@ -604,18 +610,17 @@
         r.perm[m] = jnp.where(seat_ids == place, 1.0, 0.0).astype(bf16)
         r.cots[m] = jnp.dot(r.perm[m], r.cot[m, :, mine], preferred_element_type=f32).astype(bf16)
 
-    for i in others:
-        for piece in range(3):
-            recv(r.wqkv.at[sec(S - i), z, c, :, piece * Q : (piece + 1) * Q], ("q1", piece, i))
-    weight_start(r.wqkv, "wqkv")
+        dispatch_send(r.cots, r.dge, m, "cot")
+
     for i in others:
         recv(r.vg.at[sec(S - i), d], ("v1", i))
         recv(r.evec.at[:, col(sec(S - i))], ("e1", i))
     for j in range(1, G):
         send(r.vg.at[:, d], r.vg.at[:, d], ("v2", j), to_dp(j))
-    for m in range(M):
-        dispatch_send(r.cots, r.dge, m, "cot")
-    weight_start(r.wo, "wo")
+    for i in others:
+        for piece in range(3):
+            recv(r.wqkv.at[sec(S - i), z, c, :, piece * Q : (piece + 1) * Q], ("q1", piece, i))
+    weight_start(r.wqkv, "wqkv")
 
     for m in range(M):
         end = r.bucket[m, 0]
@@ -663,11 +668,17 @@
 
     for m in range(M):
         norm_tokens(r.hidden, m, 0, True)
+    weight_far(r.wqkv, "wqkv")
+    weight_start(r.wo, "wo")
+    for m in range(M):
+        dispatch_recv(r.dge, m, "cot")
+        gather_send(r.dge, m, "dge")
     for i in others:
         recv(r.wup.at[sec(S - i), z, c], ("u1", i))
     weight_start(r.wup, "wup")
+    weight_near(r.wqkv, "wqkv")
+    weight_far(r.wo, "wo")
     weight_wait(r.wqkv, "wqkv")
-    weight_start(r.wdn, "wdn")
 
     def attend(m):
         @pl.loop(0, 3)
@@ -693,11 +704,14 @@
         )
 
     attend(0)
+    weight_near(r.wo, "wo")
+    weight_far(r.wup, "wup")
+    weight_start(r.wdn, "wdn")
     weight_wait(r.wo, "wo")
     sum_send(y1_tile(0), r.ts, r.r1, r.own, 0, "y1")
     attend(1)
     sum_send(y1_tile(1), r.ts, r.r1, r.own, 1, "y1")
-    weight_wait(r.wup, "wup")
+    weight_near(r.wup, "wup")
 
     def finish_y1(m):
         sum_recv(r.r1, m, "y1")
@@ -711,9 +725,8 @@
 
     finish_y1(0)
     finish_y1(1)
-    for m in range(M):
-        dispatch_recv(r.dge, m, "cot")
-        gather_send(r.dge, m, "dge")
+    weight_wait(r.wup, "wup")
+    weight_far(r.wdn, "wdn")
 
     def up(m):
         gather_recv(r.y1, m, "y1g")
@@ -723,8 +736,9 @@
         def _(t):
             w = r.wup[:, :, :, :, col(t)].reshape(D, Q)
             pre = jnp.dot(r.a[m], w, preferred_element_type=f32)
-            r.h[m, :, col(t)] = pre
-            r.u[m, :, col(t)] = gelu_of(pre).astype(bf16)
+            value, slope = gelu_both(pre)
+            r.u[m, :, col(t)] = value.astype(bf16)
+            r.h[m, :, col(t)] = slope
 
     def y2_tile(m):
         return lambda q: jnp.dot(
@@ -732,9 +746,10 @@
         )
 
     up(0)
+    up(1)
+    weight_near(r.wdn, "wdn")
     weight_wait(r.wdn, "wdn")
     sum_send(y2_tile(0), r.ts, r.r2, r.own, 0, "y2", "y1")
-    up(1)
     sum_send(y2_tile(1), r.ts, r.r2, r.own, 1, "y2", "y1")
 
     def finish_y2(m):
@@ -777,9 +792,9 @@
         def _(t):
             w = r.win[:, :, :, :, col(t)].reshape(D, Q)
             pre = jnp.dot(r.en[m], w, preferred_element_type=f32)
-            r.ue[m, :, col(t)] = gelu_of(pre).astype(bf16)
-            due = nt(r.dfe[m], r.wout[t].reshape(Q, D))
-            r.dhe[m, :, col(t)] = (due * gelu_slope(pre)).astype(bf16)
+            value, slope = gelu_both(pre)
+            r.ue[m, :, col(t)] = value.astype(bf16)
+            r.slope[:, col(t)] = slope
 
         stats = [jnp.zeros((R, 1), f32) for _ in range(3)]
 
@@ -798,7 +813,13 @@
             stats[1] += jnp.sum(scaled * n, axis=1, keepdims=True)
             return tile
 
-        sum_send(fe_tile, r.fes, r.fer, r.feo, m, "fe", hold=True)
+        sum_send(fe_tile, r.fes, r.fer, r.feo, m, "fe", hold=m > 0)
+
+        @pl.loop(0, FQ // Q)
+        def _(t):
+            due = nt(r.dfe[m], r.wout[t].reshape(Q, D))
+            r.dhe[m, :, col(t)] = (due * r.slope[:, col(t)]).astype(bf16)
+
         sum_send(den_tile, r.dns, r.dnr, r.dno, m, "den")
         r.ess[m] = to_rows(stats)
         for i in others:
@@ -834,10 +855,20 @@
         each(R, 64 if R % 64 == 0 else CHUNK, body)
         return_send(r.dxs, r.dxr, m, "dxb")
 
+    def finish_fe(m):
+        sum_recv(r.fer, m, "fe")
+
+        def body(rows):
+            fe = summed(r.feo, r.fer, m, rows)
+            r.ges[m, rows] = (r.est[m, rows, 2:3] * fe).astype(bf16)
+
+        each(R, 64 if R % 64 == 0 else CHUNK, body)
+        return_send(r.ges, r.ger, m, "geb")
+
     finish_den(0)
     finish_den(1)
-    for m in range(M):
-        sum_start(r.fes, r.fer, m, "fe")
+    sum_start(r.fes, r.fer, 1, "fe")
+    finish_fe(0)
 
     writes = []
     for left, right, out in ((r.en, r.dhe, r.gin_out), (r.ue, r.dfe, r.gout_out)):
@@ -859,6 +890,7 @@
 
     finish_dxe(0)
     finish_dxe(1)
+    finish_fe(1)
 
     def token_stats(m, at, src):
         stats = [jnp.zeros((T, 1), f32) for _ in range(2)]
@@ -891,7 +923,7 @@
         @pl.loop(0, FQ // Q)
         def _(t):
             du = nt(r.dy2[m], r.wdn[t].reshape(Q, D))
-            r.dh[m, :, col(t)] = (du * gelu_slope(r.h[m, :, col(t)])).astype(bf16)
+            r.dh[m, :, col(t)] = (du * r.h[m, :, col(t)]).astype(bf16)
 
         stats, add = token_stats(m, 1, r.y1)
         sum_send(
@@ -935,26 +967,44 @@
         src = g.at[:, :, 1 - c] if len(g.shape) == 5 else g.at[:, 1 - c]
         send(src, b, (k, "p"), beside)
 
+    def grads_add(g, zz, arrive):
+        if len(g.shape) == 5:
+
+            @pl.loop(0, S)
+            def _(q):
+                g[q, zz, c] = (g[q, zz, c].astype(f32) + arrive[q].astype(f32)).astype(bf16)
+        else:
+            g[zz, c] = (g[zz, c].astype(f32) + arrive[...].astype(f32)).astype(bf16)
+
+    def grads_paired(g, b, k):
+        recv(b, (k, "p"))
+        for zz in range(nz):
+            grads_add(g, zz, b.at[:, zz] if len(g.shape) == 5 else b.at[zz])
+
+    def grads_near(g, b, arrive, k):
+        grads_paired(g, b, k)
+        send(part(g, near_far, c), arrive.at[1], (k, "nf"), (s, near * 2 + c))
+        send(part(g, near, c), arrive.at[0], (k, "n"), (s, near * 2 + c))
+
+    def grads_far(g, arrive, k):
+        recv(arrive.at[1], (k, "nf"))
+        grads_add(g, far, arrive.at[1])
+        send(part(g, far, c), arrive.at[2], (k, "f"), (s, far * 2 + c))
+
+    def grads_near_recv(arrive, k):
+        recv(arrive.at[0], (k, "n"))
+        recv(arrive.at[2], (k, "f"))
+        return 0, 2
+
     def grads_spread(g, b, arrive, k):
-        recv(b, (k, "p"))
-        if len(g.shape) == 5:
-
-            @pl.loop(0, nz)
-            def _(zz):
-                for q in range(S):
-                    g[q, zz, c] = (g[q, zz, c].astype(f32) + b[q, zz].astype(f32)).astype(bf16)
-        else:
-
-            @pl.loop(0, nz)
-            def _(zz):
-                g[zz, c] = (g[zz, c].astype(f32) + b[zz].astype(f32)).astype(bf16)
-
+        grads_paired(g, b, k)
         for j in range(1, nz):
             send(part(g, zi(j), c), arrive.at[j - 1], (k, "g", j), to_z(j))
 
     def grads_recv(arrive, k):
         for j in range(1, nz):
             recv(arrive.at[j - 1], (k, "g", j))
+        return range(nz - 1)
 
     dense_back(0)
     dense_back(1)
@@ -978,21 +1028,10 @@
         r.win[t] = grad.astype(bf16).reshape(nz, 2, sh, FQ)
 
     grads_pair(r.win, r.bup, "gup")
-    grads_spread(r.wout, r.bdn, r.zdn, "gdn")
-
-    def finish_fe(m):
-        sum_recv(r.fer, m, "fe")
-
-        def body(rows):
-            fe = summed(r.feo, r.fer, m, rows)
-            r.ges[m, rows] = (r.est[m, rows, 2:3] * fe).astype(bf16)
-
-        each(R, 64 if R % 64 == 0 else CHUNK, body)
-        return_send(r.ges, r.ger, m, "geb")
+    grads_near(r.wout, r.bdn, r.zdn, "gdn")
 
     for m in range(M):
         norm_tokens(r.hidden, m, 0, False)
-        finish_fe(m)
 
     def attend_back(m):
         gather_recv(r.y1, m, "dy1")
@@ -1025,7 +1064,9 @@
         stats_send(m, 0, stats)
 
     attend_back(0)
+    grads_near(r.win, r.bup, r.zup, "gup")
     attend_back(1)
+    grads_far(r.wout, r.zdn, "gdn")
 
     @pl.loop(0, S)
     def _(t):
@@ -1037,7 +1078,7 @@
     grad = tn(r.o[...].reshape(M * T, Q), r.y1[...].reshape(M * T, D))
     r.gwo[...] = grad.astype(bf16).reshape(nz, 2, sh, D)
     grads_pair(r.gwo, r.bwo, "gwo")
-    grads_spread(r.win, r.bup, r.zup, "gup")
+    grads_far(r.win, r.zup, "gup")
     grads_spread(r.gqk, r.bqk, r.zqk, "gqk")
     grads_spread(r.gwo, r.bwo, r.zwo, "gwo")
 
@@ -1060,26 +1101,26 @@
         back = tn(r.perm[m], r.ger[m])
         r.out[m] = (r.y2q[m].astype(f32) + back).astype(bf16)
 
-    def row_result(g, arrive, out, k, rows):
-        grads_recv(arrive, k)
+    def row_result(g, arrive, out, k, rows, wait):
+        slots = wait(arrive, k)
         mine_part = part(g, z, c)
 
         def body(at):
             total = mine_part[at].astype(f32)
-            for j in range(1, nz):
-                total += arrive[j - 1, at].astype(f32)
+            for slot in slots:
+                total += arrive[slot, at].astype(f32)
             out[at] = total
 
         each(rows, CHUNK, body)
 
-    def column_send(g, arrive, out, back, k):
-        grads_recv(arrive, k)
+    def column_send(g, arrive, out, back, k, wait):
+        slots = wait(arrive, k)
 
         @pl.loop(0, S)
         def _(q):
             total = g[q, z, c].astype(f32)
-            for j in range(1, nz):
-                total += arrive[j - 1, q].astype(f32)
+            for slot in slots:
+                total += arrive[slot, q].astype(f32)
             out[q] = total.astype(bf16)
 
         for i in others:
@@ -1096,10 +1137,10 @@
                 at = pl.ds(pl.multiple_of(piece * S * width + q * width, width), width)
                 out[:, at] = value[:, piece * width : (piece + 1) * width]
 
-    row_result(r.wout, r.zdn, r.gdn_out, "gdn", shd)
-    column_send(r.win, r.zup, r.ups, r.upr, "gup")
-    column_send(r.gqk, r.zqk, r.qks, r.qkr, "gqk")
-    row_result(r.gwo, r.zwo, r.gwo_out, "gwo", sh)
+    row_result(r.wout, r.zdn, r.gdn_out, "gdn", shd, grads_near_recv)
+    column_send(r.win, r.zup, r.ups, r.upr, "gup", grads_near_recv)
+    column_send(r.gqk, r.zqk, r.qks, r.qkr, "gqk", grads_recv)
+    row_result(r.gwo, r.zwo, r.gwo_out, "gwo", sh, grads_recv)
     total = r.vsum[...]
     for j in range(1, G):
         recv(r.vsr.at[j - 1], ("vs", j))
@@ -1112,6 +1153,19 @@
     for k in list(pending):
         sent(k)
     assert len(places) <= KEYS, len(places)
+
+
+def hand_over(*refs):
+    count = len(refs) // 2
+    first = pl.program_id(0) == 0
+    for src, dst in zip(refs[:count], refs[count:]):
+        if src.shape[0] == 256 and src.shape[1] == 1024:
+            dst[...] = src[...]
+        else:
+
+            @pl.when(first)
+            def _(src=src, dst=dst):
+                dst[...] = src[...]
 
 
 def with_kernel(
@@ -1190,6 +1244,21 @@
         expert_in.reshape(S, G // 2, 2, sh, FQ),
         expert_out.reshape(G // 2, 2, shd, D),
     )
+    specs = [
+        pl.BlockSpec((256, shape[1]), lambda i: (i, 0))
+        if shape == (D, FQ) or shape == (FQ, D)
+        else pl.BlockSpec(shape, lambda i, n=len(shape): (0,) * n)
+        for shape, _ in shapes
+    ]
+    outs = pl.pallas_call(
+        hand_over,
+        name="hand_over",
+        grid=(D // 256,),
+        out_shape=[jax.ShapeDtypeStruct(*shape) for shape in shapes],
+        in_specs=specs,
+        out_specs=specs,
+        compiler_params=pltpu.CompilerParams(vmem_limit_bytes=32 << 20),
+    )(*outs)
     out, dx, vectors, gqkv, gwo, gup, gdn, gin, gout, evectors = outs
     vectors = lax.dynamic_slice_in_dim(vectors, lax.axis_index("dp") * sh, sh, 1)
     return (
@@ -1215,7 +1284,7 @@
     groups = lax.axis_size("dp")
     rows, shard = args[0].shape[1], args[11].shape[0]
     capacity = 3 * rows // (2 * groups)
-    if capacity % 16 or shard % 16:
+    if capacity % 16 or shard % 16 or groups != 8:
         return with_collectives(*args)
     return with_kernel(*args)
 

time: 320 us -> 269 us (0.84)
  Pallas kernels: 296 us -> 251 us
  local copies, waits for them, and re-layouts: 20.3 us -> 14.2 us
    pallas_call x1, Pallas kernels: 296 us -> 246 us  [with_kernel(): pl.pallas_call(functools.partial(block_kernel, dims, names), name='block'...]
    unnamed x13 -> x21, local copies, waits for them, and re-layouts: 17.6 us -> 13 us
    pallas_call x0 -> x1, Pallas kernels: none -> 4.43 us  [with_kernel(): pl.pallas_call(hand_over, name='hand_over', grid=(D // 256,), out_shape=[...]
where the time goes in v3:
time: 269 us; the launch traced here: 268 us
  Pallas kernels  251 us (93%)
  local copies, waits for them, and re-layouts  14.2 us (5%)
    pallas_call x1, Pallas kernels, with_kernel(): pl.pallas_call(functools.partial(block_kernel, dims, names), name='block'...  246 us
    unnamed x21, local copies, waits for them, and re-layouts  13 us

profile of v3, /device:TPU:0, one launch (start us, length us, event | category | flops | bytes accessed | tf_op | source)
XLA Modules:
  0.0 268.2 jit_solution(10644773265320345727)
XLA Ops:
  0.6 1.3 fusion.5.args_6_
  2.0 1.3 fusion.15.args_5_
  3.3 1.3 copy.35
  4.5 246.3 %block.1 = (bf16[2,256,256]{2,1,0:T(8,128)(2,1)}, f32[2,256,256]{2,1,0:T(8,128)}, f32[8,256]{1,0:T(8,128)}, f32[32,3072]{1,0:T(8,128)}, f32[32,1024]{1,0:T(8,128...) custom-call(bf16[2,256,1024]{2,1,0:T(8,128)(2,1)} %args_0_.4, ...), custom_call_target="tpu_custom_call" | custom-call | tf_op jit(solution)/shard_map/block/pallas_call | solution.py:1220
  250.8 0.0 copy-start
  250.8 2.2 copy-done
  253.0 0.0 copy-start.1
  253.0 2.2 copy-done.1
  255.2 0.0 copy-start.2
  255.2 1.0 copy-done.2
  256.3 0.0 copy-start.3
  256.3 1.0 copy-done.3
  257.3 0.0 copy-start.4
  257.3 1.0 copy-done.4
  258.3 0.0 copy-start.5
  258.3 1.0 copy-done.5
  259.3 0.9 copy-done.6
  260.3 0.9 copy-done.7
  261.2 0.7 copy-done.8
  261.9 0.7 copy-done.9
  262.6 4.4 %hand_over.1 = (bf16[2,256,256]{2,1,0:T(8,128)(2,1)}, f32[2,256,256]{2,1,0:T(8,128)}, f32[8,256]{1,0:T(8,128)S(1)}, f32[32,3072]{1,0:T(8,128)}, f32[32,1024]{1,0...) custom-call(bf16[2,256,256]{2,1,0:T(8,128)(2,1)S(1)} %copy-done.6, ...), custom_call_target="tpu_custom_call" | custom-call | tf_op jit(solution)/shard_map/hand_over/pallas_call | solution.py:1253
  267.0 0.1 constant_dynamic-slice_fusion
  267.1 0.5 slice_bitcast_fusion
  267.6 0.6 fusion.19
  (4 shorter events, 0.0 us)
Async XLA Ops:
  250.8 2.2 copy-start
  253.0 2.2 copy-start.1
  255.2 1.0 copy-start.2
  256.3 1.0 copy-start.3
  257.3 1.0 copy-start.4
  258.3 1.0 copy-start.5
  259.3 0.9 copy-start.6
  260.3 0.9 copy-start.7
  261.2 0.7 copy-start.8
  261.9 0.7 copy-start.9

commit v4 on v3

--- a/solution.py
+++ b/solution.py
@@ -1,4 +1,5 @@
 import functools
+import math
 import types
 
 import jax
@@ -280,7 +281,7 @@
 
 MESH = pl.DeviceIdType.MESH
 KEYS = 320
-CHUNK = 32
+CHUNK = 128
 
 
 def tn(a, b):
@@ -340,7 +341,8 @@
         dxr=((M, R, Q), bf16),
         tst=((M, T, 128), f32),
         est=((M, R, 128), f32),
-        a=((M, T, D), bf16),
+        a1=((M, T, D), bf16),
+        a2=((M, T, D), bf16),
         qkv=((M, T, 3 * Q), bf16),
         probs=((M, heads, T, T), f32),
         o=((M, T, Q), bf16),
@@ -487,7 +489,9 @@
     def recv(dst, k):
         copy(dst, dst, k, beside).wait_recv()
 
-    def each(rows, step, body):
+    def each(rows, body):
+        step = math.gcd(rows, CHUNK)
+
         @pl.loop(0, rows // step)
         def _(i):
             body(pl.ds(pl.multiple_of(i * step, step), step))
@@ -548,8 +552,10 @@
 
     def weight_start(ref, k):
         send(part(ref, z, c), part(ref, z, c), (k, "far"), (s, far * 2 + c))
+        send(part(ref, z, c), part(ref, z, c), (k, "c", 0), beside)
+
+    def weight_next(ref, k):
         send(part(ref, z, c), part(ref, z, c), (k, "near"), (s, near * 2 + c))
-        send(part(ref, z, c), part(ref, z, c), (k, "c", 0), beside)
 
     def weight_far(ref, k):
         recv(part(ref, far, c), (k, "far"))
@@ -566,39 +572,13 @@
         for i, zz in enumerate((z, far, near, near_far)):
             recv(part(ref, zz, 1 - c), (k, "c", i))
 
-    barrier = pltpu.get_barrier_semaphore()
-    for i in others:
-        pl.semaphore_signal(barrier, inc=1, device_id=to_sec(i), device_id_type=MESH)
-    for j in range(1, G):
-        pl.semaphore_signal(barrier, inc=1, device_id=to_dp(j), device_id_type=MESH)
-    pl.semaphore_wait(barrier, S + G - 2)
-
     load_in = pltpu.make_async_copy(r.win_in, r.win, r.lsem.at[0])
     load_out = pltpu.make_async_copy(r.wout_in, r.wout, r.lsem.at[1])
-    for i in others:
-        for piece in range(3):
-            src = r.wqkv_in.at[:, pl.ds(pl.multiple_of(piece * D + sec(i) * Q, Q), Q)]
-            dst = r.wqkv.at[s, z, c, :, piece * Q : (piece + 1) * Q]
-            send(src, dst, ("q1", piece, i), to_sec(i))
-        send(r.vin, r.vg.at[s, d], ("v1", i), to_sec(i))
-        send(r.ein, r.evec.at[:, mine], ("e1", i), to_sec(i))
-    for i in others:
-        send(r.wup_in.at[:, col(sec(i), FQ)], r.wup.at[s, z, c], ("u1", i), to_sec(i))
-    load_in.start()
-    load_out.start()
-    for piece in range(3):
-        r.wqkv[s, z, c, :, piece * Q : (piece + 1) * Q] = r.wqkv_in[
-            :, pl.ds(pl.multiple_of(piece * D + s * Q, Q), Q)
-        ]
-    r.wup[s, z, c] = r.wup_in[:, col(s, FQ)]
-    r.wo[z, c] = r.wo_in[...]
-    r.wdn[z, c] = r.wdn_in[...]
-    r.vg[s, d] = r.vin[...]
-    r.evec[:, mine] = r.ein[...]
 
     early = lax.broadcasted_iota(jnp.int32, (T, T), 0)
     late = lax.broadcasted_iota(jnp.int32, (T, T), 1)
-    for m in range(M):
+
+    def seat_tokens(m):
         route = r.routes[m : m + 1, :]
         expert_ids = lax.broadcasted_iota(jnp.int32, (G, T), 0)
         picks = jnp.where(expert_ids == route, 1.0, 0.0)
@@ -610,19 +590,47 @@
         r.perm[m] = jnp.where(seat_ids == place, 1.0, 0.0).astype(bf16)
         r.cots[m] = jnp.dot(r.perm[m], r.cot[m, :, mine], preferred_element_type=f32).astype(bf16)
 
-        dispatch_send(r.cots, r.dge, m, "cot")
-
-    for i in others:
-        recv(r.vg.at[sec(S - i), d], ("v1", i))
-        recv(r.evec.at[:, col(sec(S - i))], ("e1", i))
-    for j in range(1, G):
-        send(r.vg.at[:, d], r.vg.at[:, d], ("v2", j), to_dp(j))
-    for i in others:
+    def entry():
+        barrier = pltpu.get_barrier_semaphore()
+        for i in others:
+            pl.semaphore_signal(barrier, inc=1, device_id=to_sec(i), device_id_type=MESH)
+        for j in range(1, G):
+            pl.semaphore_signal(barrier, inc=1, device_id=to_dp(j), device_id_type=MESH)
+        r.vg[s, d] = r.vin[...]
+        r.evec[:, mine] = r.ein[...]
         for piece in range(3):
-            recv(r.wqkv.at[sec(S - i), z, c, :, piece * Q : (piece + 1) * Q], ("q1", piece, i))
-    weight_start(r.wqkv, "wqkv")
-
-    for m in range(M):
+            r.wqkv[s, z, c, :, piece * Q : (piece + 1) * Q] = r.wqkv_in[
+                :, pl.ds(pl.multiple_of(piece * D + s * Q, Q), Q)
+            ]
+        r.wo[z, c] = r.wo_in[...]
+        seat_tokens(0)
+        seat_tokens(1)
+        pl.semaphore_wait(barrier, S + G - 2)
+        for i in others:
+            send(r.vin, r.vg.at[s, d], ("v1", i), to_sec(i))
+        for i in others:
+            for piece in range(3):
+                src = r.wqkv_in.at[:, pl.ds(pl.multiple_of(piece * D + sec(i) * Q, Q), Q)]
+                dst = r.wqkv.at[s, z, c, :, piece * Q : (piece + 1) * Q]
+                send(src, dst, ("q1", piece, i), to_sec(i))
+        dispatch_send(r.cots, r.dge, 0, "cot")
+        dispatch_send(r.cots, r.dge, 1, "cot")
+        for i in others:
+            send(r.wup_in.at[:, col(sec(i), FQ)], r.wup.at[s, z, c], ("u1", i), to_sec(i))
+            send(r.ein, r.evec.at[:, mine], ("e1", i), to_sec(i))
+        for i in others:
+            recv(r.vg.at[sec(S - i), d], ("v1", i))
+        for j in range(1, G):
+            send(r.vg.at[:, d], r.vg.at[:, d], ("v2", j), to_dp(j))
+        for i in others:
+            for piece in range(3):
+                recv(r.wqkv.at[sec(S - i), z, c, :, piece * Q : (piece + 1) * Q], ("q1", piece, i))
+        weight_start(r.wqkv, "wqkv")
+        weight_next(r.wqkv, "wqkv")
+        load_in.start()
+        load_out.start()
+
+    def mask_tokens(m):
         end = r.bucket[m, 0]
         seg_q = (early >= end).astype(jnp.int32)
         seg_k = (late >= end).astype(jnp.int32)
@@ -634,18 +642,19 @@
         allowed = (seg_q == seg_k) & (late <= early) & ((live == 1) | (late == early))
         r.mask[m] = jnp.where(allowed, 1.0, 0.0)
 
-    for j in range(1, G):
-        recv(r.vg.at[:, dpi(G - j)], ("v2", j))
-    spread_row = lax.broadcasted_iota(jnp.int32, (128, D), 0)
-    spread_lane = lax.broadcasted_iota(jnp.int32, (128, D), 1)
-    spread = jnp.where(lax.rem(spread_lane, sh) == spread_row, 1.0, 0.0).astype(bf16)
-    stacked = r.vg[...].reshape(S * G * 8, 128).astype(bf16)
-    wide = jnp.dot(stacked, spread, preferred_element_type=f32)
-    row_id = lax.broadcasted_iota(jnp.int32, (S * G * 8, D), 0)
-    lane_id = lax.broadcasted_iota(jnp.int32, (S * G * 8, D), 1)
-    low = lax.shift_right_logical(row_id, 3) * sh
-    wide = jnp.where((lane_id >= low) & (lane_id < low + sh), wide, 0.0)
-    r.vecs[...] = jnp.sum(wide.reshape(S * G, 8, D), axis=0)
+    def spread_vectors():
+        for j in range(1, G):
+            recv(r.vg.at[:, dpi(G - j)], ("v2", j))
+        spread_row = lax.broadcasted_iota(jnp.int32, (128, D), 0)
+        spread_lane = lax.broadcasted_iota(jnp.int32, (128, D), 1)
+        spread = jnp.where(lax.rem(spread_lane, sh) == spread_row, 1.0, 0.0).astype(bf16)
+        stacked = r.vg[...].reshape(S * G * 8, 128).astype(bf16)
+        wide = jnp.dot(stacked, spread, preferred_element_type=f32)
+        row_id = lax.broadcasted_iota(jnp.int32, (S * G * 8, D), 0)
+        lane_id = lax.broadcasted_iota(jnp.int32, (S * G * 8, D), 1)
+        low = lax.shift_right_logical(row_id, 3) * sh
+        wide = jnp.where((lane_id >= low) & (lane_id < low + sh), wide, 0.0)
+        r.vecs[...] = jnp.sum(wide.reshape(S * G, 8, D), axis=0)
 
     def normed(values):
         mean = jnp.mean(values, axis=1, keepdims=True)
@@ -653,38 +662,46 @@
         rs = lax.rsqrt(jnp.mean(center * center, axis=1, keepdims=True) + epsilon)
         return center * rs, mean, rs
 
-    def norm_tokens(src, m, at, keep):
+    def norm_tokens(src, dst, m, at):
         gain = r.vecs[2 * at : 2 * at + 1, :]
         bias = r.vecs[2 * at + 1 : 2 * at + 2, :]
 
         def body(rows):
             n, mean, rs = normed(src[m, rows].astype(f32))
-            if keep:
-                r.tst[m, rows, 2 * at : 2 * at + 1] = mean
-                r.tst[m, rows, 2 * at + 1 : 2 * at + 2] = rs
-            r.a[m, rows] = (n * gain + bias).astype(bf16)
-
-        each(T, CHUNK, body)
-
-    for m in range(M):
-        norm_tokens(r.hidden, m, 0, True)
-    weight_far(r.wqkv, "wqkv")
-    weight_start(r.wo, "wo")
+            r.tst[m, rows, 2 * at : 2 * at + 1] = mean
+            r.tst[m, rows, 2 * at + 1 : 2 * at + 2] = rs
+            dst[m, rows] = (n * gain + bias).astype(bf16)
+
+        each(T, body)
+
+    entry()
+    r.wup[s, z, c] = r.wup_in[:, col(s, FQ)]
+    r.wdn[z, c] = r.wdn_in[...]
+    mask_tokens(0)
+    mask_tokens(1)
     for m in range(M):
         dispatch_recv(r.dge, m, "cot")
         gather_send(r.dge, m, "dge")
+    weight_far(r.wqkv, "wqkv")
+    weight_start(r.wo, "wo")
+    weight_next(r.wo, "wo")
     for i in others:
+        recv(r.evec.at[:, col(sec(S - i))], ("e1", i))
         recv(r.wup.at[sec(S - i), z, c], ("u1", i))
     weight_start(r.wup, "wup")
+    spread_vectors()
+    norm_tokens(r.hidden, r.a1, 0, 0)
+    norm_tokens(r.hidden, r.a1, 1, 0)
     weight_near(r.wqkv, "wqkv")
     weight_far(r.wo, "wo")
+    weight_next(r.wup, "wup")
     weight_wait(r.wqkv, "wqkv")
 
     def attend(m):
         @pl.loop(0, 3)
         def _(t):
             w = r.wqkv[:, :, :, :, col(t)].reshape(D, Q)
-            r.qkv[m, :, col(t)] = jnp.dot(r.a[m], w, preferred_element_type=f32).astype(bf16)
+            r.qkv[m, :, col(t)] = jnp.dot(r.a1[m], w, preferred_element_type=f32).astype(bf16)
 
         for hh in range(heads):
             at = hh * size
@@ -703,39 +720,38 @@
             r.o[m], r.wo[:, :, :, col(q)].reshape(Q, Q), preferred_element_type=f32
         )
 
+    def finish_y1(m):
+        sum_recv(r.r1, m, "y1")
+
+        def body(rows):
+            total = r.hidden[m, rows, mine].astype(f32) + summed(r.own, r.r1, m, rows)
+            r.y1[m, rows, mine] = total.astype(bf16)
+
+        each(T, body)
+        gather_send(r.y1, m, "y1g")
+
     attend(0)
     weight_near(r.wo, "wo")
-    weight_far(r.wup, "wup")
-    weight_start(r.wdn, "wdn")
     weight_wait(r.wo, "wo")
     sum_send(y1_tile(0), r.ts, r.r1, r.own, 0, "y1")
     attend(1)
     sum_send(y1_tile(1), r.ts, r.r1, r.own, 1, "y1")
-    weight_near(r.wup, "wup")
-
-    def finish_y1(m):
-        sum_recv(r.r1, m, "y1")
-
-        def body(rows):
-            total = r.hidden[m, rows, mine].astype(f32) + summed(r.own, r.r1, m, rows)
-            r.y1[m, rows, mine] = total.astype(bf16)
-
-        each(T, 64, body)
-        gather_send(r.y1, m, "y1g")
-
+    weight_far(r.wup, "wup")
+    weight_start(r.wdn, "wdn")
+    weight_next(r.wdn, "wdn")
     finish_y1(0)
     finish_y1(1)
+    weight_near(r.wup, "wup")
     weight_wait(r.wup, "wup")
-    weight_far(r.wdn, "wdn")
 
     def up(m):
         gather_recv(r.y1, m, "y1g")
-        norm_tokens(r.y1, m, 1, True)
+        norm_tokens(r.y1, r.a2, m, 1)
 
         @pl.loop(0, FQ // Q)
         def _(t):
             w = r.wup[:, :, :, :, col(t)].reshape(D, Q)
-            pre = jnp.dot(r.a[m], w, preferred_element_type=f32)
+            pre = jnp.dot(r.a2[m], w, preferred_element_type=f32)
             value, slope = gelu_both(pre)
             r.u[m, :, col(t)] = value.astype(bf16)
             r.h[m, :, col(t)] = slope
@@ -745,6 +761,7 @@
             r.u[m], r.wdn[:, :, :, col(q)].reshape(FQ, Q), preferred_element_type=f32
         )
 
+    weight_far(r.wdn, "wdn")
     up(0)
     up(1)
     weight_near(r.wdn, "wdn")
@@ -759,7 +776,7 @@
             total = r.y1[m, rows, mine].astype(f32) + summed(r.own, r.r2, m, rows)
             r.y2q[m, rows] = total.astype(bf16)
 
-        each(T, 64, body)
+        each(T, body)
         r.y2s[m] = jnp.dot(r.perm[m], r.y2q[m], preferred_element_type=f32).astype(bf16)
         dispatch_send(r.y2s, r.xe, m, "y2d")
 
@@ -786,7 +803,7 @@
             r.en[m, rows] = (n * gain + bias).astype(bf16)
             r.dfe[m, rows] = (alpha * r.dge[m, rows].astype(f32)).astype(bf16)
 
-        each(R, CHUNK, body)
+        each(R, body)
 
         @pl.loop(0, FQ // Q)
         def _(t):
@@ -813,14 +830,13 @@
             stats[1] += jnp.sum(scaled * n, axis=1, keepdims=True)
             return tile
 
-        sum_send(fe_tile, r.fes, r.fer, r.feo, m, "fe", hold=m > 0)
-
         @pl.loop(0, FQ // Q)
         def _(t):
             due = nt(r.dfe[m], r.wout[t].reshape(Q, D))
             r.dhe[m, :, col(t)] = (due * r.slope[:, col(t)]).astype(bf16)
 
         sum_send(den_tile, r.dns, r.dnr, r.dno, m, "den")
+        sum_send(fe_tile, r.fes, r.fer, r.feo, m, "fe", hold=True)
         r.ess[m] = to_rows(stats)
         for i in others:
             send(r.ess.at[m], r.esr.at[m, i - 1], ("est", m, i), to_sec(i))
@@ -852,7 +868,7 @@
             r.evo[1:2, :] += jnp.sum(den, axis=0, keepdims=True)
             r.evo[2:3, :] += jnp.sum(dlogit * xq, axis=0, keepdims=True)
 
-        each(R, 64 if R % 64 == 0 else CHUNK, body)
+        each(R, body)
         return_send(r.dxs, r.dxr, m, "dxb")
 
     def finish_fe(m):
@@ -862,16 +878,15 @@
             fe = summed(r.feo, r.fer, m, rows)
             r.ges[m, rows] = (r.est[m, rows, 2:3] * fe).astype(bf16)
 
-        each(R, 64 if R % 64 == 0 else CHUNK, body)
+        each(R, body)
         return_send(r.ges, r.ger, m, "geb")
 
     finish_den(0)
     finish_den(1)
-    sum_start(r.fes, r.fer, 1, "fe")
-    finish_fe(0)
 
     writes = []
-    for left, right, out in ((r.en, r.dhe, r.gin_out), (r.ue, r.dfe, r.gout_out)):
+
+    def expert_weights(left, right, out):
         for t in range(D // 256):
             slot = len(writes) % 2
             if len(writes) >= 2:
@@ -882,6 +897,8 @@
             writes.append(pltpu.make_async_copy(r.stage.at[slot], out.at[rows], r.lsem.at[2 + slot]))
             writes[-1].start()
 
+    expert_weights(r.en, r.dhe, r.gin_out)
+
     def finish_dxe(m):
         return_recv(r.dxr, m, "dxb")
         back = tn(r.perm[m], r.dxr[m])
@@ -890,7 +907,7 @@
 
     finish_dxe(0)
     finish_dxe(1)
-    finish_fe(1)
+    expert_weights(r.ue, r.dfe, r.gout_out)
 
     def token_stats(m, at, src):
         stats = [jnp.zeros((T, 1), f32) for _ in range(2)]
@@ -918,7 +935,8 @@
         r.tst[m, :, 8:16] = to_columns(total)[:, 0:8]
 
     def dense_back(m):
-        gather_recv(r.dy2, m, "dy2")
+        if m == 0:
+            gather_recv(r.dy2, m, "dy2")
 
         @pl.loop(0, FQ // Q)
         def _(t):
@@ -949,7 +967,7 @@
             r.vsum[2 * at : 2 * at + 1, :] += jnp.sum(grad * n, axis=0, keepdims=True)
             r.vsum[2 * at + 1 : 2 * at + 2, :] += jnp.sum(grad, axis=0, keepdims=True)
 
-        each(T, 64, body)
+        each(T, body)
 
     def finish_da2(m):
         sum_recv(r.r1, m, "da2")
@@ -996,45 +1014,50 @@
         recv(arrive.at[2], (k, "f"))
         return 0, 2
 
-    def grads_spread(g, b, arrive, k):
-        grads_paired(g, b, k)
-        for j in range(1, nz):
-            send(part(g, zi(j), c), arrive.at[j - 1], (k, "g", j), to_z(j))
-
-    def grads_recv(arrive, k):
-        for j in range(1, nz):
-            recv(arrive.at[j - 1], (k, "g", j))
-        return range(nz - 1)
-
+    def down_weights():
+        @pl.loop(0, nz)
+        def _(t):
+            lhs = r.u[:, :, col(t)].reshape(M * T, Q)
+            grad = tn(lhs, r.dy2[...].reshape(M * T, D))
+            r.wout[t] = grad.astype(bf16).reshape(2, shd, D)
+
+        grads_pair(r.wout, r.bdn, "gdn")
+
+    def up_weights():
+        @pl.loop(0, S)
+        def _(t):
+            lhs = r.a2[:, :, col(t)].reshape(M * T, Q)
+            grad = tn(lhs, r.dh[...].reshape(M * T, FQ))
+            r.win[t] = grad.astype(bf16).reshape(nz, 2, sh, FQ)
+
+        grads_pair(r.win, r.bup, "gup")
+
+    def attention_weights():
+        @pl.loop(0, S)
+        def _(t):
+            lhs = r.a1[:, :, col(t)].reshape(M * T, Q)
+            grad = tn(lhs, r.dqkv[...].reshape(M * T, 3 * Q))
+            r.gqk[t] = grad.astype(bf16).reshape(nz, 2, sh, 3 * Q)
+
+        grads_pair(r.gqk, r.bqk, "gqk")
+        grad = tn(r.o[...].reshape(M * T, Q), r.y1[...].reshape(M * T, D))
+        r.gwo[...] = grad.astype(bf16).reshape(nz, 2, sh, D)
+        grads_pair(r.gwo, r.bwo, "gwo")
+
+    r.vsum[...] = jnp.zeros_like(r.vsum)
     dense_back(0)
+    gather_recv(r.dy2, 1, "dy2")
+    down_weights()
     dense_back(1)
-
-    @pl.loop(0, nz)
-    def _(t):
-        lhs = r.u[:, :, col(t)].reshape(M * T, Q)
-        grad = tn(lhs, r.dy2[...].reshape(M * T, D))
-        r.wout[t] = grad.astype(bf16).reshape(2, shd, D)
-
-    grads_pair(r.wout, r.bdn, "gdn")
-
-    r.vsum[...] = jnp.zeros_like(r.vsum)
     finish_da2(0)
+    grads_near(r.wout, r.bdn, r.zdn, "gdn")
+    up_weights()
     finish_da2(1)
-
-    @pl.loop(0, S)
-    def _(t):
-        lhs = r.a[:, :, col(t)].reshape(M * T, Q)
-        grad = tn(lhs, r.dh[...].reshape(M * T, FQ))
-        r.win[t] = grad.astype(bf16).reshape(nz, 2, sh, FQ)
-
-    grads_pair(r.win, r.bup, "gup")
-    grads_near(r.wout, r.bdn, r.zdn, "gdn")
-
-    for m in range(M):
-        norm_tokens(r.hidden, m, 0, False)
+    grads_near(r.win, r.bup, r.zup, "gup")
 
     def attend_back(m):
         gather_recv(r.y1, m, "dy1")
+        sum_start(r.fes, r.fer, m, "fe")
         out_grad = nt(r.y1[m], r.wo[...].reshape(Q, D)).astype(bf16)
         for hh in range(heads):
             at = hh * size
@@ -1063,25 +1086,6 @@
         )
         stats_send(m, 0, stats)
 
-    attend_back(0)
-    grads_near(r.win, r.bup, r.zup, "gup")
-    attend_back(1)
-    grads_far(r.wout, r.zdn, "gdn")
-
-    @pl.loop(0, S)
-    def _(t):
-        lhs = r.a[:, :, col(t)].reshape(M * T, Q)
-        grad = tn(lhs, r.dqkv[...].reshape(M * T, 3 * Q))
-        r.gqk[t] = grad.astype(bf16).reshape(nz, 2, sh, 3 * Q)
-
-    grads_pair(r.gqk, r.bqk, "gqk")
-    grad = tn(r.o[...].reshape(M * T, Q), r.y1[...].reshape(M * T, D))
-    r.gwo[...] = grad.astype(bf16).reshape(nz, 2, sh, D)
-    grads_pair(r.gwo, r.bwo, "gwo")
-    grads_far(r.win, r.zup, "gup")
-    grads_spread(r.gqk, r.bqk, r.zqk, "gqk")
-    grads_spread(r.gwo, r.bwo, r.zwo, "gwo")
-
     def finish_da1(m):
         sum_recv(r.r2, m, "da1")
         stats_recv(m, 0)
@@ -1091,15 +1095,29 @@
 
         norm_back(m, 0, r.hidden, r.y1, r.own, r.r2, emit)
 
+    attend_back(0)
+    grads_far(r.wout, r.zdn, "gdn")
+    attend_back(1)
+    grads_far(r.win, r.zup, "gup")
+    attention_weights()
     finish_da1(0)
+    grads_near(r.gqk, r.bqk, r.zqk, "gqk")
+    grads_near(r.gwo, r.bwo, r.zwo, "gwo")
+    finish_fe(0)
     finish_da1(1)
     for j in range(1, G):
         send(r.vsum, r.vsr.at[j - 1], ("vs", j), to_dp(j))
-
-    for m in range(M):
+    finish_fe(1)
+    grads_far(r.gqk, r.zqk, "gqk")
+    grads_far(r.gwo, r.zwo, "gwo")
+
+    def finish_out(m):
         return_recv(r.ger, m, "geb")
         back = tn(r.perm[m], r.ger[m])
         r.out[m] = (r.y2q[m].astype(f32) + back).astype(bf16)
+
+    finish_out(0)
+    finish_out(1)
 
     def row_result(g, arrive, out, k, rows, wait):
         slots = wait(arrive, k)
@@ -1111,7 +1129,7 @@
                 total += arrive[slot, at].astype(f32)
             out[at] = total
 
-        each(rows, CHUNK, body)
+        each(rows, body)
 
     def column_send(g, arrive, out, back, k, wait):
         slots = wait(arrive, k)
@@ -1139,8 +1157,8 @@
 
     row_result(r.wout, r.zdn, r.gdn_out, "gdn", shd, grads_near_recv)
     column_send(r.win, r.zup, r.ups, r.upr, "gup", grads_near_recv)
-    column_send(r.gqk, r.zqk, r.qks, r.qkr, "gqk", grads_recv)
-    row_result(r.gwo, r.zwo, r.gwo_out, "gwo", sh, grads_recv)
+    column_send(r.gqk, r.zqk, r.qks, r.qkr, "gqk", grads_near_recv)
+    row_result(r.gwo, r.zwo, r.gwo_out, "gwo", sh, grads_near_recv)
     total = r.vsum[...]
     for j in range(1, G):
         recv(r.vsr.at[j - 1], ("vs", j))
@@ -1257,7 +1275,7 @@
         out_shape=[jax.ShapeDtypeStruct(*shape) for shape in shapes],
         in_specs=specs,
         out_specs=specs,
-        compiler_params=pltpu.CompilerParams(vmem_limit_bytes=32 << 20),
+        compiler_params=pltpu.CompilerParams(vmem_limit_bytes=63 << 20),
     )(*outs)
     out, dx, vectors, gqkv, gwo, gup, gdn, gin, gout, evectors = outs
     vectors = lax.dynamic_slice_in_dim(vectors, lax.axis_index("dp") * sh, sh, 1)

time: 269 us -> 242 us (0.90)
  Pallas kernels: 251 us -> 235 us
  local copies, waits for them, and re-layouts: 14.2 us -> 3.92 us
    pallas_call x1, Pallas kernels: 246 us -> 226 us  [with_kernel(): pl.pallas_call(functools.partial(block_kernel, dims, names), name='block'...]
    unnamed x21 -> x1, local copies, waits for them, and re-layouts: 13 us -> 1.26 us
    pallas_call x1, Pallas kernels: 4.43 us -> 8.64 us  [with_kernel(): pl.pallas_call(hand_over, name='hand_over', grid=(D // 256,), out_shape=[...]
where the time goes in v4:
time: 242 us
  Pallas kernels  235 us (97%)
  local copies, waits for them, and re-layouts  3.92 us (2%)
  other arithmetic  2.63 us (1%)
    pallas_call x1, Pallas kernels, with_kernel(): pl.pallas_call(functools.partial(block_kernel, dims, names), name='block'...  226 us
    pallas_call x1, Pallas kernels, with_kernel(): pl.pallas_call(hand_over, name='hand_over', grid=(D // 256,), out_shape=[...  8.64 us

profile of v4, /device:TPU:0, one launch (start us, length us, event | category | flops | bytes accessed | tf_op | source)
XLA Modules:
  0.0 242.1 jit_solution(11543835241180003706)
XLA Ops:
  0.6 1.3 fusion.5.args_6_
  2.0 1.3 fusion.15.args_5_
  3.3 1.3 copy.35
  4.5 226.2 %block.1 = (bf16[2,256,256]{2,1,0:T(8,128)(2,1)}, f32[2,256,256]{2,1,0:T(8,128)}, f32[8,256]{1,0:T(8,128)}, f32[32,3072]{1,0:T(8,128)}, f32[32,1024]{1,0:T(8,128...) custom-call(bf16[2,256,1024]{2,1,0:T(8,128)(2,1)} %args_0_.4, ...), custom_call_target="tpu_custom_call" | custom-call | tf_op jit(solution)/shard_map/block/pallas_call | solution.py:1238
  230.8 8.6 %hand_over.1 = (bf16[2,256,256]{2,1,0:T(8,128)(2,1)}, f32[2,256,256]{2,1,0:T(8,128)}, f32[8,256]{1,0:T(8,128)}, f32[32,3072]{1,0:T(8,128)}, f32[32,1024]{1,0:T(8...) custom-call(bf16[2,256,256]{2,1,0:T(8,128)(2,1)} %get-tuple-element., ...), custom_call_target="tpu_custom_call" | custom-call | tf_op jit(solution)/shard_map/hand_over/pallas_call | solution.py:1271
  239.4 0.8 constant_dynamic-slice_fusion
  240.2 0.5 slice_bitcast_fusion
  240.7 1.4 fusion.19

commit v5 on v4

--- a/solution.py
+++ b/solution.py
@@ -280,7 +280,48 @@
 
 
 MESH = pl.DeviceIdType.MESH
-KEYS = 320
+KEYS = 93
+CHAIN = {
+    "y1": 0,
+    "y1g": 1,
+    "y2": 0,
+    "xe": 1,
+    "den": 0,
+    "dy2": 1,
+    "da2": 0,
+    "dy1": 1,
+    "da1": 0,
+}
+SHARED = {
+    "geb": "y2d",
+    "dxb": "cot",
+    "fe": "dge",
+    "est": "stats",
+    "tst": "stats",
+    "vs": "v2",
+    "gdn": "wdn",
+    "gup": "wup",
+    "gwo": "wo",
+    "gqk": "wqkv",
+    "p": "c",
+    "n": "near",
+    "nf": "near far",
+    "f": "far",
+}
+
+
+def semaphore_of(k):
+    if k[0] in CHAIN:
+        return ("chain", CHAIN[k[0]]) + k[1:]
+    if k[0] == "q1":
+        return ("stats", k[1], k[2]) if k[1] < 2 else ("chain", 1, 0, k[2])
+    if k[0] == "v1":
+        return "chain", 1, 1, k[1]
+    if k[1] == "s":
+        return "u1" if k[0] == "gup" else "e1", k[2]
+    if k[0] == "tst":
+        return ("stats",) + k[2:]
+    return tuple(SHARED.get(part, part) for part in k)
 CHUNK = 128
 
 
@@ -328,6 +369,8 @@
         wdn=((nz, 2, shd, D), bf16),
         win=((S, nz, 2, sh, FQ), bf16),
         wout=((nz, 2, shd, D), bf16),
+        vin=((8, 128), f32),
+        ein=((8, Q), f32),
         vg=((S, G, 8, 128), f32),
         vecs=((8, D), f32),
         evec=((8, D), f32),
@@ -388,7 +431,15 @@
         upr=((S - 1, sh, FQ), bf16),
         qks=((S, sh, 3 * Q), bf16),
         qkr=((S - 1, sh, 3 * Q), bf16),
-        stage=((2, 256, D), f32),
+        stage=((2, 256, D), bf16),
+        out=((M, T, Q), bf16),
+        dx=((M, T, Q), f32),
+        vgo=((8, 128), f32),
+        gqk_out=((sh, 3 * D), f32),
+        gwo_out=((sh, D), f32),
+        gup_out=((sh, S * FQ), f32),
+        gdn_out=((shd, D), f32),
+        evo=((8, Q), f32),
         vsum=((8, Q), f32),
         vsr=((G - 1, 8, Q), f32),
     )
@@ -400,8 +451,13 @@
     "bucket",
     "live",
     "routes",
-    "vin",
-    "ein",
+    "gain_one",
+    "bias_one",
+    "gain_two",
+    "bias_two",
+    "gain_e",
+    "bias_e",
+    "centroid",
     "wqkv_in",
     "wo_in",
     "wup_in",
@@ -409,7 +465,7 @@
     "win_in",
     "wout_in",
 ]
-OUTPUTS = [
+RESULTS = [
     "out",
     "dx",
     "vgo",
@@ -417,10 +473,9 @@
     "gwo_out",
     "gup_out",
     "gdn_out",
-    "gin_out",
-    "gout_out",
     "evo",
 ]
+OUTPUTS = ["to_" + name for name in RESULTS] + ["gin_out", "gout_out"]
 
 
 def block_kernel(dims, names, *args):
@@ -469,7 +524,7 @@
     pending = {}
 
     def copy(src, dst, k, device):
-        i = places.setdefault(k, len(places))
+        i = places.setdefault(semaphore_of(k), len(places))
         return pltpu.make_async_remote_copy(
             src_ref=src,
             dst_ref=dst,
@@ -480,11 +535,14 @@
         )
 
     def send(src, dst, k, device):
-        pending[k] = copy(src, dst, k, device)
-        pending[k].start()
+        sent(k)
+        pending[semaphore_of(k)] = copy(src, dst, k, device)
+        pending[semaphore_of(k)].start()
 
     def sent(k):
-        pending.pop(k).wait_send()
+        last = pending.pop(semaphore_of(k), None)
+        if last is not None:
+            last.wait_send()
 
     def recv(dst, k):
         copy(dst, dst, k, beside).wait_recv()
@@ -519,9 +577,11 @@
         for i in others:
             send(out.at[m, i - 1], arrive.at[m, i - 1], (k, m, i), to_sec(i))
 
-    def sum_recv(arrive, m, k):
+    def sum_recv(arrive, m, k, then=None):
         for i in others:
             recv(arrive.at[m, i - 1], (k, m, i))
+            if then is not None and i == S - 2:
+                then()
 
     def summed(own, arrive, m, rows):
         total = own[m, rows]
@@ -579,7 +639,7 @@
     late = lax.broadcasted_iota(jnp.int32, (T, T), 1)
 
     def seat_tokens(m):
-        route = r.routes[m : m + 1, :]
+        route = r.routes[m]
         expert_ids = lax.broadcasted_iota(jnp.int32, (G, T), 0)
         picks = jnp.where(expert_ids == route, 1.0, 0.0)
         before = jnp.where(early < late, 1.0, 0.0).astype(bf16)
@@ -596,6 +656,12 @@
             pl.semaphore_signal(barrier, inc=1, device_id=to_sec(i), device_id_type=MESH)
         for j in range(1, G):
             pl.semaphore_signal(barrier, inc=1, device_id=to_dp(j), device_id_type=MESH)
+        r.vin[...] = jnp.zeros_like(r.vin)
+        for i, ref in enumerate((r.gain_one, r.bias_one, r.gain_two, r.bias_two)):
+            r.vin[i : i + 1, 0:sh] = ref[...].astype(f32)
+        r.ein[...] = jnp.zeros_like(r.ein)
+        for i, ref in enumerate((r.gain_e, r.bias_e, r.centroid)):
+            r.ein[i : i + 1, :] = ref[...].astype(f32)
         r.vg[s, d] = r.vin[...]
         r.evec[:, mine] = r.ein[...]
         for piece in range(3):
@@ -631,11 +697,11 @@
         load_out.start()
 
     def mask_tokens(m):
-        end = r.bucket[m, 0]
+        end = r.bucket[m, 0, 0]
         seg_q = (early >= end).astype(jnp.int32)
         seg_k = (late >= end).astype(jnp.int32)
-        for b in range(1, r.bucket.shape[1]):
-            end = end + r.bucket[m, b]
+        for b in range(1, r.bucket.shape[2]):
+            end = end + r.bucket[m, 0, b]
             seg_q += (early >= end).astype(jnp.int32)
             seg_k += (late >= end).astype(jnp.int32)
         live = jnp.broadcast_to(r.live[m : m + 1, :], (T, T))
@@ -767,10 +833,10 @@
     weight_near(r.wdn, "wdn")
     weight_wait(r.wdn, "wdn")
     sum_send(y2_tile(0), r.ts, r.r2, r.own, 0, "y2", "y1")
-    sum_send(y2_tile(1), r.ts, r.r2, r.own, 1, "y2", "y1")
+    sum_send(y2_tile(1), r.ts, r.r2, r.own, 1, "y2", "y1", hold=True)
 
     def finish_y2(m):
-        sum_recv(r.r2, m, "y2")
+        sum_recv(r.r2, m, "y2", None if m else lambda: sum_start(r.ts, r.r2, 1, "y2"))
 
         def body(rows):
             total = r.y1[m, rows, mine].astype(f32) + summed(r.own, r.r2, m, rows)
@@ -781,16 +847,18 @@
         dispatch_send(r.y2s, r.xe, m, "y2d")
 
     finish_y2(0)
+    dispatch_recv(r.xe, 0, "y2d")
+    gather_send(r.xe, 0, "xe")
     finish_y2(1)
-    for m in range(M):
-        dispatch_recv(r.xe, m, "y2d")
-        gather_send(r.xe, m, "xe")
     load_in.wait()
     load_out.wait()
 
     def expert(m):
         gather_recv(r.dge, m, "dge")
         gather_recv(r.xe, m, "xe")
+        if m == 0:
+            dispatch_recv(r.xe, 1, "y2d")
+            gather_send(r.xe, 1, "xe")
         gain, bias, centroid = r.evec[0:1, :], r.evec[1:2, :], r.evec[2:3, :]
 
         def body(rows):
@@ -881,10 +949,24 @@
         each(R, body)
         return_send(r.ges, r.ger, m, "geb")
 
+    def finish_dxe(m):
+        return_recv(r.dxr, m, "dxb")
+        back = tn(r.perm[m], r.dxr[m])
+        r.dy2[m, :, mine] = (r.cot[m, :, mine].astype(f32) + back).astype(bf16)
+        gather_send(r.dy2, m, "dy2")
+
     finish_den(0)
+    finish_dxe(0)
     finish_den(1)
 
     writes = []
+    results = []
+
+    def give(name):
+        i = RESULTS.index(name)
+        one = pltpu.make_async_copy(getattr(r, name), getattr(r, "to_" + name), r.lsem.at[4 + i])
+        one.start()
+        results.append(one)
 
     def expert_weights(left, right, out):
         for t in range(D // 256):
@@ -893,19 +975,13 @@
                 writes[-2].wait()
             rows = slice(t * 256, (t + 1) * 256)
             lhs = left[:, :, rows].reshape(M * R, 256)
-            r.stage[slot] = tn(lhs, right[...].reshape(M * R, D))
+            r.stage[slot] = tn(lhs, right[...].reshape(M * R, D)).astype(bf16)
             writes.append(pltpu.make_async_copy(r.stage.at[slot], out.at[rows], r.lsem.at[2 + slot]))
             writes[-1].start()
 
+    give("evo")
     expert_weights(r.en, r.dhe, r.gin_out)
 
-    def finish_dxe(m):
-        return_recv(r.dxr, m, "dxb")
-        back = tn(r.perm[m], r.dxr[m])
-        r.dy2[m, :, mine] = (r.cot[m, :, mine].astype(f32) + back).astype(bf16)
-        gather_send(r.dy2, m, "dy2")
-
-    finish_dxe(0)
     finish_dxe(1)
     expert_weights(r.ue, r.dfe, r.gout_out)
 
@@ -981,9 +1057,13 @@
         norm_back(m, 1, r.y1, r.dy2, r.own, r.r1, emit)
         gather_send(r.y1, m, "dy1")
 
+    blocks = (near_far, near, far, z)
+
     def grads_pair(g, b, k):
-        src = g.at[:, :, 1 - c] if len(g.shape) == 5 else g.at[:, 1 - c]
-        send(src, b, (k, "p"), beside)
+        for i, zz in enumerate(blocks):
+            src = g.at[:, zz, 1 - c] if len(g.shape) == 5 else g.at[zz, 1 - c]
+            dst = b.at[:, zz] if len(g.shape) == 5 else b.at[zz]
+            send(src, dst, (k, "p", i), beside)
 
     def grads_add(g, zz, arrive):
         if len(g.shape) == 5:
@@ -994,15 +1074,19 @@
         else:
             g[zz, c] = (g[zz, c].astype(f32) + arrive[...].astype(f32)).astype(bf16)
 
-    def grads_paired(g, b, k):
-        recv(b, (k, "p"))
-        for zz in range(nz):
-            grads_add(g, zz, b.at[:, zz] if len(g.shape) == 5 else b.at[zz])
+    def grads_paired(g, b, k, i):
+        zz = blocks[i]
+        piece = b.at[:, zz] if len(g.shape) == 5 else b.at[zz]
+        recv(piece, (k, "p", i))
+        grads_add(g, zz, piece)
 
     def grads_near(g, b, arrive, k):
-        grads_paired(g, b, k)
+        grads_paired(g, b, k, 0)
         send(part(g, near_far, c), arrive.at[1], (k, "nf"), (s, near * 2 + c))
+        grads_paired(g, b, k, 1)
         send(part(g, near, c), arrive.at[0], (k, "n"), (s, near * 2 + c))
+        grads_paired(g, b, k, 2)
+        grads_paired(g, b, k, 3)
 
     def grads_far(g, arrive, k):
         recv(arrive.at[1], (k, "nf"))
@@ -1015,13 +1099,11 @@
         return 0, 2
 
     def down_weights():
-        @pl.loop(0, nz)
-        def _(t):
+        for i, t in enumerate(blocks):
             lhs = r.u[:, :, col(t)].reshape(M * T, Q)
             grad = tn(lhs, r.dy2[...].reshape(M * T, D))
             r.wout[t] = grad.astype(bf16).reshape(2, shd, D)
-
-        grads_pair(r.wout, r.bdn, "gdn")
+            send(r.wout.at[t, 1 - c], r.bdn.at[t], ("gdn", "p", i), beside)
 
     def up_weights():
         @pl.loop(0, S)
@@ -1032,7 +1114,7 @@
 
         grads_pair(r.win, r.bup, "gup")
 
-    def attention_weights():
+    def qkv_weights():
         @pl.loop(0, S)
         def _(t):
             lhs = r.a1[:, :, col(t)].reshape(M * T, Q)
@@ -1040,6 +1122,8 @@
             r.gqk[t] = grad.astype(bf16).reshape(nz, 2, sh, 3 * Q)
 
         grads_pair(r.gqk, r.bqk, "gqk")
+
+    def out_weights():
         grad = tn(r.o[...].reshape(M * T, Q), r.y1[...].reshape(M * T, D))
         r.gwo[...] = grad.astype(bf16).reshape(nz, 2, sh, D)
         grads_pair(r.gwo, r.bwo, "gwo")
@@ -1048,15 +1132,16 @@
     dense_back(0)
     gather_recv(r.dy2, 1, "dy2")
     down_weights()
+    grads_near(r.wout, r.bdn, r.zdn, "gdn")
     dense_back(1)
     finish_da2(0)
-    grads_near(r.wout, r.bdn, r.zdn, "gdn")
     up_weights()
     finish_da2(1)
     grads_near(r.win, r.bup, r.zup, "gup")
 
     def attend_back(m):
-        gather_recv(r.y1, m, "dy1")
+        if m == 0:
+            gather_recv(r.y1, m, "dy1")
         sum_start(r.fes, r.fer, m, "fe")
         out_grad = nt(r.y1[m], r.wo[...].reshape(Q, D)).astype(bf16)
         for hh in range(heads):
@@ -1097,27 +1182,28 @@
 
     attend_back(0)
     grads_far(r.wout, r.zdn, "gdn")
+    gather_recv(r.y1, 1, "dy1")
+    out_weights()
     attend_back(1)
+    qkv_weights()
+    grads_near(r.gwo, r.bwo, r.zwo, "gwo")
     grads_far(r.win, r.zup, "gup")
-    attention_weights()
+    grads_near(r.gqk, r.bqk, r.zqk, "gqk")
     finish_da1(0)
-    grads_near(r.gqk, r.bqk, r.zqk, "gqk")
-    grads_near(r.gwo, r.bwo, r.zwo, "gwo")
+    grads_far(r.gwo, r.zwo, "gwo")
+    grads_far(r.gqk, r.zqk, "gqk")
     finish_fe(0)
+    finish_fe(1)
     finish_da1(1)
+    give("dx")
     for j in range(1, G):
         send(r.vsum, r.vsr.at[j - 1], ("vs", j), to_dp(j))
-    finish_fe(1)
-    grads_far(r.gqk, r.zqk, "gqk")
-    grads_far(r.gwo, r.zwo, "gwo")
 
     def finish_out(m):
         return_recv(r.ger, m, "geb")
         back = tn(r.perm[m], r.ger[m])
         r.out[m] = (r.y2q[m].astype(f32) + back).astype(bf16)
 
-    finish_out(0)
-    finish_out(1)
 
     def row_result(g, arrive, out, k, rows, wait):
         slots = wait(arrive, k)
@@ -1156,34 +1242,52 @@
                 out[:, at] = value[:, piece * width : (piece + 1) * width]
 
     row_result(r.wout, r.zdn, r.gdn_out, "gdn", shd, grads_near_recv)
+    give("gdn_out")
     column_send(r.win, r.zup, r.ups, r.upr, "gup", grads_near_recv)
     column_send(r.gqk, r.zqk, r.qks, r.qkr, "gqk", grads_near_recv)
     row_result(r.gwo, r.zwo, r.gwo_out, "gwo", sh, grads_near_recv)
+    give("gwo_out")
+    finish_out(0)
+    finish_out(1)
+    give("out")
     total = r.vsum[...]
     for j in range(1, G):
         recv(r.vsr.at[j - 1], ("vs", j))
         total += r.vsr[j - 1]
-    r.vgo[...] = total
+    shard = jnp.zeros((8, sh), f32)
+    for j in range(G):
+        shard += jnp.where(d == j, 1.0, 0.0) * total[:, j * sh : (j + 1) * sh]
+    r.vgo[...] = jnp.zeros_like(r.vgo)
+    r.vgo[:, 0:sh] = shard
+    give("vgo")
     column_result(r.ups, r.upr, r.gup_out, 1, "gup")
+    give("gup_out")
     column_result(r.qks, r.qkr, r.gqk_out, 3, "gqk")
-    for write in writes[-2:]:
-        write.wait()
-    for k in list(pending):
-        sent(k)
-    assert len(places) <= KEYS, len(places)
+    give("gqk_out")
+    def drain():
+        for write in writes[-2:] + results:
+            write.wait()
+        for last in pending.values():
+            last.wait_send()
+
+    drain()
+    assert len(places) == KEYS, len(places)
 
 
 def hand_over(*refs):
-    count = len(refs) // 2
-    first = pl.program_id(0) == 0
-    for src, dst in zip(refs[:count], refs[count:]):
-        if src.shape[0] == 256 and src.shape[1] == 1024:
+    (out, dx, vgo, gqk, gwo, gup, gdn, evo, gin, gout) = refs[:10]
+    results = refs[10:]
+    results[8][...] = gin[...].astype(f32)
+    results[9][...] = gout[...].astype(f32)
+
+    @pl.when(pl.program_id(0) == 0)
+    def _():
+        for src, dst in zip((out, dx, gqk, gwo, gup, gdn), results[:2] + results[4:8]):
             dst[...] = src[...]
-        else:
-
-            @pl.when(first)
-            def _(src=src, dst=dst):
-                dst[...] = src[...]
+        for i, dst in enumerate(results[2:4] + results[10:12]):
+            dst[...] = vgo[i : i + 1, 0 : dst.shape[1]]
+        for i, dst in enumerate(results[12:]):
+            dst[...] = evo[i : i + 1, :]
 
 
 def with_kernel(
@@ -1214,10 +1318,6 @@
     C = 3 * T // (2 * G)
     sh, shd = w_up.shape[0], w_down.shape[0]
     dims = (S, G, M, T, D, Q, FQ, C, sh, shd)
-    vin = jnp.stack([ln1_gain, ln1_bias, ln2_gain, ln2_bias]).astype(f32)
-    vin = jnp.pad(vin, ((0, 4), (0, 128 - sh)))
-    ein = jnp.concatenate([expert_gain, expert_bias, centroids]).astype(f32)
-    ein = jnp.pad(ein, ((0, 5), (0, 0)))
     scratch = layout(dims)
     names = INPUTS + OUTPUTS + list(scratch) + ["ssem", "rsem", "lsem"]
     vmem = pl.BlockSpec(memory_space=pltpu.VMEM)
@@ -1226,35 +1326,40 @@
     shapes = (
         ((M, T, Q), bf16),
         ((M, T, Q), f32),
-        ((8, Q), f32),
+        ((8, 128), f32),
         ((sh, 3 * D), f32),
         ((sh, D), f32),
         ((sh, S * FQ), f32),
         ((shd, D), f32),
-        ((D, FQ), f32),
-        ((FQ, D), f32),
         ((8, Q), f32),
+        ((D, FQ), bf16),
+        ((FQ, D), bf16),
     )
     outs = pl.pallas_call(
         functools.partial(block_kernel, dims, names),
         name="block",
         out_shape=[jax.ShapeDtypeStruct(*shape) for shape in shapes],
-        in_specs=[vmem, vmem, smem] + [vmem] * 8 + [anywhere] * 2,
-        out_specs=[vmem] * 7 + [anywhere] * 2 + [vmem],
+        in_specs=[vmem, vmem, smem] + [vmem] * 13 + [anywhere] * 2,
+        out_specs=[anywhere] * len(shapes),
         scratch_shapes=[pltpu.VMEM(*shape) for shape in scratch.values()]
         + [pltpu.SemaphoreType.DMA((KEYS,))] * 2
-        + [pltpu.SemaphoreType.DMA((4,))],
+        + [pltpu.SemaphoreType.DMA((4 + len(RESULTS),))],
         compiler_params=pltpu.CompilerParams(
             collective_id=0, has_side_effects=True, vmem_limit_bytes=63 << 20
         ),
     )(
         hidden_in,
         cotangent,
-        bucket_len[:, 0, :],
+        bucket_len,
         live_mask,
-        routes[:, :, 0],
-        vin,
-        ein,
+        jnp.swapaxes(routes, 1, 2),
+        ln1_gain.reshape(1, sh),
+        ln1_bias.reshape(1, sh),
+        ln2_gain.reshape(1, sh),
+        ln2_bias.reshape(1, sh),
+        expert_gain,
+        expert_bias,
+        centroids,
         w_qkv,
         w_attn_out,
         w_up,
@@ -1262,39 +1367,46 @@
         expert_in.reshape(S, G // 2, 2, sh, FQ),
         expert_out.reshape(G // 2, 2, shd, D),
     )
-    specs = [
-        pl.BlockSpec((256, shape[1]), lambda i: (i, 0))
-        if shape == (D, FQ) or shape == (FQ, D)
-        else pl.BlockSpec(shape, lambda i, n=len(shape): (0,) * n)
-        for shape, _ in shapes
-    ]
+
+    def spec(shape):
+        if shape in ((D, FQ), (FQ, D)):
+            return pl.BlockSpec((256, shape[1]), lambda i: (i, 0))
+        return pl.BlockSpec(shape, lambda i, n=len(shape): (0,) * n)
+
+    finals = (
+        shapes[:2]
+        + (((1, sh), f32),) * 2
+        + shapes[3:7]
+        + (((D, FQ), f32), ((FQ, D), f32))
+        + (((1, sh), f32),) * 2
+        + (((1, Q), f32),) * 3
+    )
     outs = pl.pallas_call(
         hand_over,
         name="hand_over",
         grid=(D // 256,),
-        out_shape=[jax.ShapeDtypeStruct(*shape) for shape in shapes],
-        in_specs=specs,
-        out_specs=specs,
+        out_shape=[jax.ShapeDtypeStruct(*shape) for shape in finals],
+        in_specs=[spec(shape) for shape, _ in shapes],
+        out_specs=[spec(shape) for shape, _ in finals],
         compiler_params=pltpu.CompilerParams(vmem_limit_bytes=63 << 20),
     )(*outs)
-    out, dx, vectors, gqkv, gwo, gup, gdn, gin, gout, evectors = outs
-    vectors = lax.dynamic_slice_in_dim(vectors, lax.axis_index("dp") * sh, sh, 1)
+    out, dx, gain1, bias1, gqkv, gwo, gup, gdn, gin, gout, gain2, bias2, eg, eb, ec = outs
     return (
         out,
         dx,
-        vectors[0],
-        vectors[1],
+        gain1.reshape(sh),
+        bias1.reshape(sh),
         gqkv,
         gwo,
-        vectors[2],
-        vectors[3],
+        gain2.reshape(sh),
+        bias2.reshape(sh),
         gup,
         gdn,
         gin[None],
         gout[None],
-        evectors[0:1],
-        evectors[1:2],
-        evectors[2:3],
+        eg,
+        eb,
+        ec,
     )
 
 

time: 242 us -> 224 us (0.926)
  Pallas kernels: 235 us -> 223 us
  local copies, waits for them, and re-layouts: 3.92 us -> 0 us
  other arithmetic: 2.63 us -> 0 us
    pallas_call x1, Pallas kernels: 226 us -> 215 us  [with_kernel(): pl.pallas_call(functools.partial(block_kernel, dims, names), name='block'...]
    pad x2 -> x0, other arithmetic: 2.63 us -> none  [the longest x1 1.32 us: with_kernel(): ein = jnp.pad(ein, ((0, 5), (0, 0)))]
where the time goes in v5:
time: 224 us
  Pallas kernels  223 us (100%)
    pallas_call x1, Pallas kernels, with_kernel(): pl.pallas_call(functools.partial(block_kernel, dims, names), name='block'...  215 us
    pallas_call x1, Pallas kernels, with_kernel(): pl.pallas_call(hand_over, name='hand_over', grid=(D // 256,), out_shape=[...  7.61 us

profile of v5, /device:TPU:0, one launch (start us, length us, event | category | flops | bytes accessed | tf_op | source)
XLA Modules:
  0.0 223.9 jit_solution(12562154553683895603)
XLA Ops:
  0.7 215.5 %block.1 = (bf16[2,256,256]{2,1,0:T(8,128)(2,1)}, f32[2,256,256]{2,1,0:T(8,128)}, f32[8,128]{1,0:T(8,128)}, f32[32,3072]{1,0:T(8,128)}, f32[32,1024]{1,0:T(8,128...) custom-call(bf16[2,256,1024]{2,1,0:T(8,128)(2,1)} %args_0_.4, ...), custom_call_target="tpu_custom_call" | custom-call | tf_op jit(solution)/shard_map/block/pallas_call | solution.py:1338
  216.1 7.6 %hand_over.1 = (bf16[2,256,256]{2,1,0:T(8,128)(2,1)}, f32[2,256,256]{2,1,0:T(8,128)}, f32[1,32]{1,0:T(1,128)}, f32[1,32]{1,0:T(1,128)}, f32[32,3072]{1,0:T(8,128...) custom-call(bf16[2,256,256]{2,1,0:T(8,128)(2,1)} %get-tuple-element., ...), custom_call_target="tpu_custom_call" | custom-call | tf_op jit(solution)/shard_map/hand_over/pallas_call | solution.py:1384
